TPU v7x, 128 devices: a whole 4x4x4 slice. The times are simulated.
128 devices in a mesh: outer: 8 (over x_hi, y), inner: 16 (over x_lo, z, core).
Axes of the slice: x: 4 (x_hi: 2, x_lo: 2; x = x_hi * 2 + x_lo), y: 4, z: 4, core: 2. Of those that a mesh axis runs over, the one named last changes fastest.
Arguments:
- image_features: bfloat16 [16384, 1024], P(('outer', 'inner')), may hold values from -40 to 40
- text_features: bfloat16 [16384, 768], P(('outer', 'inner')), may hold values from -40 to 40
- image_projection: bfloat16 [1024, 768], replicated, may hold values from -2 to 2
- text_projection: bfloat16 [768, 768], replicated, may hold values from -2 to 2
Outputs:
- total_loss: float32 [], replicated
- image_grad: bfloat16 [16384, 1024], P(('outer', 'inner'))
- text_grad: bfloat16 [16384, 768], P(('outer', 'inner'))
- image_projection_grad: float32 [1024, 768], replicated
- text_projection_grad: float32 [768, 768], replicated
All inputs are finite; a program needn't handle non-finite values.
Results may differ from a plain program's by a relative error of at most 0.02.
Values may be sent and summed in bfloat16 or wider, within the bound.
No kernel may reach another device: no remote copies, remote signals or barrier semaphores. Data moves between devices by JAX's collectives and lax.ppermute only.
A program may use at most 192 MiB of HBM per device.

v0:
```python
import jax
import jax.numpy as jnp
from jax import lax
from jax.sharding import PartitionSpec as P

sharpness_factor = 100.0
norm_eps = 1e-06


def normalize_rows(features, weight):
    projected = jnp.dot(features, weight, preferred_element_type=jnp.float32)
    radius = jnp.sqrt(jnp.sum(projected * projected, axis=1, keepdims=True) + norm_eps)
    return (projected / radius, radius)


def back_rows(unit_rows, radius, emb_grad, features, weight):
    along = jnp.sum(unit_rows * emb_grad, axis=1, keepdims=True)
    projected_grad = ((emb_grad - unit_rows * along) / radius).astype(jnp.bfloat16)
    feature_grad = jnp.dot(projected_grad, weight.T, preferred_element_type=jnp.float32).astype(
        jnp.bfloat16
    )
    weight_grad = jnp.dot(features.T, projected_grad, preferred_element_type=jnp.float32)
    return (feature_grad, weight_grad)


def body(image_features, text_features, image_projection, text_projection):
    image_unit, image_radius = normalize_rows(image_features, image_projection)
    text_unit, text_radius = normalize_rows(text_features, text_projection)
    picture_latent_vector = image_unit.astype(jnp.bfloat16)
    caption_latent_vector = text_unit.astype(jnp.bfloat16)
    all_text = lax.all_gather(caption_latent_vector, ("outer", "inner"), axis=0, tiled=True)
    pair_total = all_text.shape[0]
    affinity_matrix = sharpness_factor * jnp.einsum(
        "id,jd->ij", picture_latent_vector, all_text, preferred_element_type=jnp.float32
    )
    paired_diagonal_entries = sharpness_factor * jnp.sum(
        picture_latent_vector.astype(jnp.float32) * caption_latent_vector.astype(jnp.float32),
        axis=1,
    )
    centered_affinity_matrix = jnp.exp(affinity_matrix - sharpness_factor)
    picture_axis_normalizer = jnp.log(jnp.sum(centered_affinity_matrix, axis=1)) + sharpness_factor
    column_part = jnp.sum(centered_affinity_matrix, axis=0)
    row_part = jnp.sum(picture_axis_normalizer - 2.0 * paired_diagonal_entries)
    caption_axis_total, row_total = lax.psum((column_part, row_part), ("outer", "inner"))
    caption_axis_normalizer = jnp.log(caption_axis_total) + sharpness_factor
    total_loss = (row_total + jnp.sum(caption_axis_normalizer)) / (2.0 * pair_total)
    normalized_probabilities = (
        0.5
        * sharpness_factor
        * (
            jnp.exp(affinity_matrix - picture_axis_normalizer[:, None])
            + jnp.exp(affinity_matrix - caption_axis_normalizer[None, :])
        )
    ).astype(jnp.bfloat16)
    picture_latent_adjoint = jnp.dot(
        normalized_probabilities, all_text, preferred_element_type=jnp.float32
    ) - sharpness_factor * caption_latent_vector.astype(jnp.float32)
    caption_latent_adjoint = lax.psum_scatter(
        jnp.einsum(
            "ij,id->jd",
            normalized_probabilities,
            picture_latent_vector,
            preferred_element_type=jnp.float32,
        ),
        ("outer", "inner"),
        scatter_dimension=0,
        tiled=True,
    ) - sharpness_factor * picture_latent_vector.astype(jnp.float32)
    image_grad, image_weight_term = back_rows(
        image_unit, image_radius, picture_latent_adjoint, image_features, image_projection
    )
    text_grad, text_weight_term = back_rows(
        text_unit, text_radius, caption_latent_adjoint, text_features, text_projection
    )
    image_projection_grad, text_projection_grad = lax.psum(
        (image_weight_term, text_weight_term), ("outer", "inner")
    )
    return (total_loss, image_grad, text_grad, image_projection_grad, text_projection_grad)


def solution(mesh):
    return jax.shard_map(
        body,
        mesh=mesh,
        in_specs=(P(("outer", "inner"), None), P(("outer", "inner"), None), P(), P()),
        out_specs=(P(), P(("outer", "inner"), None), P(("outer", "inner"), None), P(), P()),
        check_vma=False,
    )
```

profile of v0, /device:TPU:1, one launch (start us, length us, event | category | flops | bytes accessed | tf_op | source)
XLA Modules:
  0.0 1308.0 jit_solution(18037497131492495436)
XLA Ops:
  7.2 0.0 copy-start
  7.2 0.0 all-gather.2.cloned.1.call-start
  7.2 1.9 multiply_reduce_fusion.2
  9.1 0.8 fusion.6
  9.9 0.0 all-gather.2.cloned.1.call-update
  9.9 0.0 all-reduce.4.cloned.1.call-start
  10.0 0.0 copy-done
  10.0 1.4 multiply_reduce_fusion.3
  11.4 229.4 %all-gather.2.cloned.1.call-done = bf16[16384,768]{1,0:T(8,128)(2,1)} async-done(((bf16[128,768]{1,0:T(8,128)(2,1)}), bf16[16384,768]{1,0:T(8,128)(2,1)}) %all-gather.2.cloned.1.call-update) | async-done | bytes 25165840 | tf_op jit(solution)/shard_map/all_gather | solution.py:31
  240.8 15.8 %fusion = (f32[16384]{0:T(1024)}, f32[128]{0:T(128)S(1)}, f32[128,16384]{1,0:T(8,128)}) fusion(bf16[16384,768]{1,0:T(8,128)(2,1)} %all-gather.2.cloned.1.call-done, f32[128,768]{1,0:T(8,128)S(1)} %get-tuple-element.19, f32[128]{0:T(128)S(1)} %add_sqrt_fusion.1), kind=kOutput, calls=%fused_computation.3 | convolution fusion | flops 3229794304 | bytes 34014208 | tf_op jit(solution)/shard_map/id,jd->ij/dot_general | solution.py:33
  256.6 0.0 copy-start.7
  256.6 0.0 all-reduce.4.cloned.1.call-update
  256.7 0.0 reduce-scatter.2.cloned.1.call-start
  256.7 136.6 %all-reduce.4.cloned.1.call-done = f32[16384]{0:T(1024)} async-done(((f32[16384]{0:T(1024)}), f32[16384]{0:T(1024)}) %all-reduce.4.cloned.1.call-update) | async-done | bytes 65552 | tf_op jit(solution)/shard_map/psum | solution.py:44
  393.3 1.5 fusion.4
  394.8 22.8 %fusion.7 = f32[16384,768]{1,0:T(8,128)} fusion(f32[128,16384]{1,0:T(8,128)} %get-tuple-element.22, f32[16384]{0:T(1024)S(1)} %get-tuple-element.17, f32[128]{0:T(128)S(1)} %log_add_fusion.1, f32[128,768]{1,0:T(8,128)S(1)} %get-tuple-element.19, f32[128]{0:T(128)S(1)} %add_sqrt_fusion.1), kind=kOutput, calls=%fused_computation.31 | convolution fusion | flops 3231907840 | bytes 59180032 | tf_op jit(solution)/shard_map/ij,id->jd/dot_general | solution.py:59
  417.6 0.0 copy-done.7
  417.6 0.0 copy-start.5
  417.6 0.0 reduce-scatter.2.cloned.1.call-update
  417.6 0.0 copy-start.4
  417.6 0.2 all-reduce.6.cloned.1.call-start
  417.9 0.7 copy-done.5
  418.5 14.4 %multiply_reduce_fusion.1 = (f32[128]{0:T(128)S(1)}, f32[128,768]{1,0:T(8,128)S(1)}) fusion(f32[128,768]{1,0:T(8,128)S(1)} %get-tuple-element.19, f32[128]{0:T(128)S(1)} %add_sqrt_fusion.1, bf16[128,768]{1,0:T(8,128)(2,1)S(1)} %copy-done.5, bf16[16384,768]{1,0:T(8,128)(2,1)} %all-gather.2.cloned.1.call-done, f32[128,16384]{1,0:T(8,128)} %get-tuple-element.22, ...), kind=kOutput, calls=%fused_computation.18 | convolution fusion | flops 3232301056 | bytes 34604544 | tf_op jit(solution)/shard_map/dot_general | solution.py:55
  432.9 0.0 copy-start.6
  432.9 0.7 copy-done.6
  433.7 0.0 copy-done.4
  433.7 2.4 convolution_bitcast_fusion
  436.0 0.0 copy-start.1
  436.0 693.5 %reduce-scatter.2.cloned.1.call-done = f32[128,768]{1,0:T(8,128)} async-done(((f32[16384,768]{1,0:T(8,128)}), f32[128,768]{1,0:T(8,128)}) %reduce-scatter.2.cloned.1.call-update) | async-done | bytes 393232 | tf_op jit(solution)/shard_map/reduce_scatter | solution.py:58
  1129.6 1.2 multiply_reduce_fusion
  1130.8 1.2 divide_convert_fusion
  1132.0 0.0 copy-start.2
  1132.0 0.7 copy-done.2
  1132.7 2.8 convolution_bitcast_fusion.1
  1135.5 0.0 copy-start.3
  1135.5 0.0 all-reduce.6.cloned.1.call-update
  1135.5 1.4 subtract_reduce_fusion
  1136.9 2.4 convolution_convert_fusion
  1139.3 68.2 %psum.28 = f32[]{:T(128)} all-reduce(f32[]{:T(128)} %subtract_reduce_fusion), channel_id=1, replica_groups=mesh['outer'=8,'inner'=16] {'outer','inner'}, use_global_device_ids=true, to_apply=%region_5.0 | all-reduce | flops 1 | bytes 8 | tf_op jit(solution)/shard_map/psum | solution.py:44
  1208.8 0.0 copy-done.1
  1208.8 0.0 copy-done.3
  1208.8 1.2 convolution_convert_fusion.1
  1210.0 83.7 %all-reduce.6.cloned.1.call-done = (f32[1024,768]{0,1:T(8,128)}, f32[768,768]{0,1:T(8,128)}) async-done(((f32[1024,768]{0,1:T(8,128)}, f32[768,768]{0,1:T(8,128)}), (f32[1024,768]{0,1:T(8,128)}, f32[768,768]{0,1:T(8,128)})) %all-reduce.6.cloned.1.call-update) | async-done | bytes 5505040 | tf_op jit(solution)/shard_map/psum | solution.py:75
  1293.7 3.5 copy.9
  1297.3 3.0 copy.10
  (3 shorter events, 0.0 us)
Async XLA Ops:
  7.2 2.8 copy-start
  7.2 233.6 %all-gather.2.cloned.1.call-start = ((), (), s32[]{:S(2)}) async-start(), calls=%async_computation.1 | async-start | bytes 25362432 | tf_op jit(solution)/shard_map/all_gather | solution.py:31
  9.9 383.4 %all-reduce.4.cloned.1.call-start = ((), (), s32[]{:S(2)}) async-start(), calls=%async_computation.2 | async-start | bytes 131072 | tf_op jit(solution)/shard_map/psum | solution.py:44
  256.6 161.0 %copy-start.7 = (f32[128]{0:T(128)}, f32[128]{0:T(128)S(1)}, u32[]{:S(2)}) copy-start(f32[128]{0:T(128)S(1)} %get-tuple-element.11) | copy-start | bytes 1540
  256.7 872.9 %reduce-scatter.2.cloned.1.call-start = ((), (), s32[]{:S(2)}) async-start(), calls=%async_computation.3 | async-start | bytes 50724864 | tf_op jit(solution)/shard_map/reduce_scatter | solution.py:58
  417.6 0.9 copy-start.5
  417.6 16.1 %copy-start.4 = (bf16[128,1024]{1,0:T(8,128)(2,1)S(1)}, bf16[128,1024]{1,0:T(8,128)(2,1)}, u32[]{:S(2)}) copy-start(bf16[128,1024]{1,0:T(8,128)(2,1)} %param.4) | copy-start | bytes 786436
  417.6 876.1 %all-reduce.6.cloned.1.call-start = ((), (), s32[]{:S(2)}) async-start(), calls=%async_computation.4 | async-start | bytes 11010048 | tf_op jit(solution)/shard_map/psum | solution.py:75
  432.9 0.8 copy-start.6
  436.0 772.7 %copy-start.1 = (bf16[768,768]{1,0:T(8,128)(2,1)S(1)}, bf16[768,768]{1,0:T(8,128)(2,1)}, u32[]{:S(2)}) copy-start(bf16[768,768]{1,0:T(8,128)(2,1)} %param.7) | copy-start | bytes 3538948
  1132.0 0.7 copy-start.2
  1135.5 73.3 %copy-start.3 = (bf16[128,768]{1,0:T(8,128)(2,1)S(1)}, bf16[128,768]{1,0:T(8,128)(2,1)}, u32[]{:S(2)}) copy-start(bf16[128,768]{1,0:T(8,128)(2,1)} %copy-done.2) | copy-start | bytes 589828
Sparse Core Ops, SparseCore 0:
  10.3 230.4 all-gather.1
  256.8 136.5 all-reduce.3
  417.8 711.7 reduce-scatter.1
  1135.9 157.8 all-reduce.5
where the time goes:
time: 1310 us
  waiting for transfers between devices  1140 us (87%)
  blocking collectives  68.2 us (5%)
  matrix products  65.1 us (5%)
  between operations  16.3 us (1%)
    reduce_scatter x1, waiting for transfers between devices, body(): lax.psum_scatter(jnp.einsum('ij,id->jd', normalized_probabilities, pictur...  694 us
    all_gather x1, waiting for transfers between devices, body(): lax.all_gather(caption_latent_vector, ('outer', 'inner'), axis=0, tiled=T...  229 us
    psum x1, waiting for transfers between devices, body(): lax.psum((column_part, row_part), ('outer', 'inner'))  137 us
    psum x1, waiting for transfers between devices, body(): lax.psum((image_weight_term, text_weight_term), ('outer', 'inner'))  83.7 us
    psum x1, blocking collectives, body(): lax.psum((column_part, row_part), ('outer', 'inner'))  68.2 us
  transfers between devices with their start and end apart: 4, of which 4 were waited for; matrix products, arithmetic and copies ran while one was open for 2% of the time, Pallas kernels for 0%

commit v1 on v0

v1 whole, which is shorter than its diff:
```python
import jax
import jax.numpy as jnp
from jax import lax
from jax.sharding import Mesh, PartitionSpec as P

sharpness_factor = 100.0
norm_eps = 1e-06
X = ("xh", "xl")
YZ = ("y", "z")
XYZ = ("xh", "xl", "y", "z")
ALL = ("xh", "y", "xl", "z", "c")
f32 = jnp.float32
bf16 = jnp.bfloat16


def normalize_rows(features, weight):
    projected = jnp.dot(features, weight, preferred_element_type=f32)
    radius = jnp.sqrt(jnp.sum(projected * projected, axis=1, keepdims=True) + norm_eps)
    return (projected / radius, radius)


def back_rows(unit_rows, radius, emb_grad, features, weight):
    along = jnp.sum(unit_rows * emb_grad, axis=1, keepdims=True)
    projected_grad = ((emb_grad - unit_rows * along) / radius).astype(bf16)
    feature_grad = lax.dot_general(
        projected_grad, weight, (((1,), (1,)), ((), ())), preferred_element_type=f32
    ).astype(bf16)
    weight_grad = lax.dot_general(
        features, projected_grad, (((0,), (0,)), ((), ())), preferred_element_type=f32
    )
    return (feature_grad, weight_grad)


def from_x(v, k):
    return lax.ppermute(v, X, [(i, (i - k) % 4) for i in range(4)])


def from_core(v):
    return lax.ppermute(v, "c", [(0, 1), (1, 0)])


def spread(v, axes, n):
    return lax.all_to_all(jnp.broadcast_to(v[None], (n,) + v.shape), axes, 0, 0)


def gather_text(t):
    half = t.shape[0] // 2
    up = from_x(t, 1)
    down = from_x(t, 3)
    far = jnp.concatenate([from_x(up[:half], 1), from_x(down[half:], 3)], axis=0)
    mine = jnp.concatenate([t, up, far, down], axis=0)
    return jnp.concatenate([mine, from_core(mine)], axis=0)


def column_totals(part):
    n = part.shape[0] // 2
    both = part[:n] + from_core(part[n:]), part[n:] + from_core(part[:n])
    both = jnp.stack(both).reshape(2, 4, n // 4)
    total = both
    for k in (1, 3, 2):
        total = total + jnp.roll(from_x(both, k), k, axis=1)
    return total.reshape(-1)


def scatter_text(g):
    n = g.shape[0] // 2
    b = n // 4
    h = b // 2
    g = g[:n] + from_core(g[n:].astype(bf16)).astype(f32)
    g0, g1, g2, g3 = (g[k * b : (k + 1) * b] for k in range(4))
    low = from_x(g2[:h].astype(bf16), 3).astype(f32)
    high = from_x(g2[h:].astype(bf16), 1).astype(f32)
    g1 = jnp.concatenate([g1[:h] + low, g1[h:]], axis=0)
    g3 = jnp.concatenate([g3[:h], g3[h:] + high], axis=0)
    return g0 + from_x(g1.astype(bf16), 3).astype(f32) + from_x(g3.astype(bf16), 1).astype(f32)


def reduce_weights(image_term, text_term, loss_part):
    rows = image_term.shape[0] + text_term.shape[0]
    core = lax.axis_index("c")
    both = jnp.concatenate([image_term, text_term], axis=0)
    width = both.shape[1]
    half = rows // 2
    both = both.reshape(2, half, width)
    mine = lax.dynamic_index_in_dim(both, core, 0, keepdims=False)
    other = lax.dynamic_index_in_dim(both, 1 - core, 0, keepdims=False)
    mine = mine + from_core(other.astype(bf16)).astype(f32)
    hi = loss_part.astype(bf16)
    lo = (loss_part - hi.astype(f32)).astype(bf16)
    n = 64
    each = half // n
    tail = jnp.zeros((16 - each, width), bf16).at[0, 0].set(hi).at[0, 1].set(lo)
    sent = jnp.concatenate(
        [mine.astype(bf16).reshape(n, each, width), jnp.broadcast_to(tail[None], (n,) + tail.shape)],
        axis=1,
    )
    got = jnp.sum(lax.all_to_all(sent, XYZ, 0, 0).astype(f32), axis=0)
    loss = got[each, 0] + got[each, 1]
    loss = loss + from_core(loss)
    full = spread(got[:each].astype(bf16), XYZ, n).reshape(half, width)
    swapped = from_core(full)
    out = jnp.zeros((2, half, width), bf16)
    out = lax.dynamic_update_index_in_dim(out, full, core, 0)
    out = lax.dynamic_update_index_in_dim(out, swapped, 1 - core, 0)
    out = out.reshape(rows, width).astype(f32)
    return out[: image_term.shape[0]], out[image_term.shape[0] :], loss


def body(image_features, text_features, image_projection, text_projection):
    image_unit, image_radius = normalize_rows(image_features, image_projection)
    text_unit, text_radius = normalize_rows(text_features, text_projection)
    image_emb = image_unit.astype(bf16)
    text_emb = text_unit.astype(bf16)
    own, width = image_emb.shape
    place = lax.axis_index(YZ)
    images = spread(image_emb, YZ, 16).reshape(16 * own, width)
    texts = gather_text(text_emb)
    logits = sharpness_factor * lax.dot_general(
        images, texts, (((1,), (1,)), ((), ())), preferred_element_type=f32
    )
    matched = sharpness_factor * jnp.sum(image_emb.astype(f32) * text_emb.astype(f32), axis=1)
    centered = jnp.exp(logits - sharpness_factor)
    row_total = jnp.sum(spread(jnp.sum(centered, axis=1), YZ, 16), axis=0)
    column_total = column_totals(jnp.sum(centered, axis=0))
    row_lse = jnp.log(row_total) + sharpness_factor
    column_lse = jnp.log(column_total) + sharpness_factor
    own_rows = lax.dynamic_slice_in_dim(row_lse, place * own, own)
    loss_part = jnp.sum(own_rows + column_lse[:own] - 2.0 * matched)
    weights = (
        0.5
        * sharpness_factor
        * (jnp.exp(logits - row_lse[:, None]) + jnp.exp(logits - column_lse[None, :]))
    ).astype(bf16)
    image_part = jnp.dot(weights, texts, preferred_element_type=f32).reshape(16, own, width)
    text_part = lax.dot_general(
        weights, images, (((0,), (0,)), ((), ())), preferred_element_type=f32
    )
    here = (jnp.arange(16) == place)[:, None, None]
    image_part = image_part - jnp.where(here, sharpness_factor * text_emb.astype(f32)[None], 0.0)
    image_emb_grad = jnp.sum(
        lax.all_to_all(image_part.astype(bf16), YZ, 0, 0).astype(f32), axis=0
    )
    text_part = jnp.concatenate(
        [text_part[:own] - sharpness_factor * image_emb.astype(f32), text_part[own:]], axis=0
    )
    text_emb_grad = scatter_text(text_part)
    image_grad, image_term = back_rows(
        image_unit, image_radius, image_emb_grad, image_features, image_projection
    )
    text_grad, text_term = back_rows(
        text_unit, text_radius, text_emb_grad, text_features, text_projection
    )
    image_projection_grad, text_projection_grad, loss = reduce_weights(
        image_term, text_term, loss_part
    )
    pairs = own * 128
    return (
        loss / (2.0 * pairs),
        image_grad,
        text_grad,
        image_projection_grad,
        text_projection_grad,
    )


def solution(mesh):
    grid = Mesh(mesh.devices.reshape(2, 4, 2, 4, 2), ALL)
    rows = P(ALL, None)
    return jax.shard_map(
        body,
        mesh=grid,
        in_specs=(rows, rows, P(), P()),
        out_specs=(P(), rows, rows, P(), P()),
        check_vma=False,
    )
```

time: 1310 us -> 286 us (0.22)
  waiting for transfers between devices: 1140 us -> 51.6 us
  starting transfers between devices: 0.34 us -> 55.8 us
  local copies, waits for them, and re-layouts: 8.68 us -> 60 us
  matrix products: 65.1 us -> 33 us
  other arithmetic: 6.07 us -> 22.9 us
    reduce_scatter x1 -> x0, waiting for transfers between devices: 694 us -> none  [body(): lax.psum_scatter(jnp.einsum('ij,id->jd', normalized_probabilities, pictur...]
    all_gather x1 -> x0, waiting for transfers between devices: 229 us -> none  [body(): lax.all_gather(caption_latent_vector, ('outer', 'inner'), axis=0, tiled=T...]
    psum x2 -> x0, waiting for transfers between devices: 220 us -> none  [the longest x1 137 us: body(): lax.psum((column_part, row_part), ('outer', 'inner'))]
    psum x1 -> x0, blocking collectives: 68.2 us -> none  [body(): lax.psum((column_part, row_part), ('outer', 'inner'))]
    all_to_all x0 -> x2, blocking collectives: none -> 56.1 us  [the longest x1 28.5 us: reduce_weights(): got = jnp.sum(lax.all_to_all(sent, XYZ, 0, 0).astype(f32), axis=0)]
    ppermute x0 -> x18, starting transfers between devices: none -> 35.1 us  [the longest x7 17.7 us: from_core(): return lax.ppermute(v, 'c', [(0, 1), (1, 0)])]
    all_to_all x0 -> x3, waiting for transfers between devices: none -> 33.3 us  [the longest x2 21.8 us: spread(): return lax.all_to_all(jnp.broadcast_to(v[None], (n,) + v.shape), axes, 0, 0)]
    dot_general x9, matrix products: 65.1 us -> 33 us  [the longest x1 9.79 us: body(): lax.dot_general(images, texts, (((1,), (1,)), ((), ())), preferred_elemen...]
  transfers between devices with their start and end apart: 4 -> 21, of which waited for: 4 -> 15; matrix products, arithmetic and copies ran while one was open for 2% -> 15% of each run, Pallas kernels for 0% -> 0%
where the time goes in v1:
time: 286 us; the launch traced here: 285 us
  local copies, waits for them, and re-layouts  60 us (21%)
  blocking collectives  56.1 us (20%)
  starting transfers between devices  55.8 us (20%)
  waiting for transfers between devices  51.6 us (18%)
  matrix products  33 us (12%)
  other arithmetic  22.9 us (8%)
  between operations  5.35 us (2%)
    all_to_all x1, blocking collectives, reduce_weights(): got = jnp.sum(lax.all_to_all(sent, XYZ, 0, 0).astype(f32), axis=0)  28.5 us
    all_to_all x1, blocking collectives, spread(): return lax.all_to_all(jnp.broadcast_to(v[None], (n,) + v.shape), axes, 0, 0)  27.6 us
    all_to_all x2, waiting for transfers between devices, spread(): return lax.all_to_all(jnp.broadcast_to(v[None], (n,) + v.shape), axes, 0, 0)  21.8 us
    ppermute x7, starting transfers between devices, from_core(): return lax.ppermute(v, 'c', [(0, 1), (1, 0)])  17.7 us
    ppermute x11, starting transfers between devices, from_x(): return lax.ppermute(v, X, [(i, (i - k) % 4) for i in range(4)])  17.4 us
    all_to_all x2, starting transfers between devices, spread(): return lax.all_to_all(jnp.broadcast_to(v[None], (n,) + v.shape), axes, 0, 0)  16.2 us
    dynamic_slice x2, local copies, waits for them, and re-layouts, reduce_weights(): mine = lax.dynamic_index_in_dim(both, core, 0, keepdims=False)  14.9 us
    ppermute x11, waiting for transfers between devices, from_x(): return lax.ppermute(v, X, [(i, (i - k) % 4) for i in range(4)])  13.3 us
  transfers between devices with their start and end apart: 21, of which 15 were waited for; matrix products, arithmetic and copies ran while one was open for 15% of the time, Pallas kernels for 0%

profile of v1, /device:TPU:1, one launch (start us, length us, event | category | flops | bytes accessed | tf_op | source)
XLA Modules:
  0.0 284.7 jit_solution(2514026751092257307)
XLA Ops:
  0.6 1.9 multiply_reduce_fusion.2
  2.6 1.4 multiply_reduce_fusion.3
  4.1 0.7 fusion.5
  4.9 2.0 broadcast_in_dim.38
  6.8 8.6 %all-to-all-start = ((bf16[16,128,768]{2,1,0:T(8,128)(2,1)}), bf16[16,128,768]{2,1,0:T(8,128)(2,1)}, u32[]{:S(2)}, u32[]{:S(2)}) async-start(bf16[16,128,768]{2,1,0:T(8,128)(2,1)} %broadcast_in_dim.38), calls=%async_computation | async-start | bytes 6291456 | tf_op jit(solution)/shard_map/all_to_all | solution.py:43
  15.5 2.5 collective-permute-start
  18.7 2.5 collective-permute-done
  21.3 3.6 %collective-permute-start.1 = (bf16[64,768]{1,0:T(8,128)(2,1)S(1)}, bf16[64,768]{1,0:T(8,128)(2,1)S(1)}, u32[]{:S(2)}, u32[]{:S(2)}) collective-permute-start(bf16[64,768]{1,0:T(8,128)(2,1)S(1)} %slice.171), channel_id=1, source_target_pairs={{0,72},{8,0},{64,8},{72,64},{1,73},{9,1},{65,9},{73,65},{2,74},{10... | collective-permute-start | bytes 294920 | tf_op jit(solution)/shard_map/ppermute | solution.py:35
  25.0 0.7 constant_dynamic-update-slice_fusion.3
  25.7 0.8 collective-permute-done.1
  27.2 2.9 %collective-permute-done.3 = bf16[64,768]{1,0:T(8,128)(2,1)S(1)} collective-permute-done((bf16[64,768]{1,0:T(8,128)(2,1)S(1)}, bf16[64,768]{1,0:T(8,128)(2,1)S(1)}, u32[]{:S(2)}, u32[]{:S(2)}) %collective-permute-start.3) | collective-permute-done | bytes 98336 | tf_op jit(solution)/shard_map/ppermute | solution.py:35
  31.4 2.8 collective-permute-start.4
  34.2 1.9 collective-permute-done.4
  36.1 0.9 constant_dynamic-update-slice_fusion.5
  37.0 18.8 %all-to-all-done = bf16[16,128,768]{2,1,0:T(8,128)(2,1)} async-done(((bf16[16,128,768]{2,1,0:T(8,128)(2,1)}), bf16[16,128,768]{2,1,0:T(8,128)(2,1)}, u32[]{:S(2)}, u32[]{:S(2)}) %all-to-all-start) | async-done | bytes 3145760 | tf_op jit(solution)/shard_map/all_to_all | solution.py:43
  55.8 9.8 %fusion.1 = (f32[2048]{0:T(1024)S(1)}, f32[1024]{0:T(1024)S(1)}, f32[2048,1024]{1,0:T(8,128)}) fusion(bf16[2048,768]{1,0:T(8,128)(2,1)} %bitcast, bf16[1024,768]{1,0:T(8,128)(2,1)} %constant_dynamic-update-slice_fusion.5), kind=kOutput, calls=%fused_computation.3 | convolution fusion | flops 3229611008 | bytes 13119488 | tf_op jit(solution)/shard_map/dot_general | solution.py:118
  65.6 3.1 %collective-permute-start.5 = (f32[512]{0:T(512)S(1)}, f32[512]{0:T(512)S(1)}, u32[]{:S(2)}, u32[]{:S(2)}) collective-permute-start(f32[512]{0:T(512)S(1)} %get-tuple-element.59), channel_id=1, source_target_pairs={{0,1},{1,0},{2,3},{3,2},{4,5},{5,4},{6,7},{7,6},{8,9},{9,8},{10,11... | collective-permute-start | bytes 6152 | tf_op jit(solution)/shard_map/ppermute | solution.py:39
  68.8 0.7 collective-permute-done.5
  69.9 2.8 collective-permute-start.9
  72.8 0.7 broadcast_in_dim.39
  73.5 7.6 %all-to-all-start.1 = ((f32[16,1,2048]{2,1,0:T(1,128)}), f32[16,1,2048]{2,1,0:T(1,128)S(1)}, u32[]{:S(2)}, u32[]{:S(2)}) async-start(f32[16,1,2048]{2,1,0:T(1,128)} %broadcast_in_dim.39), calls=%async_computation.1 | async-start | bytes 262144 | tf_op jit(solution)/shard_map/all_to_all | solution.py:43
  81.4 2.4 collective-permute-start.7
  83.8 1.0 collective-permute-done.8
  84.9 3.0 %all-to-all-done.1 = f32[16,1,2048]{2,1,0:T(1,128)S(1)} async-done(((f32[16,1,2048]{2,1,0:T(1,128)}), f32[16,1,2048]{2,1,0:T(1,128)S(1)}, u32[]{:S(2)}, u32[]{:S(2)}) %all-to-all-start.1) | async-done | bytes 131104 | tf_op jit(solution)/shard_map/all_to_all | solution.py:43
  87.9 4.9 %multiply_convert_fusion = bf16[2048,1024]{1,0:T(8,128)(2,1)S(1)} fusion(f32[2048,1024]{1,0:T(8,128)} %get-tuple-element.67, f32[1024]{0:T(1024)S(1)} %bitcast.49, f32[2048]{0:T(1024)S(1)} %log_add_fusion), kind=kLoop, calls=%fused_computation | loop fusion | flops 12582912 | bytes 12595200 | tf_op jit(solution)/shard_map/convert_element_type | solution.py:133
  92.8 6.1 %fusion.24 = f32[2048,768]{1,0:T(8,128)S(1)} fusion(bf16[2048,1024]{1,0:T(8,128)(2,1)S(1)} %multiply_convert_fusion, bf16[1024,768]{1,0:T(8,128)(2,1)} %constant_dynamic-update-slice_fusion.5), kind=kOutput, calls=%fused_computation.78 | convolution fusion | flops 3221225472 | bytes 12058624 | tf_op jit(solution)/shard_map/dot_general | solution.py:134
  98.9 2.7 subtract_convert_fusion
  101.6 4.5 %all-to-all-start.2 = ((bf16[16,128,768]{2,1,0:T(8,128)(2,1)}), bf16[16,128,768]{2,1,0:T(8,128)(2,1)}, u32[]{:S(2)}, u32[]{:S(2)}) async-start(bf16[16,128,768]{2,1,0:T(8,128)(2,1)} %subtract_convert_fusion), calls=%async_computation.2 | async-start | bytes 6291456 | tf_op jit(solution)/shard_map/all_to_all | solution.py:141
  106.2 6.3 %fusion.25 = f32[1024,768]{1,0:T(8,128)S(1)} fusion(bf16[2048,1024]{1,0:T(8,128)(2,1)} %copy-done.4, bf16[2048,768]{1,0:T(8,128)(2,1)} %bitcast), kind=kOutput, calls=%fused_computation.79 | convolution fusion | flops 3221225472 | bytes 10485760 | tf_op jit(solution)/shard_map/dot_general | solution.py:135
  112.5 1.9 collective-permute-start.10
  114.7 1.7 collective-permute-done.10
  116.9 2.5 collective-permute-start.13
  119.5 2.6 collective-permute-done.11
  122.2 0.9 collective-permute-start.12
  123.7 1.9 collective-permute-start.14
  125.6 3.3 %collective-permute-done.12 = bf16[128,768]{1,0:T(8,128)(2,1)S(1)} collective-permute-done((bf16[128,768]{1,0:T(8,128)(2,1)S(1)}, bf16[128,768]{1,0:T(8,128)(2,1)S(1)}, u32[]{:S(2)}, u32[]{:S(2)}) %collective-permute-start.12) | collective-permute-done | bytes 196640 | tf_op jit(solution)/shard_map/ppermute | solution.py:35
  129.1 1.2 multiply_reduce_fusion
  130.3 1.1 divide_convert_fusion
  131.4 1.9 convolution_bitcast_fusion.1
  133.3 11.6 %all-to-all-done.2 = bf16[16,128,768]{2,1,0:T(8,128)(2,1)} async-done(((bf16[16,128,768]{2,1,0:T(8,128)(2,1)}), bf16[16,128,768]{2,1,0:T(8,128)(2,1)}, u32[]{:S(2)}, u32[]{:S(2)}) %all-to-all-start.2) | async-done | bytes 3145760 | tf_op jit(solution)/shard_map/all_to_all | solution.py:141
  144.9 2.4 convert_reduce_fusion
  149.1 2.9 %pad_maximum_fusion = f32[1792,768]{0,1:T(8,128)} fusion(f32[768,768]{0,1:T(8,128)S(1)} %copy-done.1, f32[1024,768]{0,1:T(8,128)S(1)} %convolution_bitcast_fusion), kind=kLoop, calls=%fused_computation.6 | loop fusion | flops 1376256 | bytes 11010048 | tf_op jit(solution)/shard_map/concatenate | solution.py:81
  152.0 7.8 %reshape.166 = f32[2,896,768]{1,0,2:T(2,128)} reshape(f32[1792,768]{0,1:T(8,128)} %pad_maximum_fusion) | data formatting | bytes 11010048 | tf_op jit(solution)/shard_map/reshape | solution.py:84
  159.8 6.6 %constant_dynamic-slice_fusion = bf16[1,896,768]{1,0,2:T(2,128)(2,1)} fusion(f32[2,896,768]{1,0,2:T(2,128)} %reshape.166, s32[]{:T(128)S(6)} %select_n.19), kind=kLoop, calls=%fused_computation.64 | loop fusion | bytes 2752516 | tf_op jit(solution)/shard_map/jit(dynamic_index_in_dim)/dynamic_slice | solution.py:86
  166.4 6.9 %copy.22 = bf16[1,896,768]{2,1,0:T(8,128)(2,1)S(1)} copy(bf16[1,896,768]{1,0,2:T(2,128)(2,1)} %constant_dynamic-slice_fusion) | data formatting | bytes 2752512
  173.3 5.2 %collective-permute-start.15 = (bf16[896,768]{1,0:T(8,128)(2,1)S(1)}, bf16[896,768]{1,0:T(8,128)(2,1)}, u32[]{:S(2)}, u32[]{:S(2)}) collective-permute-start(bf16[896,768]{1,0:T(8,128)(2,1)S(1)} %bitcast.48), channel_id=1, source_target_pairs={{0,1},{1,0},{2,3},{3,2},{4,5},{5,4},{6,7},{7,6},{8,9},{9,8},{10,11... | collective-permute-start | bytes 4128776 | tf_op jit(solution)/shard_map/ppermute | solution.py:39
  181.1 1.4 scatter.9
  182.5 6.5 %constant_dynamic-slice_fusion.1 = f32[1,896,768]{1,0,2:T(1,128)} fusion(f32[2,896,768]{1,0,2:T(2,128)} %reshape.166, s32[]{:T(128)S(6)} %select_n.18), kind=kLoop, calls=%fused_computation.65 | loop fusion | bytes 5505028 | tf_op jit(solution)/shard_map/jit(dynamic_index_in_dim)/dynamic_slice | solution.py:85
  189.0 8.5 %copy.18 = f32[1,896,768]{2,1,0:T(8,128)} copy(f32[1,896,768]{1,0,2:T(1,128)} %constant_dynamic-slice_fusion.1) | data formatting | bytes 5505024 | tf_op jit(solution)/shard_map/jit(dynamic_index_in_dim)/dynamic_slice | solution.py:85
  197.5 3.5 %fusion.2 = bf16[896,768]{1,0:T(8,128)(2,1)} fusion(f32[1,896,768]{2,1,0:T(8,128)} %copy.18, bf16[896,768]{1,0:T(8,128)(2,1)} %collective-permute-done.15), kind=kLoop, calls=%fused_computation.10 | loop fusion | flops 2064384 | bytes 5505024 | tf_op jit(solution)/shard_map/convert_element_type | solution.py:94
  201.0 2.3 reshape.167
  203.9 28.5 %all_to_all.26 = bf16[64,16,768]{2,1,0:T(8,128)(2,1)S(1)} all-to-all(bf16[64,16,768]{2,1,0:T(8,128)(2,1)S(1)} %pad_maximum_fusion.2), channel_id=1, replica_groups=mesh['xh'=2,'y'=4,'xl'=2,'z'=4,'c'=2] {'xh','xl','y','z'}, dimensions={0} | all-to-all | bytes 3145728 | tf_op jit(solution)/shard_map/all_to_all | solution.py:97
  233.4 27.6 %all_to_all.27 = bf16[64,14,768]{2,1,0:T(8,128)(2,1)S(1)} all-to-all(bf16[64,14,768]{2,1,0:T(8,128)(2,1)S(1)} %broadcast_in_dim.73), channel_id=1, replica_groups=mesh['xh'=2,'y'=4,'xl'=2,'z'=4,'c'=2] {'xh','xl','y','z'}, dimensions={0} | all-to-all | bytes 2752512 | tf_op jit(solution)/shard_map/all_to_all | solution.py:43
  260.9 1.3 reshape.171
  262.2 3.7 %collective-permute-start.17 = (bf16[896,768]{1,0:T(8,128)(2,1)}, bf16[896,768]{1,0:T(8,128)(2,1)}, u32[]{:S(2)}, u32[]{:S(2)}) collective-permute-start(bf16[896,768]{1,0:T(8,128)(2,1)} %reshape.171), channel_id=1, source_target_pairs={{0,1},{1,0},{2,3},{3,2},{4,5},{5,4},{6,7},{7,6},{8,9},{9,8},{10,11... | collective-permute-start | bytes 4128776 | tf_op jit(solution)/shard_map/ppermute | solution.py:39
  265.9 2.6 convolution_convert_fusion.1
  268.5 2.4 convolution_convert_fusion
  270.9 1.3 fusion.20
  273.5 0.9 collective-permute-start.16
  275.3 1.3 broadcast_in_dim.74
  276.8 1.2 copy-done.2
  278.1 1.5 bitcast_dynamic-update-slice_fusion
  280.2 1.9 slice.192
  282.0 1.6 slice.193
  (85 shorter events, 11.4 us)
Async XLA Ops:
  0.6 1.9 copy-start
  4.0 2.8 copy-start.10
  6.8 49.0 %all-to-all-start = ((bf16[16,128,768]{2,1,0:T(8,128)(2,1)}), bf16[16,128,768]{2,1,0:T(8,128)(2,1)}, u32[]{:S(2)}, u32[]{:S(2)}) async-start(bf16[16,128,768]{2,1,0:T(8,128)(2,1)} %broadcast_in_dim.38), calls=%async_computation | async-start | bytes 6291456 | tf_op jit(solution)/shard_map/all_to_all | solution.py:43
  15.5 5.8 %collective-permute-start = (bf16[128,768]{1,0:T(8,128)(2,1)S(1)}, bf16[128,768]{1,0:T(8,128)(2,1)S(1)}, u32[]{:S(2)}, u32[]{:S(2)}) collective-permute-start(bf16[128,768]{1,0:T(8,128)(2,1)S(1)} %get-tuple-element.32), channel_id=1, source_target_pairs={{0,72},{8,0},{64,8},{72,64},{1,73},{9,1},{65,9},{73,65},{2,74},{10... | collective-permute-start | bytes 589832 | tf_op jit(solution)/shard_map/ppermute | solution.py:35
  18.0 6.8 %collective-permute-start.2 = (bf16[128,768]{1,0:T(8,128)(2,1)S(1)}, bf16[128,768]{1,0:T(8,128)(2,1)S(1)}, u32[]{:S(2)}, u32[]{:S(2)}) collective-permute-start(bf16[128,768]{1,0:T(8,128)(2,1)S(1)} %get-tuple-element.32), channel_id=1, source_target_pairs={{0,8},{8,64},{64,72},{72,0},{1,9},{9,65},{65,73},{73,1},{2,10},{10... | collective-permute-start | bytes 589832 | tf_op jit(solution)/shard_map/ppermute | solution.py:35
  21.3 5.2 %collective-permute-start.1 = (bf16[64,768]{1,0:T(8,128)(2,1)S(1)}, bf16[64,768]{1,0:T(8,128)(2,1)S(1)}, u32[]{:S(2)}, u32[]{:S(2)}) collective-permute-start(bf16[64,768]{1,0:T(8,128)(2,1)S(1)} %slice.171), channel_id=1, source_target_pairs={{0,72},{8,0},{64,8},{72,64},{1,73},{9,1},{65,9},{73,65},{2,74},{10... | collective-permute-start | bytes 294920 | tf_op jit(solution)/shard_map/ppermute | solution.py:35
  24.9 5.1 %collective-permute-start.3 = (bf16[64,768]{1,0:T(8,128)(2,1)S(1)}, bf16[64,768]{1,0:T(8,128)(2,1)S(1)}, u32[]{:S(2)}, u32[]{:S(2)}) collective-permute-start(bf16[64,768]{1,0:T(8,128)(2,1)S(1)} %slice.172), channel_id=1, source_target_pairs={{0,8},{8,64},{64,72},{72,0},{1,9},{9,65},{65,73},{73,1},{2,10},{10... | collective-permute-start | bytes 294920 | tf_op jit(solution)/shard_map/ppermute | solution.py:35
  31.4 4.7 %collective-permute-start.4 = (bf16[512,768]{1,0:T(8,128)(2,1)S(1)}, bf16[512,768]{1,0:T(8,128)(2,1)S(1)}, u32[]{:S(2)}, u32[]{:S(2)}) collective-permute-start(bf16[512,768]{1,0:T(8,128)(2,1)S(1)} %get-tuple-element.43), channel_id=1, source_target_pairs={{0,1},{1,0},{2,3},{3,2},{4,5},{5,4},{6,7},{7,6},{8,9},{9,8},{10,11... | collective-permute-start | bytes 2359304 | tf_op jit(solution)/shard_map/ppermute | solution.py:39
  65.6 3.9 %collective-permute-start.5 = (f32[512]{0:T(512)S(1)}, f32[512]{0:T(512)S(1)}, u32[]{:S(2)}, u32[]{:S(2)}) collective-permute-start(f32[512]{0:T(512)S(1)} %get-tuple-element.59), channel_id=1, source_target_pairs={{0,1},{1,0},{2,3},{3,2},{4,5},{5,4},{6,7},{7,6},{8,9},{9,8},{10,11... | collective-permute-start | bytes 6152 | tf_op jit(solution)/shard_map/ppermute | solution.py:39
  68.8 1.2 collective-permute-start.6
  69.9 13.9 %collective-permute-start.9 = (f32[2,4,128]{2,1,0:T(4,128)S(1)}, f32[2,4,128]{2,1,0:T(4,128)S(1)}, u32[]{:S(2)}, u32[]{:S(2)}) collective-permute-start(f32[2,4,128]{2,1,0:T(4,128)S(1)} %pad_maximum_fusion.5), channel_id=1, source_target_pairs={{0,64},{8,72},{64,0},{72,8},{1,65},{9,73},{65,1},{73,9},{2,66},{10... | collective-permute-start | bytes 12296 | tf_op jit(solution)/shard_map/ppermute | solution.py:35
  73.5 14.3 %all-to-all-start.1 = ((f32[16,1,2048]{2,1,0:T(1,128)}), f32[16,1,2048]{2,1,0:T(1,128)S(1)}, u32[]{:S(2)}, u32[]{:S(2)}) async-start(f32[16,1,2048]{2,1,0:T(1,128)} %broadcast_in_dim.39), calls=%async_computation.1 | async-start | bytes 262144 | tf_op jit(solution)/shard_map/all_to_all | solution.py:43
  81.1 3.7 %collective-permute-start.8 = (f32[2,4,128]{2,1,0:T(4,128)S(1)}, f32[2,4,128]{2,1,0:T(4,128)S(1)}, u32[]{:S(2)}, u32[]{:S(2)}) collective-permute-start(f32[2,4,128]{2,1,0:T(4,128)S(1)} %pad_maximum_fusion.5), channel_id=1, source_target_pairs={{0,8},{8,64},{64,72},{72,0},{1,9},{9,65},{65,73},{73,1},{2,10},{10... | collective-permute-start | bytes 12296 | tf_op jit(solution)/shard_map/ppermute | solution.py:35
  81.4 3.4 %collective-permute-start.7 = (f32[2,4,128]{2,1,0:T(4,128)S(1)}, f32[2,4,128]{2,1,0:T(4,128)S(1)}, u32[]{:S(2)}, u32[]{:S(2)}) collective-permute-start(f32[2,4,128]{2,1,0:T(4,128)S(1)} %pad_maximum_fusion.5), channel_id=1, source_target_pairs={{0,72},{8,0},{64,8},{72,64},{1,73},{9,1},{65,9},{73,65},{2,74},{10... | collective-permute-start | bytes 12296 | tf_op jit(solution)/shard_map/ppermute | solution.py:35
  92.8 6.1 %copy-start.4 = (bf16[2048,1024]{1,0:T(8,128)(2,1)}, bf16[2048,1024]{1,0:T(8,128)(2,1)S(1)}, u32[]{:S(2)}) copy-start(bf16[2048,1024]{1,0:T(8,128)(2,1)S(1)} %multiply_convert_fusion) | copy-start | bytes 12582916
  101.6 43.3 %all-to-all-start.2 = ((bf16[16,128,768]{2,1,0:T(8,128)(2,1)}), bf16[16,128,768]{2,1,0:T(8,128)(2,1)}, u32[]{:S(2)}, u32[]{:S(2)}) async-start(bf16[16,128,768]{2,1,0:T(8,128)(2,1)} %subtract_convert_fusion), calls=%async_computation.2 | async-start | bytes 6291456 | tf_op jit(solution)/shard_map/all_to_all | solution.py:141
  112.5 3.8 %collective-permute-start.10 = (bf16[512,768]{1,0:T(8,128)(2,1)S(1)}, bf16[512,768]{1,0:T(8,128)(2,1)S(1)}, u32[]{:S(2)}, u32[]{:S(2)}) collective-permute-start(bf16[512,768]{1,0:T(8,128)(2,1)S(1)} %slice.213), channel_id=1, source_target_pairs={{0,1},{1,0},{2,3},{3,2},{4,5},{5,4},{6,7},{7,6},{8,9},{9,8},{10,11... | collective-permute-start | bytes 2359304 | tf_op jit(solution)/shard_map/ppermute | solution.py:39
  116.5 5.6 %copy-start.3 = (f32[512,768]{1,0:T(8,128)}, f32[512,768]{1,0:T(8,128)S(1)}, u32[]{:S(2)}) copy-start(f32[512,768]{1,0:T(8,128)S(1)} %get-tuple-element.34) | copy-start | bytes 4718596
  116.5 14.9 %copy-start.8 = (bf16[128,768]{1,0:T(8,128)(2,1)S(1)}, bf16[128,768]{1,0:T(8,128)(2,1)}, u32[]{:S(2)}) copy-start(bf16[128,768]{1,0:T(8,128)(2,1)} %param.9) | copy-start | bytes 589828
  116.6 5.5 %collective-permute-start.11 = (bf16[64,768]{1,0:T(8,128)(2,1)S(1)}, bf16[64,768]{1,0:T(8,128)(2,1)S(1)}, u32[]{:S(2)}, u32[]{:S(2)}) collective-permute-start(bf16[64,768]{1,0:T(8,128)(2,1)S(1)} %get-tuple-element.39), channel_id=1, source_target_pairs={{0,8},{8,64},{64,72},{72,0},{1,9},{9,65},{65,73},{73,1},{2,10},{10... | collective-permute-start | bytes 294920 | tf_op jit(solution)/shard_map/ppermute | solution.py:35
  116.9 5.2 %collective-permute-start.13 = (bf16[64,768]{1,0:T(8,128)(2,1)S(1)}, bf16[64,768]{1,0:T(8,128)(2,1)S(1)}, u32[]{:S(2)}, u32[]{:S(2)}) collective-permute-start(bf16[64,768]{1,0:T(8,128)(2,1)S(1)} %get-tuple-element.40), channel_id=1, source_target_pairs={{0,72},{8,0},{64,8},{72,64},{1,73},{9,1},{65,9},{73,65},{2,74},{10... | collective-permute-start | bytes 294920 | tf_op jit(solution)/shard_map/ppermute | solution.py:35
  122.2 6.7 %collective-permute-start.12 = (bf16[128,768]{1,0:T(8,128)(2,1)S(1)}, bf16[128,768]{1,0:T(8,128)(2,1)S(1)}, u32[]{:S(2)}, u32[]{:S(2)}) collective-permute-start(bf16[128,768]{1,0:T(8,128)(2,1)S(1)} %pad_maximum_fusion.3), channel_id=1, source_target_pairs={{0,8},{8,64},{64,72},{72,0},{1,9},{9,65},{65,73},{73,1},{2,10},{10... | collective-permute-start | bytes 589832 | tf_op jit(solution)/shard_map/ppermute | solution.py:35
  123.7 5.3 %collective-permute-start.14 = (bf16[128,768]{1,0:T(8,128)(2,1)}, bf16[128,768]{1,0:T(8,128)(2,1)S(1)}, u32[]{:S(2)}, u32[]{:S(2)}) collective-permute-start(bf16[128,768]{1,0:T(8,128)(2,1)} %pad_maximum_fusion.4), channel_id=1, source_target_pairs={{0,72},{8,0},{64,8},{72,64},{1,73},{9,1},{65,9},{73,65},{2,74},{10... | collective-permute-start | bytes 589832 | tf_op jit(solution)/shard_map/ppermute | solution.py:35
  131.4 15.9 %copy-start.6 = (bf16[128,768]{1,0:T(8,128)(2,1)}, bf16[128,768]{1,0:T(8,128)(2,1)S(1)}, u32[]{:S(2)}) copy-start(bf16[128,768]{1,0:T(8,128)(2,1)S(1)} %divide_convert_fusion) | copy-start | bytes 589828
  131.4 15.9 %copy-start.11 = (f32[128]{0:T(128)S(1)}, f32[128]{0:T(128)}, u32[]{:S(2)}) copy-start(f32[128]{0:T(128)} %copy-done.10) | copy-start | bytes 1540
  133.3 14.7 %copy-start.7 = (bf16[128,1024]{1,0:T(8,128)(2,1)S(1)}, bf16[128,1024]{1,0:T(8,128)(2,1)}, u32[]{:S(2)}) copy-start(bf16[128,1024]{1,0:T(8,128)(2,1)} %param.8) | copy-start | bytes 786436
  147.3 0.8 copy-start.5
  147.3 1.8 copy-start.1
  148.1 4.0 %copy-start.12 = (f32[128]{0:T(128)}, f32[128]{0:T(128)S(1)}, u32[]{:S(2)}) copy-start(f32[128]{0:T(128)S(1)} %multiply_reduce_fusion.1) | copy-start | bytes 1540
  166.4 12.7 %copy-start.14 = (f32[128]{0:T(128)S(1)}, f32[128]{0:T(128)}, u32[]{:S(2)}) copy-start(f32[128]{0:T(128)} %get-tuple-element.35) | copy-start | bytes 1540
  173.3 24.1 %collective-permute-start.15 = (bf16[896,768]{1,0:T(8,128)(2,1)S(1)}, bf16[896,768]{1,0:T(8,128)(2,1)}, u32[]{:S(2)}, u32[]{:S(2)}) collective-permute-start(bf16[896,768]{1,0:T(8,128)(2,1)S(1)} %bitcast.48), channel_id=1, source_target_pairs={{0,1},{1,0},{2,3},{3,2},{4,5},{5,4},{6,7},{7,6},{8,9},{9,8},{10,11... | collective-permute-start | bytes 4128776 | tf_op jit(solution)/shard_map/ppermute | solution.py:39
  232.6 0.6 copy-start.9
  260.9 7.6 %copy-start.13 = (f32[128]{0:T(128)S(1)}, f32[128]{0:T(128)}, u32[]{:S(2)}) copy-start(f32[128]{0:T(128)} %copy-done.12) | copy-start | bytes 1540
  262.2 15.9 %collective-permute-start.17 = (bf16[896,768]{1,0:T(8,128)(2,1)}, bf16[896,768]{1,0:T(8,128)(2,1)}, u32[]{:S(2)}, u32[]{:S(2)}) collective-permute-start(bf16[896,768]{1,0:T(8,128)(2,1)} %reshape.171), channel_id=1, source_target_pairs={{0,1},{1,0},{2,3},{3,2},{4,5},{5,4},{6,7},{7,6},{8,9},{9,8},{10,11... | collective-permute-start | bytes 4128776 | tf_op jit(solution)/shard_map/ppermute | solution.py:39
  273.5 1.2 collective-permute-start.16
  276.6 1.3 copy-start.2

commit v2 on v1

v2 whole, which is shorter than its diff:
```python
import jax
import jax.numpy as jnp
from jax import lax
from jax.experimental import pallas as pl
from jax.experimental.pallas import tpu as pltpu
from jax.sharding import Mesh, PartitionSpec as P

sharpness_factor = 100.0
norm_eps = 1e-06
X = ("xh", "xl")
YZ = ("y", "z")
XYZ = ("xh", "xl", "y", "z")
ALL = ("xh", "y", "xl", "z", "c")
TILE = 256
f32 = jnp.float32
bf16 = jnp.bfloat16


def normalize_rows(features, weight):
    projected = jnp.dot(features, weight, preferred_element_type=f32)
    radius = jnp.sqrt(jnp.sum(projected * projected, axis=1, keepdims=True) + norm_eps)
    return (projected / radius, radius)


def from_x(v, k):
    return lax.ppermute(v, X, [(i, (i - k) % 4) for i in range(4)])


def from_core(v):
    return lax.ppermute(v, "c", [(0, 1), (1, 0)])


def spread(v, axes, n):
    return lax.all_to_all(jnp.broadcast_to(v[None], (n,) + v.shape), axes, 0, 0)


def gather_text(t):
    half = t.shape[0] // 2
    up = from_x(t, 1)
    down = from_x(t, 3)
    far = jnp.concatenate([from_x(up[:half], 1), from_x(down[half:], 3)], axis=0)
    mine = jnp.concatenate([t, up, far, down], axis=0)
    return jnp.concatenate([mine, from_core(mine)], axis=0)


def column_totals(part):
    n = part.shape[0] // 2
    both = part[:n] + from_core(part[n:]), part[n:] + from_core(part[:n])
    both = jnp.stack(both).reshape(2, 4, n // 4)
    total = both
    for k in (1, 3, 2):
        total = total + jnp.roll(from_x(both, k), k, axis=1)
    return total.reshape(-1)


def scatter_text(g):
    n = g.shape[0] // 2
    b = n // 4
    h = b // 2
    g = g[:n] + from_core(g[n:].astype(bf16)).astype(f32)
    g0, g1, g2, g3 = (g[k * b : (k + 1) * b] for k in range(4))
    low = from_x(g2[:h].astype(bf16), 3).astype(f32)
    high = from_x(g2[h:].astype(bf16), 1).astype(f32)
    g1 = jnp.concatenate([g1[:h] + low, g1[h:]], axis=0)
    g3 = jnp.concatenate([g3[:h], g3[h:] + high], axis=0)
    return g0 + from_x(g1.astype(bf16), 3).astype(f32) + from_x(g3.astype(bf16), 1).astype(f32)


def params():
    return pltpu.CompilerParams(vmem_limit_bytes=40 * 1024 * 1024)

def turned(row):
    return jnp.broadcast_to(row, (128, row.shape[1])).T


def logits_kernel(images, texts, logits, row_sum, column_sum):
    value = sharpness_factor * lax.dot_general(
        images[...], texts[...], (((1,), (1,)), ((), ())), preferred_element_type=f32
    )
    logits[...] = value
    e = jnp.exp(value - sharpness_factor)
    rows, columns = e.shape
    by_lane = e[:, :128]
    for k in range(1, columns // 128):
        by_lane = by_lane + e[:, k * 128 : (k + 1) * 128]
    row_sum[...] = jnp.sum(by_lane.T, axis=0, keepdims=True)
    by_column = jnp.sum(e, axis=0, keepdims=True)

    @pl.when(pl.program_id(0) == 0)
    def _():
        column_sum[...] = by_column

    @pl.when(pl.program_id(0) > 0)
    def _():
        column_sum[...] += by_column


def block_logits(images, texts):
    n, width = images.shape
    m = texts.shape[0]
    return pl.pallas_call(
        logits_kernel,
        grid=(n // TILE,),
        in_specs=[
            pl.BlockSpec((TILE, width), lambda i: (i, 0)),
            pl.BlockSpec((m, width), lambda i: (0, 0)),
        ],
        out_specs=[
            pl.BlockSpec((TILE, m), lambda i: (i, 0)),
            pl.BlockSpec((1, TILE), lambda i: (0, i)),
            pl.BlockSpec((1, m), lambda i: (0, 0)),
        ],
        out_shape=[
            jax.ShapeDtypeStruct((n, m), f32),
            jax.ShapeDtypeStruct((1, n), f32),
            jax.ShapeDtypeStruct((1, m), f32),
        ],
        compiler_params=params(),
        cost_estimate=pl.CostEstimate(
            flops=2 * n * m * width, bytes_accessed=4 * n * m + 2 * (n + m) * width, transcendentals=n * m
        ),
        name="block_logits",
    )(images, texts)


def weights_kernel(place, logits, row_parts, column_parts, texts, weights, grad):
    row_lse = jnp.log(jnp.sum(row_parts[...], axis=0, keepdims=True)) + sharpness_factor
    column_lse = jnp.log(jnp.sum(column_parts[...], axis=0, keepdims=True)) + sharpness_factor
    value = logits[...]
    rows, columns = value.shape
    row_lse = jnp.concatenate([turned(row_lse)] * (columns // 128), axis=1)
    w = (
        0.5 * sharpness_factor * (jnp.exp(value - row_lse) + jnp.exp(value - column_lse))
    ).astype(bf16)
    weights[...] = w
    part = jnp.dot(w, texts[...], preferred_element_type=f32)
    i = pl.program_id(0)
    per = rows // 128
    for k in range(per):
        here = jnp.where(place[0] == i * per + k, sharpness_factor, 0.0)
        grad[k * 128 : (k + 1) * 128, :] = (
            part[k * 128 : (k + 1) * 128] - here * texts[:128, :].astype(f32)
        ).astype(bf16)


def block_weights(place, logits, row_parts, column_parts, texts):
    n, m = logits.shape
    width = texts.shape[1]
    return pl.pallas_call(
        weights_kernel,
        grid=(n // TILE,),
        in_specs=[
            pl.BlockSpec(memory_space=pltpu.SMEM),
            pl.BlockSpec((TILE, m), lambda i: (i, 0)),
            pl.BlockSpec((row_parts.shape[0], TILE), lambda i: (0, i)),
            pl.BlockSpec(column_parts.shape, lambda i: (0, 0)),
            pl.BlockSpec((m, width), lambda i: (0, 0)),
        ],
        out_specs=[
            pl.BlockSpec((TILE, m), lambda i: (i, 0)),
            pl.BlockSpec((TILE, width), lambda i: (i, 0)),
        ],
        out_shape=[
            jax.ShapeDtypeStruct((n, m), bf16),
            jax.ShapeDtypeStruct((n, width), bf16),
        ],
        compiler_params=params(),
        cost_estimate=pl.CostEstimate(
            flops=2 * n * m * width,
            bytes_accessed=6 * n * m + 2 * (n + m) * width,
            transcendentals=2 * n * m,
        ),
        name="block_weights",
    )(place, logits, row_parts, column_parts, texts)


def text_kernel(weights, images, own, grad):
    part = lax.dot_general(
        weights[...], images[...], (((0,), (0,)), ((), ())), preferred_element_type=f32
    )
    i = pl.program_id(0)
    here = jnp.where(i == 0, sharpness_factor, 0.0)
    grad[128:, :] = part[128:]
    grad[:128, :] = part[:128] - here * own[...].astype(f32)


def block_text_grad(weights, images, own):
    n, m = weights.shape
    width = images.shape[1]
    return pl.pallas_call(
        text_kernel,
        grid=(m // TILE,),
        in_specs=[
            pl.BlockSpec((n, TILE), lambda i: (0, i)),
            pl.BlockSpec((n, width), lambda i: (0, 0)),
            pl.BlockSpec(own.shape, lambda i: (0, 0)),
        ],
        out_specs=pl.BlockSpec((TILE, width), lambda i: (i, 0)),
        out_shape=jax.ShapeDtypeStruct((m, width), f32),
        compiler_params=params(),
        cost_estimate=pl.CostEstimate(
            flops=2 * n * m * width, bytes_accessed=2 * n * m + 2 * n * width + 4 * m * width, transcendentals=0
        ),
        name="block_text_grad",
    )(weights, images, own)


def other_half(v, core):
    n = v.shape[1] // 2
    mine = lax.dynamic_slice_in_dim(v, core * n, n, axis=1)
    away = lax.dynamic_slice_in_dim(v, (1 - core) * n, n, axis=1)
    return jnp.concatenate([mine, from_core(away)], axis=0)


def back_rows(unit_rows, radius, emb_grad):
    along = jnp.sum(unit_rows * emb_grad, axis=1, keepdims=True)
    return ((emb_grad - unit_rows * along) / radius).astype(bf16)


def feature_grad(projected_grad, weight):
    return lax.dot_general(
        projected_grad, weight, (((1,), (1,)), ((), ())), preferred_element_type=f32
    ).astype(bf16)


def weight_grad(features, projected_grad):
    return lax.dot_general(
        features, projected_grad, (((0,), (0,)), ((), ())), preferred_element_type=f32
    )


def reduce_weights(image_term, text_term, loss_part, core):
    n = 64
    width = image_term.shape[1]
    image_blocks = image_term.astype(bf16).reshape(n, 8, width)
    text_blocks = text_term.astype(bf16).reshape(-1, 8, width)
    used = text_blocks.shape[0]
    hi = loss_part.astype(bf16)
    lo = (loss_part - hi.astype(f32)).astype(bf16)
    lanes = jnp.arange(width)
    extra = jnp.where(lanes == 0, hi, jnp.where(lanes == 1, lo, jnp.zeros((), bf16)))
    extra = jnp.broadcast_to(extra, (n - used, 8, width))
    sent = jnp.concatenate(
        [image_blocks, jnp.concatenate([text_blocks, extra], axis=0)], axis=1
    )
    got = jnp.sum(lax.all_to_all(sent, XYZ, 0, 0).astype(f32), axis=0)
    high = got.astype(bf16)
    low = jnp.broadcast_to((got[:, 0:1] + got[:, 1:2]), got.shape)
    low = (low - low.astype(bf16).astype(f32)).astype(bf16)
    total = (got[:, 0:1] + got[:, 1:2]).astype(bf16)
    row = lax.broadcasted_iota(jnp.int32, got.shape, 0)
    lane = lax.broadcasted_iota(jnp.int32, got.shape, 1)
    carries = (lax.axis_index(XYZ) >= used) & (row >= 8)
    block = jnp.where(carries, jnp.where(lane == 0, total, low), high)
    full = spread(block, XYZ, n)
    swapped = from_core(full)
    first = core == 0

    def whole(a, b):
        a, b = a.reshape(-1, width).astype(f32), b.reshape(-1, width).astype(f32)
        return jnp.concatenate([jnp.where(first, a, b), jnp.where(first, b, a)], axis=0)

    image = whole(full[:, :8], swapped[:, :8])
    text = whole(full[:used, 8:], swapped[:used, 8:])
    loss = full[n - 1, 8, :2].astype(f32) + swapped[n - 1, 8, :2].astype(f32)
    return image, text, loss[0] + loss[1]


def body(image_features, text_features, image_projection, text_projection):
    core = lax.axis_index("c")
    place = lax.axis_index(YZ)
    image_unit, image_radius = normalize_rows(image_features, image_projection)
    image_emb = image_unit.astype(bf16)
    own, width = image_emb.shape
    images = spread(image_emb, YZ, 16).reshape(16 * own, width)
    text_unit, text_radius = normalize_rows(text_features, text_projection)
    text_emb = text_unit.astype(bf16)
    texts = gather_text(text_emb)
    image_halves = other_half(image_features, core)
    text_halves = other_half(text_features, core)
    logits, row_part, column_part = block_logits(images, texts)
    matched = sharpness_factor * jnp.sum(image_emb.astype(f32) * text_emb.astype(f32), axis=1)
    row_parts = spread(row_part, YZ, 16).reshape(16, -1)
    column_total = column_totals(column_part.reshape(-1)).reshape(1, -1)
    weights, image_part = block_weights(
        place.reshape(1), logits, row_parts, column_total, texts
    )
    own_rows = jnp.sum(lax.dynamic_slice_in_dim(row_parts, place * own, own, axis=1), axis=0)
    loss_part = jnp.sum(
        jnp.log(own_rows)
        + jnp.log(column_total[0, :own])
        + 2.0 * (sharpness_factor - matched)
    )
    image_emb_grad = jnp.sum(
        lax.all_to_all(image_part.reshape(16, own, width), YZ, 0, 0).astype(f32), axis=0
    )
    text_part = block_text_grad(weights, images, image_emb)
    text_emb_grad = scatter_text(text_part)
    text_back = back_rows(text_unit, text_radius, text_emb_grad)
    image_back = back_rows(image_unit, image_radius, image_emb_grad)
    text_both = jnp.concatenate([text_back, from_core(text_back)], axis=0)
    image_both = jnp.concatenate([image_back, from_core(image_back)], axis=0)
    text_term = weight_grad(text_halves, text_both)
    image_term = weight_grad(image_halves, image_both)
    image_projection_grad, text_projection_grad, loss = reduce_weights(
        image_term, text_term, loss_part, core
    )
    pairs = own * 128
    return (
        loss / (2.0 * pairs),
        feature_grad(image_back, image_projection),
        feature_grad(text_back, text_projection),
        image_projection_grad,
        text_projection_grad,
    )


def solution(mesh):
    grid = Mesh(mesh.devices.reshape(2, 4, 2, 4, 2), ALL)
    rows = P(ALL, None)
    return jax.shard_map(
        body,
        mesh=grid,
        in_specs=(rows, rows, P(), P()),
        out_specs=(P(), rows, rows, P(), P()),
        check_vma=False,
    )
```

time: 286 us -> 233 us (0.81)
  local copies, waits for them, and re-layouts: 60 us -> 16.2 us
  blocking collectives: 56.1 us -> 27.6 us
  matrix products: 33 us -> 7.88 us
  Pallas kernels: 0 us -> 23.5 us
  waiting for transfers between devices: 51.6 us -> 68.4 us
  starting transfers between devices: 55.8 us -> 64.9 us
  other arithmetic: 22.9 us -> 18.5 us
    all_to_all x1 -> x0, blocking collectives: 28.5 us -> none  [reduce_weights(): got = jnp.sum(lax.all_to_all(sent, XYZ, 0, 0).astype(f32), axis=0)]
    dot_general x7 -> x4, matrix products: 29.7 us -> 5.5 us  [the longest x2 3.83 us: feature_grad(): lax.dot_general(projected_grad, weight, (((1,), (1,)), ((), ())), preferr...]
    pallas_call x0 -> x3, Pallas kernels: none -> 23.5 us  [the longest x1 9.16 us: block_weights(): pl.pallas_call(weights_kernel, grid=(n // TILE,), in_specs=[pl.BlockSpec(...]
    dynamic_slice x3 -> x2, local copies, waits for them, and re-layouts: 21.5 us -> 0.7 us  [other_half(): mine = lax.dynamic_slice_in_dim(v, core * n, n, axis=1)]
    all_to_all x1 -> x2, waiting for transfers between devices: 11.6 us -> 29.3 us  [the longest x1 22.4 us: reduce_weights(): got = jnp.sum(lax.all_to_all(sent, XYZ, 0, 0).astype(f32), axis=0)]
    convert_element_type x5 -> x4, other arithmetic: 12.9 us -> 1.48 us  [the longest x2 1.29 us: back_rows(): return ((emb_grad - unit_rows * along) / radius).astype(bf16)]
    reshape x3 -> x0, local copies, waits for them, and re-layouts: 11.4 us -> none  [the longest x1 7.81 us: reduce_weights(): both = both.reshape(2, half, width)]
    all_to_all x1 -> x2, starting transfers between devices: 4.51 us -> 10.8 us  [the longest x1 6.27 us: reduce_weights(): got = jnp.sum(lax.all_to_all(sent, XYZ, 0, 0).astype(f32), axis=0)]
  transfers between devices with their start and end apart: 21 -> 24, of which waited for: 15 -> 15; matrix products, arithmetic and copies ran while one was open for 15% -> 7% of each run, Pallas kernels for 0% -> 3%
where the time goes in v2:
time: 233 us; the launch traced here: 232 us
  waiting for transfers between devices  68.4 us (29%)
  starting transfers between devices  64.9 us (28%)
  blocking collectives  27.6 us (12%)
  Pallas kernels  23.5 us (10%)
  other arithmetic  18.5 us (8%)
  local copies, waits for them, and re-layouts  16.2 us (7%)
  matrix products  7.88 us (3%)
  between operations  4.8 us (2%)
    all_to_all x1, blocking collectives, spread(): return lax.all_to_all(jnp.broadcast_to(v[None], (n,) + v.shape), axes, 0, 0)  27.6 us
    all_to_all x1, waiting for transfers between devices, reduce_weights(): got = jnp.sum(lax.all_to_all(sent, XYZ, 0, 0).astype(f32), axis=0)  22.4 us
    all_to_all x2, waiting for transfers between devices, spread(): return lax.all_to_all(jnp.broadcast_to(v[None], (n,) + v.shape), axes, 0, 0)  22.4 us
    ppermute x9, starting transfers between devices, from_core(): return lax.ppermute(v, 'c', [(0, 1), (1, 0)])  20.5 us
    ppermute x11, starting transfers between devices, from_x(): return lax.ppermute(v, X, [(i, (i - k) % 4) for i in range(4)])  17.4 us
    all_to_all x2, starting transfers between devices, spread(): return lax.all_to_all(jnp.broadcast_to(v[None], (n,) + v.shape), axes, 0, 0)  16.2 us
    ppermute x11, waiting for transfers between devices, from_x(): return lax.ppermute(v, X, [(i, (i - k) % 4) for i in range(4)])  11.6 us
    unnamed x29, local copies, waits for them, and re-layouts  11.2 us
  transfers between devices with their start and end apart: 24, of which 15 were waited for; matrix products, arithmetic and copies ran while one was open for 7% of the time, Pallas kernels for 3%

profile of v2, /device:TPU:1, one launch (start us, length us, event | category | flops | bytes accessed | tf_op | source)
XLA Modules:
  0.0 231.7 jit_solution(2672507183295081028)
XLA Ops:
  0.7 1.9 multiply_reduce_fusion.3
  3.1 0.8 constant_dynamic-update-slice_fusion.4
  4.1 2.0 broadcast_in_dim.56
  6.1 8.6 %all-to-all-start = ((bf16[16,128,768]{2,1,0:T(8,128)(2,1)}), bf16[16,128,768]{2,1,0:T(8,128)(2,1)}, u32[]{:S(2)}, u32[]{:S(2)}) async-start(bf16[16,128,768]{2,1,0:T(8,128)(2,1)} %broadcast_in_dim.56), calls=%async_computation | async-start | bytes 6291456 | tf_op jit(solution)/shard_map/all_to_all | solution.py:34
  14.7 2.5 %collective-permute-start.1 = (bf16[128,768]{1,0:T(8,128)(2,1)S(1)}, bf16[128,768]{1,0:T(8,128)(2,1)S(1)}, u32[]{:S(2)}, u32[]{:S(2)}) collective-permute-start(bf16[128,768]{1,0:T(8,128)(2,1)S(1)} %get-tuple-element.18), channel_id=1, source_target_pairs={{0,72},{8,0},{64,8},{72,64},{1,73},{9,1},{65,9},{73,65},{2,74},{10... | collective-permute-start | bytes 589832 | tf_op jit(solution)/shard_map/ppermute | solution.py:26
  17.3 3.2 %collective-permute-done.1 = bf16[128,768]{1,0:T(8,128)(2,1)S(1)} collective-permute-done((bf16[128,768]{1,0:T(8,128)(2,1)S(1)}, bf16[128,768]{1,0:T(8,128)(2,1)S(1)}, u32[]{:S(2)}, u32[]{:S(2)}) %collective-permute-start.1) | collective-permute-done | bytes 196640 | tf_op jit(solution)/shard_map/ppermute | solution.py:26
  20.6 3.6 %collective-permute-start.2 = (bf16[64,768]{1,0:T(8,128)(2,1)S(1)}, bf16[64,768]{1,0:T(8,128)(2,1)S(1)}, u32[]{:S(2)}, u32[]{:S(2)}) collective-permute-start(bf16[64,768]{1,0:T(8,128)(2,1)S(1)} %slice.154), channel_id=1, source_target_pairs={{0,72},{8,0},{64,8},{72,64},{1,73},{9,1},{65,9},{73,65},{2,74},{10... | collective-permute-start | bytes 294920 | tf_op jit(solution)/shard_map/ppermute | solution.py:26
  24.2 0.7 constant_dynamic-update-slice_fusion.3
  24.9 0.8 collective-permute-done.2
  25.8 0.7 constant_dynamic-update-slice_fusion.2
  26.4 2.9 %collective-permute-done.4 = bf16[64,768]{1,0:T(8,128)(2,1)S(1)} collective-permute-done((bf16[64,768]{1,0:T(8,128)(2,1)S(1)}, bf16[64,768]{1,0:T(8,128)(2,1)S(1)}, u32[]{:S(2)}, u32[]{:S(2)}) %collective-permute-start.4) | collective-permute-done | bytes 98336 | tf_op jit(solution)/shard_map/ppermute | solution.py:26
  29.3 0.7 constant_dynamic-update-slice_fusion.1
  30.0 0.7 constant_dynamic-update-slice_fusion
  30.7 2.8 %collective-permute-start.5 = (bf16[512,768]{1,0:T(8,128)(2,1)}, bf16[512,768]{1,0:T(8,128)(2,1)S(1)}, u32[]{:S(2)}, u32[]{:S(2)}) collective-permute-start(bf16[512,768]{1,0:T(8,128)(2,1)} %get-tuple-element.35), channel_id=1, source_target_pairs={{0,1},{1,0},{2,3},{3,2},{4,5},{5,4},{6,7},{7,6},{8,9},{9,8},{10,11... | collective-permute-start | bytes 2359304 | tf_op jit(solution)/shard_map/ppermute | solution.py:30
  33.5 2.1 collective-permute-done.5
  35.6 19.5 %all-to-all-done = bf16[16,128,768]{2,1,0:T(8,128)(2,1)} async-done(((bf16[16,128,768]{2,1,0:T(8,128)(2,1)}), bf16[16,128,768]{2,1,0:T(8,128)(2,1)}, u32[]{:S(2)}, u32[]{:S(2)}) %all-to-all-start) | async-done | bytes 3145760 | tf_op jit(solution)/shard_map/all_to_all | solution.py:34
  55.1 7.8 %block_logits.1 = (f32[2048,1024]{1,0:T(8,128)S(1)}, f32[1,2048]{1,0:T(1,128)S(1)}, f32[1,1024]{1,0:T(1,128)S(1)}) custom-call(bf16[2048,768]{1,0:T(8,128)(2,1)} %bitcast.1.images, bf16[1024,768]{1,0:T(8,128)(2,1)S(1)} %constant_dynamic-update-slice_fusion.5.texts), custom_call_target="tpu_custom_call" | custom-call | flops 3221225472 | bytes 13107200 | tf_op jit(solution)/shard_map/block_logits/pallas_call | solution.py:101
  63.0 3.3 %copy-done.4 = f32[2048,1024]{1,0:T(8,128)} copy-done((f32[2048,1024]{1,0:T(8,128)}, f32[2048,1024]{1,0:T(8,128)S(1)}, u32[]{:S(2)}) %copy-start.4) | copy-done | bytes 8388632
  66.2 3.1 %collective-permute-start.6 = (f32[512]{0:T(512)S(1)}, f32[512]{0:T(512)S(1)}, u32[]{:S(2)}, u32[]{:S(2)}) collective-permute-start(f32[512]{0:T(512)S(1)} %bitcast.49), channel_id=1, source_target_pairs={{0,1},{1,0},{2,3},{3,2},{4,5},{5,4},{6,7},{7,6},{8,9},{9,8},{10,11... | collective-permute-start | bytes 6152 | tf_op jit(solution)/shard_map/ppermute | solution.py:30
  69.3 0.8 collective-permute-done.6
  70.5 2.8 %collective-permute-start.10 = (f32[2,4,128]{2,1,0:T(4,128)S(1)}, f32[2,4,128]{2,1,0:T(4,128)S(1)}, u32[]{:S(2)}, u32[]{:S(2)}) collective-permute-start(f32[2,4,128]{2,1,0:T(4,128)S(1)} %pad_maximum_fusion.4), channel_id=1, source_target_pairs={{0,64},{8,72},{64,0},{72,8},{1,65},{9,73},{65,1},{73,9},{2,66},{10... | collective-permute-start | bytes 12296 | tf_op jit(solution)/shard_map/ppermute | solution.py:26
  73.3 0.7 broadcast_in_dim.58
  74.1 7.5 %all-to-all-start.1 = ((f32[16,1,2048]{2,1,0:T(1,128)}), f32[16,1,2048]{2,1,0:T(1,128)S(1)}, u32[]{:S(2)}, u32[]{:S(2)}) async-start(f32[16,1,2048]{2,1,0:T(1,128)} %broadcast_in_dim.58), calls=%async_computation.1 | async-start | bytes 262144 | tf_op jit(solution)/shard_map/all_to_all | solution.py:34
  82.0 2.3 %collective-permute-start.8 = (f32[2,4,128]{2,1,0:T(4,128)S(1)}, f32[2,4,128]{2,1,0:T(4,128)S(1)}, u32[]{:S(2)}, u32[]{:S(2)}) collective-permute-start(f32[2,4,128]{2,1,0:T(4,128)S(1)} %pad_maximum_fusion.4), channel_id=1, source_target_pairs={{0,72},{8,0},{64,8},{72,64},{1,73},{9,1},{65,9},{73,65},{2,74},{10... | collective-permute-start | bytes 12296 | tf_op jit(solution)/shard_map/ppermute | solution.py:26
  84.4 1.0 collective-permute-done.9
  85.4 2.9 %all-to-all-done.1 = f32[16,1,2048]{2,1,0:T(1,128)S(1)} async-done(((f32[16,1,2048]{2,1,0:T(1,128)}), f32[16,1,2048]{2,1,0:T(1,128)S(1)}, u32[]{:S(2)}, u32[]{:S(2)}) %all-to-all-start.1) | async-done | bytes 131104 | tf_op jit(solution)/shard_map/all_to_all | solution.py:34
  88.4 9.2 %block_weights.1 = (bf16[2048,1024]{1,0:T(8,128)(2,1)S(1)}, bf16[2048,768]{1,0:T(8,128)(2,1)S(1)}) custom-call(s32[1]{0:T(128)} %bitcast.place, f32[2048,1024]{1,0:T(8,128)} %copy-done.4, f32[16,2048]{1,0:T(8,128)S(1)} %bitcast.45, f32[1,1024]{1,0:T(1,128)S(1)} %bitcast.47, bf16[1024,768]{1,0:T(8,128)(2,1)S(1)} %constant_dynamic-update-slice_fusion.5.texts), custom_call_target="tpu_custom_call" | custom-call | flops 3221225472 | bytes 17301504 | tf_op jit(solution)/shard_map/block_weights/pallas_call | solution.py:149
  97.5 1.7 copy-done.1
  99.2 1.9 copy-done.2
  101.2 4.5 %all-to-all-start.2 = ((bf16[16,128,768]{2,1,0:T(8,128)(2,1)}), bf16[16,128,768]{2,1,0:T(8,128)(2,1)}, u32[]{:S(2)}, u32[]{:S(2)}) async-start(bf16[16,128,768]{2,1,0:T(8,128)(2,1)} %bitcast.44), calls=%async_computation.2 | async-start | bytes 6291456 | tf_op jit(solution)/shard_map/all_to_all | solution.py:295
  105.7 2.2 copy-done.3
  107.8 6.5 %block_text_grad.1 = f32[1024,768]{1,0:T(8,128)S(1)} custom-call(bf16[2048,1024]{1,0:T(8,128)(2,1)S(1)} %copy-done.3, bf16[2048,768]{1,0:T(8,128)(2,1)} %bitcast.1.images, bf16[128,768]{1,0:T(8,128)(2,1)S(1)} %get-tuple-element.20.own), custom_call_target="tpu_custom_call" | custom-call | flops 3221225472 | bytes 10485760 | tf_op jit(solution)/shard_map/block_text_grad/pallas_call | solution.py:190
  114.4 1.9 collective-permute-start.13
  116.3 1.9 collective-permute-done.13
  118.2 1.3 fusion.35
  120.0 2.5 %collective-permute-start.16 = (bf16[64,768]{1,0:T(8,128)(2,1)S(1)}, bf16[64,768]{1,0:T(8,128)(2,1)S(1)}, u32[]{:S(2)}, u32[]{:S(2)}) collective-permute-start(bf16[64,768]{1,0:T(8,128)(2,1)S(1)} %get-tuple-element.28), channel_id=1, source_target_pairs={{0,72},{8,0},{64,8},{72,64},{1,73},{9,1},{65,9},{73,65},{2,74},{10... | collective-permute-start | bytes 294920 | tf_op jit(solution)/shard_map/ppermute | solution.py:26
  122.4 2.6 %collective-permute-done.14 = bf16[64,768]{1,0:T(8,128)(2,1)S(1)} collective-permute-done((bf16[64,768]{1,0:T(8,128)(2,1)S(1)}, bf16[64,768]{1,0:T(8,128)(2,1)S(1)}, u32[]{:S(2)}, u32[]{:S(2)}) %collective-permute-start.14) | collective-permute-done | bytes 98336 | tf_op jit(solution)/shard_map/ppermute | solution.py:26
  125.1 1.1 fusion.17
  126.2 0.9 collective-permute-start.15
  127.0 0.7 pad_maximum_fusion.3
  127.7 1.9 collective-permute-start.17
  129.6 0.7 constant_dynamic-slice_fusion.3
  130.3 1.6 collective-permute-start
  132.0 0.9 collective-permute-done.15
  133.0 1.2 multiply_reduce_fusion.1
  134.2 1.1 divide_convert_fusion
  135.4 2.5 %collective-permute-start.18 = (bf16[128,768]{1,0:T(8,128)(2,1)S(1)}, bf16[128,768]{1,0:T(8,128)(2,1)S(1)}, u32[]{:S(2)}, u32[]{:S(2)}) collective-permute-start(bf16[128,768]{1,0:T(8,128)(2,1)S(1)} %divide_convert_fusion), channel_id=1, source_target_pairs={{0,1},{1,0},{2,3},{3,2},{4,5},{5,4},{6,7},{7,6},{8,9},{9,8},{10,11... | collective-permute-start | bytes 589832 | tf_op jit(solution)/shard_map/ppermute | solution.py:30
  137.9 6.8 %all-to-all-done.2 = bf16[16,128,768]{2,1,0:T(8,128)(2,1)} async-done(((bf16[16,128,768]{2,1,0:T(8,128)(2,1)}), bf16[16,128,768]{2,1,0:T(8,128)(2,1)}, u32[]{:S(2)}, u32[]{:S(2)}) %all-to-all-start.2) | async-done | bytes 3145760 | tf_op jit(solution)/shard_map/all_to_all | solution.py:295
  144.7 2.4 %convert_reduce_fusion = f32[128,768]{1,0:T(8,128)S(1)} fusion(bf16[16,128,768]{2,1,0:T(8,128)(2,1)} %all-to-all-done.2), kind=kLoop, calls=%fused_computation | loop fusion | flops 3047424 | bytes 3538944 | tf_op jit(solution)/shard_map/reduce_sum | solution.py:294
  147.4 4.9 %collective-permute-start.11 = (bf16[128,768]{1,0:T(8,128)(2,1)S(1)}, bf16[128,768]{1,0:T(8,128)(2,1)S(1)}, u32[]{:S(2)}, u32[]{:S(2)}) collective-permute-start(bf16[128,768]{1,0:T(8,128)(2,1)S(1)} %divide_convert_fusion.1), channel_id=1, source_target_pairs={{0,1},{1,0},{2,3},{3,2},{4,5},{5,4},{6,7},{7,6},{8,9},{9,8},{10,11... | collective-permute-start | bytes 589832 | tf_op jit(solution)/shard_map/ppermute | solution.py:30
  152.3 0.6 fusion.30
  154.7 1.3 fusion.2
  156.0 1.3 maximum_maximum_fusion
  157.3 6.3 %all-to-all-start.3 = ((bf16[64,16,768]{2,1,0:T(8,128)(2,1)}), bf16[64,16,768]{2,1,0:T(8,128)(2,1)S(1)}, u32[]{:S(2)}, u32[]{:S(2)}) async-start(bf16[64,16,768]{2,1,0:T(8,128)(2,1)} %maximum_maximum_fusion), calls=%async_computation.3 | async-start | bytes 3145728 | tf_op jit(solution)/shard_map/all_to_all | solution.py:246
  163.6 22.4 %all-to-all-done.3 = bf16[64,16,768]{2,1,0:T(8,128)(2,1)S(1)} async-done(((bf16[64,16,768]{2,1,0:T(8,128)(2,1)}), bf16[64,16,768]{2,1,0:T(8,128)(2,1)S(1)}, u32[]{:S(2)}, u32[]{:S(2)}) %all-to-all-start.3) | async-done | bytes 1572896 | tf_op jit(solution)/shard_map/all_to_all | solution.py:246
  186.8 27.6 %all_to_all.25 = bf16[64,16,768]{2,1,0:T(8,128)(2,1)S(1)} all-to-all(bf16[64,16,768]{2,1,0:T(8,128)(2,1)S(1)} %broadcast_in_dim.67), channel_id=1, replica_groups=mesh['xh'=2,'y'=4,'xl'=2,'z'=4,'c'=2] {'xh','xl','y','z'}, dimensions={0} | all-to-all | bytes 3145728 | tf_op jit(solution)/shard_map/all_to_all | solution.py:34
  214.4 3.7 %collective-permute-start.19 = (bf16[64,16,768]{2,1,0:T(8,128)(2,1)S(1)}, bf16[64,16,768]{2,1,0:T(8,128)(2,1)}, u32[]{:S(2)}, u32[]{:S(2)}) collective-permute-start(bf16[64,16,768]{2,1,0:T(8,128)(2,1)S(1)} %all_to_all.25), channel_id=1, source_target_pairs={{0,1},{1,0},{2,3},{3,2},{4,5},{5,4},{6,7},{7,6},{8,9},{9,8},{10,11... | collective-permute-start | bytes 4718600 | tf_op jit(solution)/shard_map/ppermute | solution.py:30
  218.1 2.5 %convolution_convert_fusion.3 = bf16[128,768]{1,0:T(8,128)(2,1)} fusion(bf16[128,768]{1,0:T(8,128)(2,1)S(1)} %divide_convert_fusion, bf16[768,768]{1,0:T(8,128)(2,1)} %param.7), kind=kOutput, calls=%fused_computation.20 | convolution fusion | flops 151093248 | bytes 1572864 | tf_op jit(solution)/shard_map/dot_general | solution.py:221
  220.6 1.3 convolution_convert_fusion.2
  221.9 0.7 fusion.26
  223.2 1.2 fusion.4
  224.4 1.6 pad_maximum_fusion.1
  226.0 1.4 fusion
  227.4 1.9 pad_maximum_fusion
  (74 shorter events, 4.7 us)
Async XLA Ops:
  0.6 2.0 copy-start
  0.6 2.0 copy-start.9
  2.6 1.5 copy-start.7
  3.1 0.8 copy-start.5
  6.1 49.0 %all-to-all-start = ((bf16[16,128,768]{2,1,0:T(8,128)(2,1)}), bf16[16,128,768]{2,1,0:T(8,128)(2,1)}, u32[]{:S(2)}, u32[]{:S(2)}) async-start(bf16[16,128,768]{2,1,0:T(8,128)(2,1)} %broadcast_in_dim.56), calls=%async_computation | async-start | bytes 6291456 | tf_op jit(solution)/shard_map/all_to_all | solution.py:34
  14.7 5.8 %collective-permute-start.1 = (bf16[128,768]{1,0:T(8,128)(2,1)S(1)}, bf16[128,768]{1,0:T(8,128)(2,1)S(1)}, u32[]{:S(2)}, u32[]{:S(2)}) collective-permute-start(bf16[128,768]{1,0:T(8,128)(2,1)S(1)} %get-tuple-element.18), channel_id=1, source_target_pairs={{0,72},{8,0},{64,8},{72,64},{1,73},{9,1},{65,9},{73,65},{2,74},{10... | collective-permute-start | bytes 589832 | tf_op jit(solution)/shard_map/ppermute | solution.py:26
  17.3 6.8 %collective-permute-start.3 = (bf16[128,768]{1,0:T(8,128)(2,1)S(1)}, bf16[128,768]{1,0:T(8,128)(2,1)S(1)}, u32[]{:S(2)}, u32[]{:S(2)}) collective-permute-start(bf16[128,768]{1,0:T(8,128)(2,1)S(1)} %get-tuple-element.18), channel_id=1, source_target_pairs={{0,8},{8,64},{64,72},{72,0},{1,9},{9,65},{65,73},{73,1},{2,10},{10... | collective-permute-start | bytes 589832 | tf_op jit(solution)/shard_map/ppermute | solution.py:26
  20.6 5.2 %collective-permute-start.2 = (bf16[64,768]{1,0:T(8,128)(2,1)S(1)}, bf16[64,768]{1,0:T(8,128)(2,1)S(1)}, u32[]{:S(2)}, u32[]{:S(2)}) collective-permute-start(bf16[64,768]{1,0:T(8,128)(2,1)S(1)} %slice.154), channel_id=1, source_target_pairs={{0,72},{8,0},{64,8},{72,64},{1,73},{9,1},{65,9},{73,65},{2,74},{10... | collective-permute-start | bytes 294920 | tf_op jit(solution)/shard_map/ppermute | solution.py:26
  24.2 5.1 %collective-permute-start.4 = (bf16[64,768]{1,0:T(8,128)(2,1)S(1)}, bf16[64,768]{1,0:T(8,128)(2,1)S(1)}, u32[]{:S(2)}, u32[]{:S(2)}) collective-permute-start(bf16[64,768]{1,0:T(8,128)(2,1)S(1)} %slice.155), channel_id=1, source_target_pairs={{0,8},{8,64},{64,72},{72,0},{1,9},{9,65},{65,73},{73,1},{2,10},{10... | collective-permute-start | bytes 294920 | tf_op jit(solution)/shard_map/ppermute | solution.py:26
  30.7 4.9 %collective-permute-start.5 = (bf16[512,768]{1,0:T(8,128)(2,1)}, bf16[512,768]{1,0:T(8,128)(2,1)S(1)}, u32[]{:S(2)}, u32[]{:S(2)}) collective-permute-start(bf16[512,768]{1,0:T(8,128)(2,1)} %get-tuple-element.35), channel_id=1, source_target_pairs={{0,1},{1,0},{2,3},{3,2},{4,5},{5,4},{6,7},{7,6},{8,9},{9,8},{10,11... | collective-permute-start | bytes 2359304 | tf_op jit(solution)/shard_map/ppermute | solution.py:30
  63.0 3.3 %copy-start.4 = (f32[2048,1024]{1,0:T(8,128)}, f32[2048,1024]{1,0:T(8,128)S(1)}, u32[]{:S(2)}) copy-start(f32[2048,1024]{1,0:T(8,128)S(1)} %get-tuple-element.10.logits) | copy-start | bytes 25165828
  66.2 3.9 %collective-permute-start.6 = (f32[512]{0:T(512)S(1)}, f32[512]{0:T(512)S(1)}, u32[]{:S(2)}, u32[]{:S(2)}) collective-permute-start(f32[512]{0:T(512)S(1)} %bitcast.49), channel_id=1, source_target_pairs={{0,1},{1,0},{2,3},{3,2},{4,5},{5,4},{6,7},{7,6},{8,9},{9,8},{10,11... | collective-permute-start | bytes 6152 | tf_op jit(solution)/shard_map/ppermute | solution.py:30
  69.3 1.2 collective-permute-start.7
  70.5 13.9 %collective-permute-start.10 = (f32[2,4,128]{2,1,0:T(4,128)S(1)}, f32[2,4,128]{2,1,0:T(4,128)S(1)}, u32[]{:S(2)}, u32[]{:S(2)}) collective-permute-start(f32[2,4,128]{2,1,0:T(4,128)S(1)} %pad_maximum_fusion.4), channel_id=1, source_target_pairs={{0,64},{8,72},{64,0},{72,8},{1,65},{9,73},{65,1},{73,9},{2,66},{10... | collective-permute-start | bytes 12296 | tf_op jit(solution)/shard_map/ppermute | solution.py:26
  74.1 14.2 %all-to-all-start.1 = ((f32[16,1,2048]{2,1,0:T(1,128)}), f32[16,1,2048]{2,1,0:T(1,128)S(1)}, u32[]{:S(2)}, u32[]{:S(2)}) async-start(f32[16,1,2048]{2,1,0:T(1,128)} %broadcast_in_dim.58), calls=%async_computation.1 | async-start | bytes 262144 | tf_op jit(solution)/shard_map/all_to_all | solution.py:34
  81.6 3.7 %collective-permute-start.9 = (f32[2,4,128]{2,1,0:T(4,128)S(1)}, f32[2,4,128]{2,1,0:T(4,128)S(1)}, u32[]{:S(2)}, u32[]{:S(2)}) collective-permute-start(f32[2,4,128]{2,1,0:T(4,128)S(1)} %pad_maximum_fusion.4), channel_id=1, source_target_pairs={{0,8},{8,64},{64,72},{72,0},{1,9},{9,65},{65,73},{73,1},{2,10},{10... | collective-permute-start | bytes 12296 | tf_op jit(solution)/shard_map/ppermute | solution.py:26
  82.0 3.3 %collective-permute-start.8 = (f32[2,4,128]{2,1,0:T(4,128)S(1)}, f32[2,4,128]{2,1,0:T(4,128)S(1)}, u32[]{:S(2)}, u32[]{:S(2)}) collective-permute-start(f32[2,4,128]{2,1,0:T(4,128)S(1)} %pad_maximum_fusion.4), channel_id=1, source_target_pairs={{0,72},{8,0},{64,8},{72,64},{1,73},{9,1},{65,9},{73,65},{2,74},{10... | collective-permute-start | bytes 12296 | tf_op jit(solution)/shard_map/ppermute | solution.py:26
  97.5 1.7 copy-start.1
  99.2 1.9 copy-start.2
  101.2 43.6 %all-to-all-start.2 = ((bf16[16,128,768]{2,1,0:T(8,128)(2,1)}), bf16[16,128,768]{2,1,0:T(8,128)(2,1)}, u32[]{:S(2)}, u32[]{:S(2)}) async-start(bf16[16,128,768]{2,1,0:T(8,128)(2,1)} %bitcast.44), calls=%async_computation.2 | async-start | bytes 6291456 | tf_op jit(solution)/shard_map/all_to_all | solution.py:295
  105.7 2.2 copy-start.3
  114.4 3.8 %collective-permute-start.13 = (bf16[512,768]{1,0:T(8,128)(2,1)S(1)}, bf16[512,768]{1,0:T(8,128)(2,1)S(1)}, u32[]{:S(2)}, u32[]{:S(2)}) collective-permute-start(bf16[512,768]{1,0:T(8,128)(2,1)S(1)} %slice.228), channel_id=1, source_target_pairs={{0,1},{1,0},{2,3},{3,2},{4,5},{5,4},{6,7},{7,6},{8,9},{9,8},{10,11... | collective-permute-start | bytes 2359304 | tf_op jit(solution)/shard_map/ppermute | solution.py:30
  119.5 10.1 %copy-start.10 = (bf16[128,1024]{1,0:T(8,128)(2,1)S(1)}, bf16[128,1024]{1,0:T(8,128)(2,1)}, u32[]{:S(2)}) copy-start(bf16[128,1024]{1,0:T(8,128)(2,1)} %param.4) | copy-start | bytes 786436
  119.5 12.4 %copy-start.11 = (bf16[128,768]{1,0:T(8,128)(2,1)S(1)}, bf16[128,768]{1,0:T(8,128)(2,1)}, u32[]{:S(2)}) copy-start(bf16[128,768]{1,0:T(8,128)(2,1)} %param.5) | copy-start | bytes 589828
  119.5 13.5 %copy-start.8 = (f32[128,768]{1,0:T(8,128)S(1)}, f32[128,768]{1,0:T(8,128)}, u32[]{:S(2)}) copy-start(f32[128,768]{1,0:T(8,128)} %copy-done.7) | copy-start | bytes 1179652
  119.5 5.5 %collective-permute-start.14 = (bf16[64,768]{1,0:T(8,128)(2,1)S(1)}, bf16[64,768]{1,0:T(8,128)(2,1)S(1)}, u32[]{:S(2)}, u32[]{:S(2)}) collective-permute-start(bf16[64,768]{1,0:T(8,128)(2,1)S(1)} %get-tuple-element.27), channel_id=1, source_target_pairs={{0,8},{8,64},{64,72},{72,0},{1,9},{9,65},{65,73},{73,1},{2,10},{10... | collective-permute-start | bytes 294920 | tf_op jit(solution)/shard_map/ppermute | solution.py:26
  120.0 5.1 %collective-permute-start.16 = (bf16[64,768]{1,0:T(8,128)(2,1)S(1)}, bf16[64,768]{1,0:T(8,128)(2,1)S(1)}, u32[]{:S(2)}, u32[]{:S(2)}) collective-permute-start(bf16[64,768]{1,0:T(8,128)(2,1)S(1)} %get-tuple-element.28), channel_id=1, source_target_pairs={{0,72},{8,0},{64,8},{72,64},{1,73},{9,1},{65,9},{73,65},{2,74},{10... | collective-permute-start | bytes 294920 | tf_op jit(solution)/shard_map/ppermute | solution.py:26
  126.2 6.7 %collective-permute-start.15 = (bf16[128,768]{1,0:T(8,128)(2,1)S(1)}, bf16[128,768]{1,0:T(8,128)(2,1)S(1)}, u32[]{:S(2)}, u32[]{:S(2)}) collective-permute-start(bf16[128,768]{1,0:T(8,128)(2,1)S(1)} %pad_maximum_fusion.2), channel_id=1, source_target_pairs={{0,8},{8,64},{64,72},{72,0},{1,9},{9,65},{65,73},{73,1},{2,10},{10... | collective-permute-start | bytes 589832 | tf_op jit(solution)/shard_map/ppermute | solution.py:26
  127.7 5.3 %collective-permute-start.17 = (bf16[128,768]{1,0:T(8,128)(2,1)}, bf16[128,768]{1,0:T(8,128)(2,1)S(1)}, u32[]{:S(2)}, u32[]{:S(2)}) collective-permute-start(bf16[128,768]{1,0:T(8,128)(2,1)} %pad_maximum_fusion.3), channel_id=1, source_target_pairs={{0,72},{8,0},{64,8},{72,64},{1,73},{9,1},{65,9},{73,65},{2,74},{10... | collective-permute-start | bytes 589832 | tf_op jit(solution)/shard_map/ppermute | solution.py:26
  130.3 24.4 %collective-permute-start = (bf16[128,512]{1,0:T(8,128)(2,1)}, bf16[128,512]{1,0:T(8,128)(2,1)}, u32[]{:S(2)}, u32[]{:S(2)}) collective-permute-start(bf16[128,512]{1,0:T(8,128)(2,1)} %get-tuple-element.32), channel_id=1, source_target_pairs={{0,1},{1,0},{2,3},{3,2},{4,5},{5,4},{6,7},{7,6},{8,9},{9,8},{10,11... | collective-permute-start | bytes 393224 | tf_op jit(solution)/shard_map/ppermute | solution.py:30
  131.9 22.4 %collective-permute-start.12 = (bf16[128,384]{1,0:T(8,128)(2,1)S(1)}, bf16[128,384]{1,0:T(8,128)(2,1)S(1)}, u32[]{:S(2)}, u32[]{:S(2)}) collective-permute-start(bf16[128,384]{1,0:T(8,128)(2,1)S(1)} %get-tuple-element.34), channel_id=1, source_target_pairs={{0,1},{1,0},{2,3},{3,2},{4,5},{5,4},{6,7},{7,6},{8,9},{9,8},{10,11... | collective-permute-start | bytes 294920 | tf_op jit(solution)/shard_map/ppermute | solution.py:30
  135.4 11.7 %copy-start.6 = (f32[128,768]{1,0:T(8,128)S(1)}, f32[128,768]{1,0:T(8,128)}, u32[]{:S(2)}) copy-start(f32[128,768]{1,0:T(8,128)} %copy-done.5) | copy-start | bytes 1179652
  135.4 18.9 %collective-permute-start.18 = (bf16[128,768]{1,0:T(8,128)(2,1)S(1)}, bf16[128,768]{1,0:T(8,128)(2,1)S(1)}, u32[]{:S(2)}, u32[]{:S(2)}) collective-permute-start(bf16[128,768]{1,0:T(8,128)(2,1)S(1)} %divide_convert_fusion), channel_id=1, source_target_pairs={{0,1},{1,0},{2,3},{3,2},{4,5},{5,4},{6,7},{7,6},{8,9},{9,8},{10,11... | collective-permute-start | bytes 589832 | tf_op jit(solution)/shard_map/ppermute | solution.py:30
  147.4 7.2 %collective-permute-start.11 = (bf16[128,768]{1,0:T(8,128)(2,1)S(1)}, bf16[128,768]{1,0:T(8,128)(2,1)S(1)}, u32[]{:S(2)}, u32[]{:S(2)}) collective-permute-start(bf16[128,768]{1,0:T(8,128)(2,1)S(1)} %divide_convert_fusion.1), channel_id=1, source_target_pairs={{0,1},{1,0},{2,3},{3,2},{4,5},{5,4},{6,7},{7,6},{8,9},{9,8},{10,11... | collective-permute-start | bytes 589832 | tf_op jit(solution)/shard_map/ppermute | solution.py:30
  157.3 28.7 %all-to-all-start.3 = ((bf16[64,16,768]{2,1,0:T(8,128)(2,1)}), bf16[64,16,768]{2,1,0:T(8,128)(2,1)S(1)}, u32[]{:S(2)}, u32[]{:S(2)}) async-start(bf16[64,16,768]{2,1,0:T(8,128)(2,1)} %maximum_maximum_fusion), calls=%async_computation.3 | async-start | bytes 3145728 | tf_op jit(solution)/shard_map/all_to_all | solution.py:246
  214.4 7.5 %collective-permute-start.19 = (bf16[64,16,768]{2,1,0:T(8,128)(2,1)S(1)}, bf16[64,16,768]{2,1,0:T(8,128)(2,1)}, u32[]{:S(2)}, u32[]{:S(2)}) collective-permute-start(bf16[64,16,768]{2,1,0:T(8,128)(2,1)S(1)} %all_to_all.25), channel_id=1, source_target_pairs={{0,1},{1,0},{2,3},{3,2},{4,5},{5,4},{6,7},{7,6},{8,9},{9,8},{10,11... | collective-permute-start | bytes 4718600 | tf_op jit(solution)/shard_map/ppermute | solution.py:30

commit v3 on v2

v3 whole, which is shorter than its diff:
```python
import jax
import jax.numpy as jnp
from jax import lax
from jax.experimental import pallas as pl
from jax.experimental.pallas import tpu as pltpu
from jax.sharding import Mesh, PartitionSpec as P

sharpness_factor = 100.0
norm_eps = 1e-06
X = ("xh", "xl")
PAIR_Z = ("xl", "z")
PAIR_YZ = ("xl", "y", "z")
PAIR_ZC = ("xl", "z", "c")
ALL = ("xh", "y", "xl", "z", "c")
TILE = 512
LTILE = 512
f32 = jnp.float32
bf16 = jnp.bfloat16


def normalize_rows(features, weight):
    projected = jnp.dot(features, weight, preferred_element_type=f32)
    radius = jnp.sqrt(jnp.sum(projected * projected, axis=1, keepdims=True) + norm_eps)
    return (projected / radius, radius)


def from_core(v):
    return lax.ppermute(v, "c", [(0, 1), (1, 0)])


def from_mirror(v):
    return lax.ppermute(v, X, [(i, 3 - i) for i in range(4)])


def from_y(v, k):
    return lax.ppermute(v, "y", [(i, (i - k) % 4) for i in range(4)])


def spread(v, axes, n):
    return lax.all_to_all(jnp.broadcast_to(v[None], (n,) + v.shape), axes, 0, 0)


def gather_text(t):
    n = t.shape[0]
    pair = jnp.concatenate([t, from_mirror(t)], axis=0)
    up = from_y(pair, 1)
    down = from_y(pair, 3)
    far = [from_y(up[:n], 1), from_y(down[n:], 3)]
    return jnp.concatenate([pair, up] + far + [down], axis=0)


def column_totals(part):
    part = part.reshape(4, 2, -1)
    part = part + from_mirror(part)[:, ::-1]
    total = part
    for k in (1, 3, 2):
        total = total + jnp.roll(from_y(part, k), k, axis=0)
    return total.reshape(1, -1)


def plus(*parts):
    return sum(p.astype(f32) for p in parts)


def scatter_text(g):
    b = g.shape[0] // 4
    h = b // 2
    g0, g1, g2, g3 = (g[k * b : (k + 1) * b] for k in range(4))
    low = from_y(g2[:h], 3)
    high = from_y(g2[h:], 1)
    g1 = jnp.concatenate([plus(g1[:h], low).astype(bf16), g1[h:]], axis=0)
    g3 = jnp.concatenate([g3[:h], plus(g3[h:], high).astype(bf16)], axis=0)
    g0 = plus(g0, from_y(g1, 3), from_y(g3, 1))
    return g0[:h] + from_mirror(g0[h:].astype(bf16)).astype(f32)


def params():
    return pltpu.CompilerParams(vmem_limit_bytes=40 * 1024 * 1024)


def logits_kernel(images, texts, logits, row_sum, column_sum):
    value = sharpness_factor * lax.dot_general(
        images[...], texts[...], (((1,), (1,)), ((), ())), preferred_element_type=f32
    )
    logits[...] = value
    e = jnp.exp(value - sharpness_factor)
    by_lane = e[:, :128]
    for k in range(1, e.shape[1] // 128):
        by_lane = by_lane + e[:, k * 128 : (k + 1) * 128]
    row_sum[...] = jnp.sum(by_lane.T, axis=0, keepdims=True)
    by_column = jnp.sum(e, axis=0, keepdims=True)

    @pl.when(pl.program_id(0) == 0)
    def _():
        column_sum[...] = by_column

    @pl.when(pl.program_id(0) > 0)
    def _():
        column_sum[...] += by_column


def block_logits(images, texts):
    n, width = images.shape
    m = texts.shape[0]
    return pl.pallas_call(
        logits_kernel,
        grid=(n // LTILE,),
        in_specs=[
            pl.BlockSpec((LTILE, width), lambda i: (i, 0)),
            pl.BlockSpec((m, width), lambda i: (0, 0)),
        ],
        out_specs=[
            pl.BlockSpec((LTILE, m), lambda i: (i, 0)),
            pl.BlockSpec((1, LTILE), lambda i: (0, i)),
            pl.BlockSpec((1, m), lambda i: (0, 0)),
        ],
        out_shape=[
            jax.ShapeDtypeStruct((n, m), f32),
            jax.ShapeDtypeStruct((1, n), f32),
            jax.ShapeDtypeStruct((1, m), f32),
        ],
        compiler_params=params(),
        cost_estimate=pl.CostEstimate(
            flops=2 * n * m * width, bytes_accessed=4 * n * m + 2 * (n + m) * width, transcendentals=n * m
        ),
        name="block_logits",
    )(images, texts)


def grads_kernel(place, logits, row_parts, column_parts, images, texts, own, image_part, text_part, total):
    i = pl.program_id(0)
    row_lse = jnp.log(jnp.sum(row_parts[...], axis=0, keepdims=True)) + sharpness_factor
    column_lse = jnp.log(jnp.sum(column_parts[...], axis=0, keepdims=True)) + sharpness_factor
    value = logits[...]
    rows, columns = value.shape
    by_row = jnp.broadcast_to(row_lse, (128, rows)).T
    by_row = jnp.concatenate([by_row] * (columns // 128), axis=1)
    weights = (
        0.5 * sharpness_factor * (jnp.exp(value - by_row) + jnp.exp(value - column_lse))
    ).astype(bf16)
    part = jnp.dot(weights, texts[...], preferred_element_type=f32)
    per = rows // 128
    for k in range(per):
        here = jnp.where(place[0] == i * per + k, sharpness_factor, 0.0)
        image_part[k * 128 : (k + 1) * 128, :] = (
            part[k * 128 : (k + 1) * 128] - here * texts[:128, :].astype(f32)
        ).astype(bf16)
    share = lax.dot_general(
        weights, images[...], (((0,), (0,)), ((), ())), preferred_element_type=f32
    )

    @pl.when(i == 0)
    def _():
        total[...] = share

    @pl.when(i > 0)
    def _():
        total[...] += share

    @pl.when(i == pl.num_programs(0) - 1)
    def _():
        text_part[:128, :] = (total[:128, :] - sharpness_factor * own[...].astype(f32)).astype(bf16)
        text_part[128:, :] = total[128:, :].astype(bf16)


def block_grads(place, logits, row_parts, column_parts, images, texts, own):
    n, m = logits.shape
    width = texts.shape[1]
    return pl.pallas_call(
        grads_kernel,
        grid=(n // TILE,),
        in_specs=[
            pl.BlockSpec(memory_space=pltpu.SMEM),
            pl.BlockSpec((TILE, m), lambda i: (i, 0)),
            pl.BlockSpec((row_parts.shape[0], TILE), lambda i: (0, i)),
            pl.BlockSpec(column_parts.shape, lambda i: (0, 0)),
            pl.BlockSpec((TILE, width), lambda i: (i, 0)),
            pl.BlockSpec((m, width), lambda i: (0, 0)),
            pl.BlockSpec(own.shape, lambda i: (0, 0)),
        ],
        out_specs=[
            pl.BlockSpec((TILE, width), lambda i: (i, 0)),
            pl.BlockSpec((m, width), lambda i: (0, 0)),
        ],
        out_shape=[
            jax.ShapeDtypeStruct((n, width), bf16),
            jax.ShapeDtypeStruct((m, width), bf16),
        ],
        scratch_shapes=[pltpu.VMEM((m, width), f32)],
        compiler_params=params(),
        cost_estimate=pl.CostEstimate(
            flops=4 * n * m * width,
            bytes_accessed=4 * n * m + 4 * (n + m) * width,
            transcendentals=2 * n * m,
        ),
        name="block_grads",
    )(place, logits, row_parts, column_parts, images, texts, own)


def whole_kernel(core, mine, other, image, text):
    h = pl.program_id(0)
    n, rows, width = mine.shape
    half = rows // 2
    used = text.shape[0] // half

    def put(src):
        image[...] = src[:, :half].astype(f32).reshape(image.shape)
        text[...] = src[:used, half:].astype(f32).reshape(text.shape)

    @pl.when(h == core[0])
    def _():
        put(mine)

    @pl.when(h != core[0])
    def _():
        put(other)


def whole_terms(core, mine, other, used):
    n, rows, width = mine.shape
    half = rows // 2
    block = pl.BlockSpec(mine.shape, lambda h: (0, 0, 0))
    return pl.pallas_call(
        whole_kernel,
        grid=(2,),
        in_specs=[pl.BlockSpec(memory_space=pltpu.SMEM), block, block],
        out_specs=[
            pl.BlockSpec((n * half, width), lambda h: (h, 0)),
            pl.BlockSpec((used * half, width), lambda h: (h, 0)),
        ],
        out_shape=[
            jax.ShapeDtypeStruct((2 * n * half, width), f32),
            jax.ShapeDtypeStruct((2 * used * half, width), f32),
        ],
        compiler_params=params(),
        cost_estimate=pl.CostEstimate(flops=0, bytes_accessed=8 * n * rows * width, transcendentals=0),
        name="whole_terms",
    )(core, mine, other)


def other_half(v, core):
    n = v.shape[1] // 2
    mine = lax.dynamic_slice_in_dim(v, core * n, n, axis=1)
    away = lax.dynamic_slice_in_dim(v, (1 - core) * n, n, axis=1)
    return jnp.concatenate([mine, from_core(away)], axis=0)


def back_rows(unit_rows, radius, emb_grad):
    along = jnp.sum(unit_rows * emb_grad, axis=1, keepdims=True)
    return ((emb_grad - unit_rows * along) / radius).astype(bf16)


def feature_grad(projected_grad, weight):
    return lax.dot_general(
        projected_grad, weight, (((1,), (1,)), ((), ())), preferred_element_type=f32
    ).astype(bf16)


def weight_grad(features, projected_grad):
    return lax.dot_general(
        features, projected_grad, (((0,), (0,)), ((), ())), preferred_element_type=f32
    )


def reduce_weights(image_term, text_term, loss_part, core):
    n = 32
    rows = 16
    width = image_term.shape[1]
    image_blocks = image_term.astype(bf16).reshape(n, rows, width)
    text_blocks = text_term.astype(bf16).reshape(-1, rows, width)
    used = text_blocks.shape[0]
    lane = lax.broadcasted_iota(jnp.int32, (rows, width), 1)

    def split(v):
        high = v.astype(bf16)
        low = (v - high.astype(f32)).astype(bf16)
        return jnp.where(lane == 0, high, jnp.where(lane == 1, low, jnp.zeros((), bf16)))

    extra = jnp.broadcast_to(split(loss_part), (n - used, rows, width))
    sent = jnp.concatenate(
        [image_blocks, jnp.concatenate([text_blocks, extra], axis=0)], axis=1
    )
    got = jnp.sum(lax.all_to_all(sent, PAIR_YZ, 0, 0).astype(f32), axis=0)
    total = got[rows : rows + 1, 0:1] + got[rows : rows + 1, 1:2]
    block = jnp.concatenate(
        [
            got[:rows].astype(bf16),
            jnp.where(lax.axis_index(PAIR_YZ) >= used, split(total), got[rows:].astype(bf16)),
        ],
        axis=0,
    )
    block = plus(block, lax.ppermute(block, "xh", [(0, 1), (1, 0)]))
    total = block[rows : rows + 1, 0:1] + block[rows : rows + 1, 1:2]
    block = jnp.concatenate(
        [
            block[:rows].astype(bf16),
            jnp.where(lax.axis_index(PAIR_YZ) >= used, split(total), block[rows:].astype(bf16)),
        ],
        axis=0,
    )
    full = spread(block, PAIR_YZ, n)
    swapped = from_core(full)
    image, text = whole_terms(core.reshape(1), full, swapped, used)
    loss = plus(full[n - 1, rows, :2], swapped[n - 1, rows, :2])
    return image, text, loss[0] + loss[1]


def body(image_features, text_features, image_projection, text_projection):
    core = lax.axis_index("c")
    place = lax.axis_index(PAIR_Z)
    image_unit, image_radius = normalize_rows(image_features, image_projection)
    image_emb = image_unit.astype(bf16)
    own, width = image_emb.shape
    images = spread(image_emb, PAIR_Z, 8).reshape(8 * own, width)
    text_unit, text_radius = normalize_rows(text_features, text_projection)
    text_emb = text_unit.astype(bf16)
    image_halves = other_half(image_features, core)
    text_halves = other_half(text_features, core)
    images, texts, image_halves, text_halves = lax.optimization_barrier(
        (images, gather_text(text_emb), image_halves, text_halves)
    )
    rows = images.shape[0]
    images = jnp.concatenate([images, from_core(images)], axis=0)
    logits, row_part, column_part = block_logits(images, texts)
    row_flip = jnp.concatenate([row_part[:, rows:], row_part[:, :rows]], axis=1)
    first = core == 0
    row_pair = jnp.stack(
        [jnp.where(first, row_part[0], row_flip[0]), jnp.where(first, row_flip[0], row_part[0])]
    )
    row_parts = lax.all_to_all(
        jnp.broadcast_to(row_pair[None], (8, 2, 2 * rows)).reshape(16, 1, 2 * rows), PAIR_ZC, 0, 0
    ).reshape(16, -1)
    column_total = column_totals(column_part)
    image_parts, text_part = block_grads(
        place.reshape(1), logits, row_parts, column_total, images, texts, image_emb
    )
    other_part = from_core(image_parts[rows:])
    image_part = plus(image_parts[:rows], other_part).astype(bf16)
    image_emb_grad = jnp.sum(
        lax.all_to_all(image_part.reshape(8, own, width), PAIR_Z, 0, 0).astype(f32), axis=0
    )
    text_emb_grad = scatter_text(text_part)
    matched = sharpness_factor * jnp.sum(image_emb.astype(f32) * text_emb.astype(f32), axis=1)
    own_rows = jnp.sum(lax.dynamic_slice_in_dim(row_parts, place * own, own, axis=1), axis=0)
    loss_part = jnp.sum(
        jnp.log(own_rows)
        + jnp.log(column_total[0, :own])
        + 2.0 * (sharpness_factor - matched)
    )
    text_back = back_rows(text_unit, text_radius, text_emb_grad)
    image_back = back_rows(image_unit, image_radius, image_emb_grad)
    text_both = jnp.concatenate([text_back, from_core(text_back)], axis=0)
    image_both = jnp.concatenate([image_back, from_core(image_back)], axis=0)
    text_term = weight_grad(text_halves, text_both)
    image_term = weight_grad(image_halves, image_both)
    image_projection_grad, text_projection_grad, loss = reduce_weights(
        image_term, text_term, loss_part, core
    )
    pairs = own * 128
    return (
        loss / (2.0 * pairs),
        feature_grad(image_back, image_projection),
        feature_grad(text_back, text_projection),
        image_projection_grad,
        text_projection_grad,
    )


def solution(mesh):
    grid = Mesh(mesh.devices.reshape(2, 4, 2, 4, 2), ALL)
    rows = P(ALL, None)
    return jax.shard_map(
        body,
        mesh=grid,
        in_specs=(rows, rows, P(), P()),
        out_specs=(P(), rows, rows, P(), P()),
        check_vma=False,
    )
```

time: 233 us -> 212 us (0.910)
  waiting for transfers between devices: 68.4 us -> 58.8 us
  starting transfers between devices: 64.9 us -> 56 us
  local copies, waits for them, and re-layouts: 16.2 us -> 20.9 us
  Pallas kernels: 23.5 us -> 19.3 us
  other arithmetic: 18.5 us -> 15.2 us
  between operations: 4.8 us -> 7.55 us
    all_to_all x2 -> x1, waiting for transfers between devices: 22.4 us -> 0.01 us  [spread(): return lax.all_to_all(jnp.broadcast_to(v[None], (n,) + v.shape), axes, 0, 0)]
    ppermute x11 -> x15, waiting for transfers between devices: 11.6 us -> 30 us  [the longest x11 22.3 us: from_y(): return lax.ppermute(v, 'y', [(i, (i - k) % 4) for i in range(4)])]
    all_to_all x2 -> x1, starting transfers between devices: 16.2 us -> 5.03 us  [spread(): return lax.all_to_all(jnp.broadcast_to(v[None], (n,) + v.shape), axes, 0, 0)]
    ppermute x9 -> x7, starting transfers between devices: 20.5 us -> 11 us  [from_core(): return lax.ppermute(v, 'c', [(0, 1), (1, 0)])]
    ppermute x11 -> x15, starting transfers between devices: 17.4 us -> 24.1 us  [the longest x11 14.2 us: from_y(): return lax.ppermute(v, 'y', [(i, (i - k) % 4) for i in range(4)])]
    all_to_all x2 -> x3, starting transfers between devices: 10.8 us -> 15.8 us  [the longest x1 6.79 us: body(): lax.all_to_all(jnp.broadcast_to(row_pair[None], (8, 2, 2 * rows)).reshape...]
    pallas_call x3, Pallas kernels: 23.5 us -> 19.3 us  [the longest x1 11.8 us: block_grads(): pl.pallas_call(grads_kernel, grid=(n // TILE,), in_specs=[pl.BlockSpec(me...]
    all_to_all x2 -> x3, waiting for transfers between devices: 29.3 us -> 26.3 us  [the longest x1 20.3 us: reduce_weights(): got = jnp.sum(lax.all_to_all(sent, PAIR_YZ, 0, 0).astype(f32), axis=0)]
  transfers between devices with their start and end apart: 24 -> 26, of which waited for: 15 -> 13; matrix products, arithmetic and copies ran while one was open for 7% -> 13% of each run, Pallas kernels for 3% -> 0%
where the time goes in v3:
time: 212 us; the launch traced here: 211 us
  waiting for transfers between devices  58.8 us (28%)
  starting transfers between devices  56 us (26%)
  blocking collectives  26.9 us (13%)
  local copies, waits for them, and re-layouts  20.9 us (10%)
  Pallas kernels  19.3 us (9%)
  other arithmetic  15.2 us (7%)
  between operations  7.55 us (4%)
  matrix products  6.63 us (3%)
    all_to_all x1, blocking collectives, spread(): return lax.all_to_all(jnp.broadcast_to(v[None], (n,) + v.shape), axes, 0, 0)  26.9 us
    ppermute x11, waiting for transfers between devices, from_y(): return lax.ppermute(v, 'y', [(i, (i - k) % 4) for i in range(4)])  22.3 us
    all_to_all x1, waiting for transfers between devices, reduce_weights(): got = jnp.sum(lax.all_to_all(sent, PAIR_YZ, 0, 0).astype(f32), axis=0)  20.3 us
    ppermute x11, starting transfers between devices, from_y(): return lax.ppermute(v, 'y', [(i, (i - k) % 4) for i in range(4)])  14.2 us
    unnamed x36, local copies, waits for them, and re-layouts  12.2 us
    pallas_call x1, Pallas kernels, block_grads(): pl.pallas_call(grads_kernel, grid=(n // TILE,), in_specs=[pl.BlockSpec(me...  11.8 us
    ppermute x7, starting transfers between devices, from_core(): return lax.ppermute(v, 'c', [(0, 1), (1, 0)])  11 us
    ppermute x3, starting transfers between devices, from_mirror(): return lax.ppermute(v, X, [(i, 3 - i) for i in range(4)])  6.92 us
  transfers between devices with their start and end apart: 26, of which 13 were waited for; matrix products, arithmetic and copies ran while one was open for 13% of the time, Pallas kernels for 0%

profile of v3, /device:TPU:1, one launch (start us, length us, event | category | flops | bytes accessed | tf_op | source)
XLA Modules:
  0.0 211.3 jit_solution(13464385155056575900)
XLA Ops:
  0.7 1.9 multiply_reduce_fusion.3
  2.7 0.6 copy-done.8
  3.3 3.3 %collective-permute-start = (bf16[128,768]{1,0:T(8,128)(2,1)S(1)}, bf16[128,768]{1,0:T(8,128)(2,1)}, u32[]{:S(2)}, u32[]{:S(2)}) collective-permute-start(bf16[128,768]{1,0:T(8,128)(2,1)S(1)} %get-tuple-element.28), channel_id=1, source_target_pairs={{0,72},{8,64},{64,8},{72,0},{1,73},{9,65},{65,9},{73,1},{2,74},{10... | collective-permute-start | bytes 589832 | tf_op jit(solution)/shard_map/ppermute | solution.py:32
  7.1 0.8 copy-done.6
  8.1 1.3 broadcast_in_dim.74
  9.4 5.0 %all-to-all-start = ((bf16[8,128,768]{2,1,0:T(8,128)(2,1)}), bf16[8,128,768]{2,1,0:T(8,128)(2,1)}, u32[]{:S(2)}, u32[]{:S(2)}) async-start(bf16[8,128,768]{2,1,0:T(8,128)(2,1)} %broadcast_in_dim.74), calls=%async_computation | async-start | bytes 3145728 | tf_op jit(solution)/shard_map/all_to_all | solution.py:40
  14.4 1.7 pad_maximum_fusion
  16.1 2.7 %collective-permute-start.1 = (bf16[256,768]{1,0:T(8,128)(2,1)}, bf16[256,768]{1,0:T(8,128)(2,1)}, u32[]{:S(2)}, u32[]{:S(2)}) collective-permute-start(bf16[256,768]{1,0:T(8,128)(2,1)} %pad_maximum_fusion), channel_id=1, source_target_pairs={{0,48},{16,0},{32,16},{48,32},{1,49},{17,1},{33,17},{49,33},{2,50}... | collective-permute-start | bytes 1179656 | tf_op jit(solution)/shard_map/ppermute | solution.py:36
  18.8 1.0 constant_dynamic-slice_fusion.1
  19.8 1.6 collective-permute-start.6
  21.4 1.0 constant_dynamic-slice_fusion.3
  22.6 1.6 pad_maximum_fusion.4
  24.2 0.7 pad_maximum_fusion.3
  24.9 1.4 collective-permute-done.1
  26.3 0.9 slice.158
  27.3 3.5 %collective-permute-start.2 = (bf16[128,768]{1,0:T(8,128)(2,1)S(1)}, bf16[128,768]{1,0:T(8,128)(2,1)S(1)}, u32[]{:S(2)}, u32[]{:S(2)}) collective-permute-start(bf16[128,768]{1,0:T(8,128)(2,1)S(1)} %slice.158), channel_id=1, source_target_pairs={{0,48},{16,0},{32,16},{48,32},{1,49},{17,1},{33,17},{49,33},{2,50}... | collective-permute-start | bytes 589832 | tf_op jit(solution)/shard_map/ppermute | solution.py:36
  30.8 0.9 constant_dynamic-update-slice_fusion.4
  31.7 1.9 collective-permute-done.3
  33.7 1.0 constant_dynamic-update-slice_fusion.3
  34.8 5.8 %collective-permute-done.4 = bf16[128,768]{1,0:T(8,128)(2,1)S(1)} collective-permute-done((bf16[128,768]{1,0:T(8,128)(2,1)S(1)}, bf16[128,768]{1,0:T(8,128)(2,1)S(1)}, u32[]{:S(2)}, u32[]{:S(2)}) %collective-permute-start.4) | collective-permute-done | bytes 196640 | tf_op jit(solution)/shard_map/ppermute | solution.py:36
  40.7 1.7 collective-permute-start.7
  42.4 1.5 constant_dynamic-update-slice_fusion.7
  43.9 1.9 collective-permute-done.7
  45.8 1.5 constant_dynamic-update-slice_fusion.6.images
  47.3 4.9 %block_logits.1 = (f32[2048,1024]{1,0:T(8,128)S(1)}, f32[1,2048]{1,0:T(1,128)S(1)}, f32[1,1024]{1,0:T(1,128)S(1)}) custom-call(bf16[2048,768]{1,0:T(8,128)(2,1)S(1)} %constant_dynamic-update-slice_fusion.6.images, bf16[1024,768]{1,0:T(8,128)(2,1)S(1)} %constant_dynamic-update-slice_fusion.texts), custom_call_target="tpu_custom_call" | custom-call | flops 3221225472 | bytes 13107200 | tf_op jit(solution)/shard_map/block_logits/pallas_call | solution.py:105
  52.2 3.3 %copy-done.5 = f32[2048,1024]{1,0:T(8,128)} copy-done((f32[2048,1024]{1,0:T(8,128)}, f32[2048,1024]{1,0:T(8,128)S(1)}, u32[]{:S(2)}) %copy-start.5) | copy-done | bytes 8388632
  55.4 1.7 collective-permute-start.8
  57.1 2.0 collective-permute-done.8
  59.3 2.7 %collective-permute-start.9 = (f32[4,2,128]{2,1,0:T(2,128)S(1)}, f32[4,2,128]{2,1,0:T(2,128)S(1)}, u32[]{:S(2)}, u32[]{:S(2)}) collective-permute-start(f32[4,2,128]{2,1,0:T(2,128)S(1)} %add.103), channel_id=1, source_target_pairs={{0,48},{16,0},{32,16},{48,32},{1,49},{17,1},{33,17},{49,33},{2,50}... | collective-permute-start | bytes 12296 | tf_op jit(solution)/shard_map/ppermute | solution.py:36
  62.1 0.9 reshape.73
  62.9 6.8 %all-to-all-start.1 = ((f32[16,1,2048]{2,1,0:T(1,128)}), f32[16,1,2048]{2,1,0:T(1,128)S(1)}, u32[]{:S(2)}, u32[]{:S(2)}) async-start(f32[16,1,2048]{2,1,0:T(1,128)} %reshape.73), calls=%async_computation.1 | async-start | bytes 262144 | tf_op jit(solution)/shard_map/all_to_all | solution.py:330
  69.8 6.0 %all-to-all-done.1 = f32[16,1,2048]{2,1,0:T(1,128)S(1)} async-done(((f32[16,1,2048]{2,1,0:T(1,128)}), f32[16,1,2048]{2,1,0:T(1,128)S(1)}, u32[]{:S(2)}, u32[]{:S(2)}) %all-to-all-start.1) | async-done | bytes 131104 | tf_op jit(solution)/shard_map/all_to_all | solution.py:330
  75.9 0.6 copy-done.13
  76.5 1.9 copy-done.2
  78.4 1.4 copy-done.4
  79.8 11.8 %block_grads.1 = (bf16[2048,768]{1,0:T(8,128)(2,1)S(1)}, bf16[1024,768]{1,0:T(8,128)(2,1)S(1)}) custom-call(s32[1]{0:T(128)} %bitcast.1.place, f32[2048,1024]{1,0:T(8,128)} %copy-done.5, f32[16,2048]{1,0:T(8,128)S(1)} %bitcast.34, f32[1,1024]{1,0:T(1,128)S(1)} %bitcast.35, bf16[2048,768]{1,0:T(8,128)(2,1)S(1)} %copy-done.2, bf16[1024,768]{1,0:T(8,128)(2,1)S(1)} %copy-done.4, ...), custom_call_target="tpu_custom_call" | custom-call | flops 6442450944 | bytes 17825792 | tf_op jit(solution)/shard_map/block_grads/pallas_call | solution.py:169
  91.7 0.7 collective-permute-start.12
  92.6 2.7 %collective-permute-start.16 = (bf16[128,768]{1,0:T(8,128)(2,1)S(1)}, bf16[128,768]{1,0:T(8,128)(2,1)S(1)}, u32[]{:S(2)}, u32[]{:S(2)}) collective-permute-start(bf16[128,768]{1,0:T(8,128)(2,1)S(1)} %get-tuple-element.34), channel_id=1, source_target_pairs={{0,48},{16,0},{32,16},{48,32},{1,49},{17,1},{33,17},{49,33},{2,50}... | collective-permute-start | bytes 589832 | tf_op jit(solution)/shard_map/ppermute | solution.py:36
  95.2 5.0 %collective-permute-done.14 = bf16[128,768]{1,0:T(8,128)(2,1)S(1)} collective-permute-done((bf16[128,768]{1,0:T(8,128)(2,1)S(1)}, bf16[128,768]{1,0:T(8,128)(2,1)S(1)}, u32[]{:S(2)}, u32[]{:S(2)}) %collective-permute-start.14) | collective-permute-done | bytes 196640 | tf_op jit(solution)/shard_map/ppermute | solution.py:36
  100.4 0.8 pad_maximum_fusion.2
  101.2 2.4 %collective-permute-start.17 = (bf16[256,768]{1,0:T(8,128)(2,1)}, bf16[256,768]{1,0:T(8,128)(2,1)}, u32[]{:S(2)}, u32[]{:S(2)}) collective-permute-start(bf16[256,768]{1,0:T(8,128)(2,1)} %pad_maximum_fusion.2), channel_id=1, source_target_pairs={{0,48},{16,0},{32,16},{48,32},{1,49},{17,1},{33,17},{49,33},{2,50}... | collective-permute-start | bytes 1179656 | tf_op jit(solution)/shard_map/ppermute | solution.py:36
  103.5 1.5 add_convert_fusion
  105.1 4.5 %all-to-all-start.2 = ((bf16[8,128,768]{2,1,0:T(8,128)(2,1)}), bf16[8,128,768]{2,1,0:T(8,128)(2,1)}, u32[]{:S(2)}, u32[]{:S(2)}) async-start(bf16[8,128,768]{2,1,0:T(8,128)(2,1)} %bitcast.39), calls=%async_computation.2 | async-start | bytes 3145728 | tf_op jit(solution)/shard_map/all_to_all | solution.py:340
  109.5 0.8 pad_maximum_fusion.1
  110.3 0.7 dynamic-slice_reduce_fusion
  111.1 0.6 fusion.15
  113.0 8.0 %collective-permute-done.15 = bf16[256,768]{1,0:T(8,128)(2,1)} collective-permute-done((bf16[256,768]{1,0:T(8,128)(2,1)}, bf16[256,768]{1,0:T(8,128)(2,1)}, u32[]{:S(2)}, u32[]{:S(2)}) %collective-permute-start.15) | collective-permute-done | bytes 393248 | tf_op jit(solution)/shard_map/ppermute | solution.py:36
  121.1 1.3 convert_add_fusion
  122.4 2.0 collective-permute-start.18
  124.4 4.2 %collective-permute-done.18 = bf16[128,768]{1,0:T(8,128)(2,1)S(1)} collective-permute-done((bf16[128,768]{1,0:T(8,128)(2,1)S(1)}, bf16[128,768]{1,0:T(8,128)(2,1)S(1)}, u32[]{:S(2)}, u32[]{:S(2)}) %collective-permute-start.18) | collective-permute-done | bytes 196640 | tf_op jit(solution)/shard_map/ppermute | solution.py:32
  128.6 1.2 multiply_reduce_fusion.1
  130.0 3.1 %collective-permute-start.19 = (bf16[128,768]{1,0:T(8,128)(2,1)S(1)}, bf16[128,768]{1,0:T(8,128)(2,1)}, u32[]{:S(2)}, u32[]{:S(2)}) collective-permute-start(bf16[128,768]{1,0:T(8,128)(2,1)S(1)} %divide_convert_fusion), channel_id=1, source_target_pairs={{0,1},{1,0},{2,3},{3,2},{4,5},{5,4},{6,7},{7,6},{8,9},{9,8},{10,11... | collective-permute-start | bytes 589832 | tf_op jit(solution)/shard_map/ppermute | solution.py:28
  133.1 1.7 convert_reduce_fusion.1
  135.3 1.3 convolution_convert_fusion.1
  137.1 1.3 maximum_maximum_fusion
  138.5 4.5 %all-to-all-start.3 = ((bf16[32,32,768]{2,1,0:T(8,128)(2,1)}), bf16[32,32,768]{2,1,0:T(8,128)(2,1)S(1)}, u32[]{:S(2)}, u32[]{:S(2)}) async-start(bf16[32,32,768]{2,1,0:T(8,128)(2,1)} %maximum_maximum_fusion), calls=%async_computation.3 | async-start | bytes 3145728 | tf_op jit(solution)/shard_map/all_to_all | solution.py:283
  143.0 20.3 %all-to-all-done.3 = bf16[32,32,768]{2,1,0:T(8,128)(2,1)S(1)} async-done(((bf16[32,32,768]{2,1,0:T(8,128)(2,1)}), bf16[32,32,768]{2,1,0:T(8,128)(2,1)S(1)}, u32[]{:S(2)}, u32[]{:S(2)}) %all-to-all-start.3) | async-done | bytes 1572896 | tf_op jit(solution)/shard_map/all_to_all | solution.py:283
  165.5 3.0 %collective-permute-start.20 = (bf16[32,768]{1,0:T(8,128)(2,1)S(1)}, bf16[32,768]{1,0:T(8,128)(2,1)S(1)}, u32[]{:S(2)}, u32[]{:S(2)}) collective-permute-start(bf16[32,768]{1,0:T(8,128)(2,1)S(1)} %pad_maximum_fusion.5), channel_id=1, source_target_pairs={{0,64},{64,0},{1,65},{65,1},{2,66},{66,2},{3,67},{67,3},{4,68},{68... | collective-permute-start | bytes 147464 | tf_op jit(solution)/shard_map/ppermute | solution.py:292
  168.5 1.5 collective-permute-done.20
  172.1 26.9 %all_to_all.25.mine = bf16[32,32,768]{2,1,0:T(8,128)(2,1)S(1)} all-to-all(bf16[32,32,768]{2,1,0:T(8,128)(2,1)S(1)} %broadcast_in_dim.88), channel_id=1, replica_groups=mesh['xh'=2,'y'=4,'xl'=2,'z'=4,'c'=2] {'xl','y','z'}, dimensions={0} | all-to-all | bytes 3145728 | tf_op jit(solution)/shard_map/all_to_all | solution.py:40
  199.0 3.5 %collective-permute-start.21 = (bf16[32,32,768]{2,1,0:T(8,128)(2,1)S(1)}, bf16[32,32,768]{2,1,0:T(8,128)(2,1)S(1)}, u32[]{:S(2)}, u32[]{:S(2)}) collective-permute-start(bf16[32,32,768]{2,1,0:T(8,128)(2,1)S(1)} %all_to_all.25.mine), channel_id=1, source_target_pairs={{0,1},{1,0},{2,3},{3,2},{4,5},{5,4},{6,7},{7,6},{8,9},{9,8},{10,11... | collective-permute-start | bytes 4718600 | tf_op jit(solution)/shard_map/ppermute | solution.py:28
  202.6 1.2 convolution_convert_fusion.3
  203.8 1.3 convolution_convert_fusion.2
  207.5 2.7 %whole_terms.1 = (f32[1024,768]{1,0:T(8,128)}, f32[768,768]{1,0:T(8,128)}) custom-call(s32[1]{0:T(128)} %bitcast.13.core, bf16[32,32,768]{2,1,0:T(8,128)(2,1)S(1)} %all_to_all.25.mine, bf16[32,32,768]{2,1,0:T(8,128)(2,1)S(1)} %collective-permute-done.21.other), custom_call_target="tpu_custom_call" | custom-call | bytes 6291456 | tf_op jit(solution)/shard_map/whole_terms/pallas_call | solution.py:223
  (95 shorter events, 5.7 us)
Async XLA Ops:
  0.6 6.0 %copy-start = (bf16[1024,768]{1,0:T(8,128)(2,1)S(1)}, bf16[1024,768]{1,0:T(8,128)(2,1)}, u32[]{:S(2)}) copy-start(bf16[1024,768]{1,0:T(8,128)(2,1)} %param.6) | copy-start | bytes 4718596
  0.6 6.0 %copy-start.11 = (bf16[128,1024]{1,0:T(8,128)(2,1)S(1)}, bf16[128,1024]{1,0:T(8,128)(2,1)}, u32[]{:S(2)}) copy-start(bf16[128,1024]{1,0:T(8,128)(2,1)} %param.4) | copy-start | bytes 786436
  2.6 0.8 copy-start.8
  3.3 11.1 %collective-permute-start = (bf16[128,768]{1,0:T(8,128)(2,1)S(1)}, bf16[128,768]{1,0:T(8,128)(2,1)}, u32[]{:S(2)}, u32[]{:S(2)}) collective-permute-start(bf16[128,768]{1,0:T(8,128)(2,1)S(1)} %get-tuple-element.28), channel_id=1, source_target_pairs={{0,72},{8,64},{64,8},{72,0},{1,73},{9,65},{65,9},{73,1},{2,74},{10... | collective-permute-start | bytes 589832 | tf_op jit(solution)/shard_map/ppermute | solution.py:32
  7.1 0.8 copy-start.6
  9.4 31.3 %all-to-all-start = ((bf16[8,128,768]{2,1,0:T(8,128)(2,1)}), bf16[8,128,768]{2,1,0:T(8,128)(2,1)}, u32[]{:S(2)}, u32[]{:S(2)}) async-start(bf16[8,128,768]{2,1,0:T(8,128)(2,1)} %broadcast_in_dim.74), calls=%async_computation | async-start | bytes 3145728 | tf_op jit(solution)/shard_map/all_to_all | solution.py:40
  16.1 10.2 %collective-permute-start.1 = (bf16[256,768]{1,0:T(8,128)(2,1)}, bf16[256,768]{1,0:T(8,128)(2,1)}, u32[]{:S(2)}, u32[]{:S(2)}) collective-permute-start(bf16[256,768]{1,0:T(8,128)(2,1)} %pad_maximum_fusion), channel_id=1, source_target_pairs={{0,48},{16,0},{32,16},{48,32},{1,49},{17,1},{33,17},{49,33},{2,50}... | collective-permute-start | bytes 1179656 | tf_op jit(solution)/shard_map/ppermute | solution.py:36
  19.8 2.8 %collective-permute-start.6 = (bf16[128,384]{1,0:T(8,128)(2,1)S(1)}, bf16[128,384]{1,0:T(8,128)(2,1)}, u32[]{:S(2)}, u32[]{:S(2)}) collective-permute-start(bf16[128,384]{1,0:T(8,128)(2,1)S(1)} %get-tuple-element.40), channel_id=1, source_target_pairs={{0,1},{1,0},{2,3},{3,2},{4,5},{5,4},{6,7},{7,6},{8,9},{9,8},{10,11... | collective-permute-start | bytes 294920 | tf_op jit(solution)/shard_map/ppermute | solution.py:28
  21.4 12.2 %collective-permute-start.3 = (bf16[256,768]{1,0:T(8,128)(2,1)}, bf16[256,768]{1,0:T(8,128)(2,1)S(1)}, u32[]{:S(2)}, u32[]{:S(2)}) collective-permute-start(bf16[256,768]{1,0:T(8,128)(2,1)} %pad_maximum_fusion), channel_id=1, source_target_pairs={{0,16},{16,32},{32,48},{48,0},{1,17},{17,33},{33,49},{49,1},{2,18}... | collective-permute-start | bytes 1179656 | tf_op jit(solution)/shard_map/ppermute | solution.py:36
  22.4 1.8 collective-permute-start.5
  27.3 7.5 %collective-permute-start.2 = (bf16[128,768]{1,0:T(8,128)(2,1)S(1)}, bf16[128,768]{1,0:T(8,128)(2,1)S(1)}, u32[]{:S(2)}, u32[]{:S(2)}) collective-permute-start(bf16[128,768]{1,0:T(8,128)(2,1)S(1)} %slice.158), channel_id=1, source_target_pairs={{0,48},{16,0},{32,16},{48,32},{1,49},{17,1},{33,17},{49,33},{2,50}... | collective-permute-start | bytes 589832 | tf_op jit(solution)/shard_map/ppermute | solution.py:36
  33.6 7.0 %collective-permute-start.4 = (bf16[128,768]{1,0:T(8,128)(2,1)S(1)}, bf16[128,768]{1,0:T(8,128)(2,1)S(1)}, u32[]{:S(2)}, u32[]{:S(2)}) collective-permute-start(bf16[128,768]{1,0:T(8,128)(2,1)S(1)} %slice.159), channel_id=1, source_target_pairs={{0,16},{16,32},{32,48},{48,0},{1,17},{17,33},{33,49},{49,1},{2,18}... | collective-permute-start | bytes 589832 | tf_op jit(solution)/shard_map/ppermute | solution.py:36
  40.6 6.6 %copy-start.3 = (bf16[1024,768]{1,0:T(8,128)(2,1)}, bf16[1024,768]{1,0:T(8,128)(2,1)S(1)}, u32[]{:S(2)}) copy-start(bf16[1024,768]{1,0:T(8,128)(2,1)S(1)} %constant_dynamic-update-slice_fusion.texts) | copy-start | bytes 4718596
  40.7 5.1 %collective-permute-start.7 = (bf16[1024,768]{1,0:T(8,128)(2,1)}, bf16[1024,768]{1,0:T(8,128)(2,1)}, u32[]{:S(2)}, u32[]{:S(2)}) collective-permute-start(bf16[1024,768]{1,0:T(8,128)(2,1)} %bitcast), channel_id=1, source_target_pairs={{0,1},{1,0},{2,3},{3,2},{4,5},{5,4},{6,7},{7,6},{8,9},{9,8},{10,11... | collective-permute-start | bytes 4718600 | tf_op jit(solution)/shard_map/ppermute | solution.py:28
  47.3 4.9 %copy-start.1 = (bf16[2048,768]{1,0:T(8,128)(2,1)}, bf16[2048,768]{1,0:T(8,128)(2,1)S(1)}, u32[]{:S(2)}) copy-start(bf16[2048,768]{1,0:T(8,128)(2,1)S(1)} %constant_dynamic-update-slice_fusion.6.images) | copy-start | bytes 9437188
  52.2 3.3 %copy-start.5 = (f32[2048,1024]{1,0:T(8,128)}, f32[2048,1024]{1,0:T(8,128)S(1)}, u32[]{:S(2)}) copy-start(f32[2048,1024]{1,0:T(8,128)S(1)} %get-tuple-element.19.logits) | copy-start | bytes 25165828
  55.4 3.7 %collective-permute-start.8 = (f32[4,2,128]{2,1,0:T(2,128)S(1)}, f32[4,2,128]{2,1,0:T(2,128)S(1)}, u32[]{:S(2)}, u32[]{:S(2)}) collective-permute-start(f32[4,2,128]{2,1,0:T(2,128)S(1)} %bitcast.37), channel_id=1, source_target_pairs={{0,72},{8,64},{64,8},{72,0},{1,73},{9,65},{65,9},{73,1},{2,74},{10... | collective-permute-start | bytes 12296 | tf_op jit(solution)/shard_map/ppermute | solution.py:32
  59.1 10.6 %collective-permute-start.11 = (f32[4,2,128]{2,1,0:T(2,128)S(1)}, f32[4,2,128]{2,1,0:T(2,128)S(1)}, u32[]{:S(2)}, u32[]{:S(2)}) collective-permute-start(f32[4,2,128]{2,1,0:T(2,128)S(1)} %add.103), channel_id=1, source_target_pairs={{0,32},{16,48},{32,0},{48,16},{1,33},{17,49},{33,1},{49,17},{2,34}... | collective-permute-start | bytes 12296 | tf_op jit(solution)/shard_map/ppermute | solution.py:36
  59.2 10.5 %collective-permute-start.10 = (f32[4,2,128]{2,1,0:T(2,128)S(1)}, f32[4,2,128]{2,1,0:T(2,128)S(1)}, u32[]{:S(2)}, u32[]{:S(2)}) collective-permute-start(f32[4,2,128]{2,1,0:T(2,128)S(1)} %add.103), channel_id=1, source_target_pairs={{0,16},{16,32},{32,48},{48,0},{1,17},{17,33},{33,49},{49,1},{2,18}... | collective-permute-start | bytes 12296 | tf_op jit(solution)/shard_map/ppermute | solution.py:36
  59.3 10.4 %collective-permute-start.9 = (f32[4,2,128]{2,1,0:T(2,128)S(1)}, f32[4,2,128]{2,1,0:T(2,128)S(1)}, u32[]{:S(2)}, u32[]{:S(2)}) collective-permute-start(f32[4,2,128]{2,1,0:T(2,128)S(1)} %add.103), channel_id=1, source_target_pairs={{0,48},{16,0},{32,16},{48,32},{1,49},{17,1},{33,17},{49,33},{2,50}... | collective-permute-start | bytes 12296 | tf_op jit(solution)/shard_map/ppermute | solution.py:36
  62.9 12.9 %all-to-all-start.1 = ((f32[16,1,2048]{2,1,0:T(1,128)}), f32[16,1,2048]{2,1,0:T(1,128)S(1)}, u32[]{:S(2)}, u32[]{:S(2)}) async-start(f32[16,1,2048]{2,1,0:T(1,128)} %reshape.73), calls=%async_computation.1 | async-start | bytes 262144 | tf_op jit(solution)/shard_map/all_to_all | solution.py:330
  75.8 0.6 copy-start.13
  76.5 1.9 copy-start.2
  78.4 1.4 copy-start.4
  91.7 11.8 %collective-permute-start.12 = (bf16[1024,768]{1,0:T(8,128)(2,1)S(1)}, bf16[1024,768]{1,0:T(8,128)(2,1)S(1)}, u32[]{:S(2)}, u32[]{:S(2)}) collective-permute-start(bf16[1024,768]{1,0:T(8,128)(2,1)S(1)} %slice.135), channel_id=1, source_target_pairs={{0,1},{1,0},{2,3},{3,2},{4,5},{5,4},{6,7},{7,6},{8,9},{9,8},{10,11... | collective-permute-start | bytes 4718600 | tf_op jit(solution)/shard_map/ppermute | solution.py:28
  92.5 7.8 %collective-permute-start.14 = (bf16[128,768]{1,0:T(8,128)(2,1)S(1)}, bf16[128,768]{1,0:T(8,128)(2,1)S(1)}, u32[]{:S(2)}, u32[]{:S(2)}) collective-permute-start(bf16[128,768]{1,0:T(8,128)(2,1)S(1)} %get-tuple-element.33), channel_id=1, source_target_pairs={{0,16},{16,32},{32,48},{48,0},{1,17},{17,33},{33,49},{49,1},{2,18}... | collective-permute-start | bytes 589832 | tf_op jit(solution)/shard_map/ppermute | solution.py:36
  92.6 7.7 %collective-permute-start.16 = (bf16[128,768]{1,0:T(8,128)(2,1)S(1)}, bf16[128,768]{1,0:T(8,128)(2,1)S(1)}, u32[]{:S(2)}, u32[]{:S(2)}) collective-permute-start(bf16[128,768]{1,0:T(8,128)(2,1)S(1)} %get-tuple-element.34), channel_id=1, source_target_pairs={{0,48},{16,0},{32,16},{48,32},{1,49},{17,1},{33,17},{49,33},{2,50}... | collective-permute-start | bytes 589832 | tf_op jit(solution)/shard_map/ppermute | solution.py:36
  101.2 11.8 %collective-permute-start.17 = (bf16[256,768]{1,0:T(8,128)(2,1)}, bf16[256,768]{1,0:T(8,128)(2,1)}, u32[]{:S(2)}, u32[]{:S(2)}) collective-permute-start(bf16[256,768]{1,0:T(8,128)(2,1)} %pad_maximum_fusion.2), channel_id=1, source_target_pairs={{0,48},{16,0},{32,16},{48,32},{1,49},{17,1},{33,17},{49,33},{2,50}... | collective-permute-start | bytes 1179656 | tf_op jit(solution)/shard_map/ppermute | solution.py:36
  105.1 28.0 %all-to-all-start.2 = ((bf16[8,128,768]{2,1,0:T(8,128)(2,1)}), bf16[8,128,768]{2,1,0:T(8,128)(2,1)}, u32[]{:S(2)}, u32[]{:S(2)}) async-start(bf16[8,128,768]{2,1,0:T(8,128)(2,1)} %bitcast.39), calls=%async_computation.2 | async-start | bytes 3145728 | tf_op jit(solution)/shard_map/all_to_all | solution.py:340
  110.3 10.7 %collective-permute-start.15 = (bf16[256,768]{1,0:T(8,128)(2,1)}, bf16[256,768]{1,0:T(8,128)(2,1)}, u32[]{:S(2)}, u32[]{:S(2)}) collective-permute-start(bf16[256,768]{1,0:T(8,128)(2,1)} %pad_maximum_fusion.1), channel_id=1, source_target_pairs={{0,16},{16,32},{32,48},{48,0},{1,17},{17,33},{33,49},{49,1},{2,18}... | collective-permute-start | bytes 1179656 | tf_op jit(solution)/shard_map/ppermute | solution.py:36
  113.0 16.8 %copy-start.9 = (f32[128,768]{1,0:T(8,128)S(1)}, f32[128,768]{1,0:T(8,128)}, u32[]{:S(2)}) copy-start(f32[128,768]{1,0:T(8,128)} %copy-done.8) | copy-start | bytes 1179652
  122.4 6.2 %collective-permute-start.18 = (bf16[128,768]{1,0:T(8,128)(2,1)S(1)}, bf16[128,768]{1,0:T(8,128)(2,1)S(1)}, u32[]{:S(2)}, u32[]{:S(2)}) collective-permute-start(bf16[128,768]{1,0:T(8,128)(2,1)S(1)} %slice.206), channel_id=1, source_target_pairs={{0,72},{8,64},{64,8},{72,0},{1,73},{9,65},{65,9},{73,1},{2,74},{10... | collective-permute-start | bytes 589832 | tf_op jit(solution)/shard_map/ppermute | solution.py:32
  129.8 5.0 %copy-start.7 = (f32[128,768]{1,0:T(8,128)S(1)}, f32[128,768]{1,0:T(8,128)}, u32[]{:S(2)}) copy-start(f32[128,768]{1,0:T(8,128)} %copy-done.6) | copy-start | bytes 1179652
  130.0 5.3 %copy-start.14 = (bf16[256,384]{1,0:T(8,128)(2,1)S(1)}, bf16[256,384]{1,0:T(8,128)(2,1)}, u32[]{:S(2)}) copy-start(bf16[256,384]{1,0:T(8,128)(2,1)} %pad_maximum_fusion.4) | copy-start | bytes 589828
  130.0 5.3 %collective-permute-start.19 = (bf16[128,768]{1,0:T(8,128)(2,1)S(1)}, bf16[128,768]{1,0:T(8,128)(2,1)}, u32[]{:S(2)}, u32[]{:S(2)}) collective-permute-start(bf16[128,768]{1,0:T(8,128)(2,1)S(1)} %divide_convert_fusion), channel_id=1, source_target_pairs={{0,1},{1,0},{2,3},{3,2},{4,5},{5,4},{6,7},{7,6},{8,9},{9,8},{10,11... | collective-permute-start | bytes 589832 | tf_op jit(solution)/shard_map/ppermute | solution.py:28
  134.8 1.9 copy-start.12
  135.2 1.5 collective-permute-start.13
  138.5 24.8 %all-to-all-start.3 = ((bf16[32,32,768]{2,1,0:T(8,128)(2,1)}), bf16[32,32,768]{2,1,0:T(8,128)(2,1)S(1)}, u32[]{:S(2)}, u32[]{:S(2)}) async-start(bf16[32,32,768]{2,1,0:T(8,128)(2,1)} %maximum_maximum_fusion), calls=%async_computation.3 | async-start | bytes 3145728 | tf_op jit(solution)/shard_map/all_to_all | solution.py:283
  165.5 4.5 %collective-permute-start.20 = (bf16[32,768]{1,0:T(8,128)(2,1)S(1)}, bf16[32,768]{1,0:T(8,128)(2,1)S(1)}, u32[]{:S(2)}, u32[]{:S(2)}) collective-permute-start(bf16[32,768]{1,0:T(8,128)(2,1)S(1)} %pad_maximum_fusion.5), channel_id=1, source_target_pairs={{0,64},{64,0},{1,65},{65,1},{2,66},{66,2},{3,67},{67,3},{4,68},{68... | collective-permute-start | bytes 147464 | tf_op jit(solution)/shard_map/ppermute | solution.py:292
  172.1 30.4 %copy-start.10 = (bf16[768,768]{1,0:T(8,128)(2,1)S(1)}, bf16[768,768]{1,0:T(8,128)(2,1)}, u32[]{:S(2)}) copy-start(bf16[768,768]{1,0:T(8,128)(2,1)} %param.7) | copy-start | bytes 3538948
  199.0 6.6 %collective-permute-start.21 = (bf16[32,32,768]{2,1,0:T(8,128)(2,1)S(1)}, bf16[32,32,768]{2,1,0:T(8,128)(2,1)S(1)}, u32[]{:S(2)}, u32[]{:S(2)}) collective-permute-start(bf16[32,32,768]{2,1,0:T(8,128)(2,1)S(1)} %all_to_all.25.mine), channel_id=1, source_target_pairs={{0,1},{1,0},{2,3},{3,2},{4,5},{5,4},{6,7},{7,6},{8,9},{9,8},{10,11... | collective-permute-start | bytes 4718600 | tf_op jit(solution)/shard_map/ppermute | solution.py:28

commit v4 on v3

v4 whole, which is shorter than its diff:
```python
import jax
import jax.numpy as jnp
from jax import lax
from jax.experimental import pallas as pl
from jax.experimental.pallas import tpu as pltpu
from jax.sharding import Mesh, PartitionSpec as P

sharpness_factor = 100.0
norm_eps = 1e-06
X = ("xh", "xl")
PAIR_Z = ("xl", "z")
YZ = ("y", "z")
ALL = ("xh", "y", "xl", "z", "c")
TILE = 512
LTILE = 512
GRADS_MIB = 40
f32 = jnp.float32
bf16 = jnp.bfloat16


def normalize_rows(features, weight):
    projected = jnp.dot(features, weight, preferred_element_type=f32)
    radius = jnp.sqrt(jnp.sum(projected * projected, axis=1, keepdims=True) + norm_eps)
    return (projected / radius, radius)


def from_core(v):
    return lax.ppermute(v, "c", [(0, 1), (1, 0)])


def from_mirror(v):
    return lax.ppermute(v, X, [(i, 3 - i) for i in range(4)])


def from_x(v, k):
    return lax.ppermute(v, X, [(i, (i - k) % 4) for i in range(4)])


def from_y(v, k):
    return lax.ppermute(v, "y", [(i, (i - k) % 4) for i in range(4)])


def hbm(v):
    return pltpu.with_memory_space_constraint(v, pltpu.HBM)


def spread(v, axes, n):
    return lax.all_to_all(jnp.broadcast_to(v[None], (n,) + v.shape), axes, 0, 0)


def gather_text(pair):
    n = pair.shape[0] // 2
    up = from_y(pair, 1)
    down = from_y(pair, 3)
    far = [from_y(up[:n], 1), from_y(down[n:], 3)]
    return jnp.concatenate([pair, up] + far + [down], axis=0)


def column_totals(part):
    part = part.reshape(4, 2, -1)
    part = part + from_mirror(part)[:, ::-1]
    total = part
    for k in (1, 3, 2):
        total = total + jnp.roll(from_y(part, k), k, axis=0)
    return total.reshape(1, -1)


def row_totals(part):
    n = part.shape[1] // 2
    other = from_core(part)
    part = part + jnp.concatenate([other[:, n:], other[:, :n]], axis=1)
    part = part + lax.ppermute(part, "xl", [(0, 1), (1, 0)])
    return part + sum(lax.ppermute(part, "z", [(i, (i - k) % 4) for i in range(4)]) for k in (1, 3, 2))


def plus(*parts):
    return sum(p.astype(f32) for p in parts)


def scatter_text(g):
    b = g.shape[0] // 4
    h = b // 2
    g0, g1, g2, g3 = (g[k * b : (k + 1) * b] for k in range(4))
    low = from_y(g2[:h], 3)
    high = from_y(g2[h:], 1)
    g1 = jnp.concatenate([plus(g1[:h], low).astype(bf16), g1[h:]], axis=0)
    g3 = jnp.concatenate([g3[:h], plus(g3[h:], high).astype(bf16)], axis=0)
    g1, g3 = lax.optimization_barrier((g1, g3))
    g0 = plus(g0, from_y(g1, 3), from_y(g3, 1))
    return g0[:h] + from_mirror(g0[h:].astype(bf16)).astype(f32)


def params(mib=40):
    return pltpu.CompilerParams(vmem_limit_bytes=mib * 1024 * 1024)


def logits_kernel(mine, other, texts, logits, row_sum, column_sum):
    i = pl.program_id(0)
    images = jnp.where(i < pl.num_programs(0) // 2, mine[...], other[...])
    value = sharpness_factor * lax.dot_general(
        images, texts[...], (((1,), (1,)), ((), ())), preferred_element_type=f32
    )
    logits[...] = value
    e = jnp.exp(value - sharpness_factor)
    by_lane = e[:, :128]
    for k in range(1, e.shape[1] // 128):
        by_lane = by_lane + e[:, k * 128 : (k + 1) * 128]
    row_sum[...] = jnp.sum(by_lane.T, axis=0, keepdims=True)
    by_column = jnp.sum(e, axis=0, keepdims=True)

    @pl.when(i == 0)
    def _():
        column_sum[...] = by_column

    @pl.when(i > 0)
    def _():
        column_sum[...] += by_column


def block_logits(mine, other, texts):
    n, width = mine.shape
    half = n // LTILE
    n = 2 * n
    m = texts.shape[0]
    return pl.pallas_call(
        logits_kernel,
        grid=(n // LTILE,),
        in_specs=[
            pl.BlockSpec((LTILE, width), lambda i: (jnp.minimum(i, half - 1), 0)),
            pl.BlockSpec((LTILE, width), lambda i: (jnp.maximum(i - half, 0), 0)),
            pl.BlockSpec((m, width), lambda i: (0, 0)),
        ],
        out_specs=[
            pl.BlockSpec((LTILE, m), lambda i: (i, 0)),
            pl.BlockSpec((1, LTILE), lambda i: (0, i)),
            pl.BlockSpec((1, m), lambda i: (0, 0)),
        ],
        out_shape=[
            pltpu.HBM((n, m), f32),
            jax.ShapeDtypeStruct((1, n), f32),
            jax.ShapeDtypeStruct((1, m), f32),
        ],
        compiler_params=params(),
        cost_estimate=pl.CostEstimate(
            flops=2 * n * m * width, bytes_accessed=4 * n * m + 2 * (n + m) * width, transcendentals=n * m
        ),
        name="block_logits",
    )(mine, other, texts)


def grads_kernel(
    place, logits, row_total, column_total, mine, other, texts, own, part_mine, part_other, text_part, total
):
    i = pl.program_id(0)
    half = pl.num_programs(0) // 2
    images = jnp.where(i < half, mine[...], other[...])
    row_lse = jnp.log(row_total[...]) + sharpness_factor
    column_lse = jnp.log(column_total[...]) + sharpness_factor
    value = logits[...]
    rows, columns = value.shape
    by_row = jnp.broadcast_to(row_lse, (128, rows)).T
    by_row = jnp.concatenate([by_row] * (columns // 128), axis=1)
    weights = (
        0.5 * sharpness_factor * (jnp.exp(value - by_row) + jnp.exp(value - column_lse))
    ).astype(bf16)
    part = jnp.dot(weights, texts[...], preferred_element_type=f32)
    per = rows // 128

    @pl.when(i < half)
    def _():
        for k in range(per):
            here = jnp.where(place[0] == i * per + k, sharpness_factor, 0.0)
            part_mine[k * 128 : (k + 1) * 128, :] = (
                part[k * 128 : (k + 1) * 128] - here * texts[:128, :].astype(f32)
            ).astype(bf16)

    @pl.when(i >= half)
    def _():
        part_other[...] = part.astype(bf16)

    share = lax.dot_general(
        weights, images, (((0,), (0,)), ((), ())), preferred_element_type=f32
    )

    @pl.when(i == 0)
    def _():
        total[...] = share

    @pl.when(i > 0)
    def _():
        total[...] += share

    @pl.when(i == pl.num_programs(0) - 1)
    def _():
        text_part[:128, :] = (total[:128, :] - sharpness_factor * own[...].astype(f32)).astype(bf16)
        text_part[128:, :] = total[128:, :].astype(bf16)


def block_grads(place, logits, row_total, column_total, mine, other, texts, own):
    n, m = logits.shape
    width = texts.shape[1]
    half = n // TILE // 2
    first = pl.BlockSpec((TILE, width), lambda i: (jnp.minimum(i, half - 1), 0))
    second = pl.BlockSpec((TILE, width), lambda i: (jnp.maximum(i - half, 0), 0))
    return pl.pallas_call(
        grads_kernel,
        grid=(n // TILE,),
        in_specs=[
            pl.BlockSpec(memory_space=pltpu.SMEM),
            pl.BlockSpec((TILE, m), lambda i: (i, 0)),
            pl.BlockSpec((1, TILE), lambda i: (0, i)),
            pl.BlockSpec((1, m), lambda i: (0, 0)),
            first,
            second,
            pl.BlockSpec((m, width), lambda i: (0, 0)),
            pl.BlockSpec(own.shape, lambda i: (0, 0)),
        ],
        out_specs=[first, second, pl.BlockSpec((m, width), lambda i: (0, 0))],
        out_shape=[
            jax.ShapeDtypeStruct((n // 2, width), bf16),
            jax.ShapeDtypeStruct((n // 2, width), bf16),
            jax.ShapeDtypeStruct((m, width), bf16),
        ],
        scratch_shapes=[pltpu.VMEM((m, width), f32)],
        compiler_params=params(GRADS_MIB),
        cost_estimate=pl.CostEstimate(
            flops=4 * n * m * width,
            bytes_accessed=4 * n * m + 4 * (n + m) * width,
            transcendentals=2 * n * m,
        ),
        name="block_grads",
    )(place, logits, row_total, column_total, mine, other, texts, own)


def whole_kernel(core, mine, other, image, text):
    rows = image.shape[0] // mine.shape[0]

    def put(src):
        image[...] = src[:, :rows].astype(f32).reshape(image.shape)
        text[...] = src[:, rows:].astype(f32).reshape(text.shape)

    @pl.when(pl.program_id(0) == core[0])
    def _():
        put(mine)

    @pl.when(pl.program_id(0) != core[0])
    def _():
        put(other)


def whole_terms(core, mine, other, rows):
    n, both, width = mine.shape
    block = pl.BlockSpec(mine.shape, lambda h: (0, 0, 0))
    return pl.pallas_call(
        whole_kernel,
        grid=(2,),
        in_specs=[pl.BlockSpec(memory_space=pltpu.SMEM), block, block],
        out_specs=[
            pl.BlockSpec((n * rows, width), lambda h: (h, 0)),
            pl.BlockSpec((n * (both - rows), width), lambda h: (h, 0)),
        ],
        out_shape=[
            jax.ShapeDtypeStruct((2 * n * rows, width), f32),
            jax.ShapeDtypeStruct((2 * n * (both - rows), width), f32),
        ],
        compiler_params=params(),
        cost_estimate=pl.CostEstimate(flops=0, bytes_accessed=12 * n * both * width, transcendentals=0),
        name="whole_terms",
    )(core, mine, other)


def other_half(v, core):
    n = v.shape[1] // 2
    mine = lax.dynamic_slice_in_dim(v, core * n, n, axis=1)
    away = lax.dynamic_slice_in_dim(v, (1 - core) * n, n, axis=1)
    return jnp.concatenate([mine, from_core(away)], axis=0)


def back_rows(unit_rows, radius, emb_grad):
    along = jnp.sum(unit_rows * emb_grad, axis=1, keepdims=True)
    return ((emb_grad - unit_rows * along) / radius).astype(bf16)


def feature_grad(projected_grad, weight):
    return lax.dot_general(
        projected_grad, weight, (((1,), (1,)), ((), ())), preferred_element_type=f32
    ).astype(bf16)


def weight_grad(features, projected_grad):
    return lax.dot_general(
        features, projected_grad, (((0,), (0,)), ((), ())), preferred_element_type=f32
    )


def reduce_weights(image_term, text_term, loss_part, core):
    n = 16
    width = image_term.shape[1]
    image_blocks = image_term.astype(bf16).reshape(n, -1, width)
    text_blocks = text_term.astype(bf16).reshape(n, -1, width)
    rows = image_blocks.shape[1]
    both = rows + text_blocks.shape[1]
    lane = lax.broadcasted_iota(jnp.int32, (8, width), 1)

    def split(v):
        high = lax.reduce_precision(v, 8, 7)
        low = (v - high).astype(bf16)
        return jnp.where(lane == 0, high.astype(bf16), jnp.where(lane == 1, low, jnp.zeros((), bf16)))

    extra = jnp.broadcast_to(split(loss_part), (n, 8, width))
    sent = jnp.concatenate([image_blocks, text_blocks, extra], axis=1)
    got = plus(*lax.all_to_all(sent, YZ, 0, 0))
    block = jnp.concatenate(
        [got[:both].astype(bf16), split(got[both:, 0:1] + got[both:, 1:2])], axis=0
    )
    total = plus(block, *(from_x(block, k) for k in (1, 3, 2)))
    loss = total[both, 0] + total[both, 1]
    full = spread(total[:both].astype(bf16), YZ, n)
    image, text = whole_terms(core.reshape(1), full, from_core(full), rows)
    return image, text, loss


def body(image_features, text_features, image_projection, text_projection):
    core = lax.axis_index("c")
    place = lax.axis_index(PAIR_Z)
    text_unit, text_radius = normalize_rows(text_features, text_projection)
    text_emb = text_unit.astype(bf16)
    image_unit, image_radius = normalize_rows(image_features, image_projection)
    image_emb = image_unit.astype(bf16)
    own, width = image_emb.shape
    images = spread(image_emb, PAIR_Z, 8).reshape(8 * own, width)
    pair = jnp.concatenate([text_emb, from_mirror(text_emb)], axis=0)
    pair, later_image, later_text = lax.optimization_barrier((pair, image_features, text_features))
    image_halves = other_half(later_image, core)
    text_halves = other_half(later_text, core)
    images, texts, image_halves, text_halves = lax.optimization_barrier(
        (images, gather_text(pair), image_halves, text_halves)
    )
    images_other = hbm(from_core(images))
    texts = hbm(texts)
    logits, row_part, column_part = block_logits(images, images_other, texts)
    row_total = row_totals(row_part)
    column_total = column_totals(column_part)
    image_part, other_part, text_part = block_grads(
        place.reshape(1), logits, row_total, column_total, images, images_other, texts, image_emb
    )
    image_part = plus(image_part, from_core(other_part)).astype(bf16)
    image_emb_grad = plus(*lax.all_to_all(image_part.reshape(8, own, width), PAIR_Z, 0, 0))
    text_emb_grad = scatter_text(text_part)
    matched = sharpness_factor * jnp.sum(image_emb.astype(f32) * text_emb.astype(f32), axis=1)
    own_rows = lax.dynamic_slice_in_dim(row_total[0], place * own, own)
    loss_part = jnp.sum(
        jnp.log(own_rows)
        + jnp.log(column_total[0, :own])
        + 2.0 * (sharpness_factor - matched)
    )
    loss_part = loss_part + from_core(loss_part)
    text_back = back_rows(text_unit, text_radius, text_emb_grad)
    image_back = back_rows(image_unit, image_radius, image_emb_grad)
    text_both = jnp.concatenate([text_back, from_core(text_back)], axis=0)
    image_both = jnp.concatenate([image_back, from_core(image_back)], axis=0)
    text_term = weight_grad(text_halves, text_both)
    image_term = weight_grad(image_halves, image_both)
    image_projection_grad, text_projection_grad, loss = reduce_weights(
        image_term, text_term, loss_part, core
    )
    pairs = own * 128
    return (
        loss / (2.0 * pairs),
        feature_grad(image_back, image_projection),
        feature_grad(text_back, text_projection),
        image_projection_grad,
        text_projection_grad,
    )


def solution(mesh):
    grid = Mesh(mesh.devices.reshape(2, 4, 2, 4, 2), ALL)
    rows = P(ALL, None)
    return jax.shard_map(
        body,
        mesh=grid,
        in_specs=(rows, rows, P(), P()),
        out_specs=(P(), rows, rows, P(), P()),
        check_vma=False,
    )
```

time: 212 us -> 205 us (0.967)
  local copies, waits for them, and re-layouts: 20.9 us -> 10.7 us
  starting transfers between devices: 56 us -> 65.3 us
  Pallas kernels: 19.3 us -> 26.1 us
  blocking collectives: 26.9 us -> 20.7 us
  waiting for transfers between devices: 58.8 us -> 53.6 us
    ppermute x7 -> x9, starting transfers between devices: 11 us -> 19.5 us  [from_core(): return lax.ppermute(v, 'c', [(0, 1), (1, 0)])]
    ppermute x11, waiting for transfers between devices: 22.3 us -> 14.2 us  [from_y(): return lax.ppermute(v, 'y', [(i, (i - k) % 4) for i in range(4)])]
    unnamed x36 -> x40, local copies, waits for them, and re-layouts: 12.2 us -> 5.85 us
    all_to_all x1, blocking collectives: 26.9 us -> 20.7 us  [spread(): return lax.all_to_all(jnp.broadcast_to(v[None], (n,) + v.shape), axes, 0, 0)]
    ppermute x1 -> x7, starting transfers between devices: 3 us -> 8.94 us  [the longest x3 4.49 us: row_totals(): lax.ppermute(part, 'z', [(i, (i - k) % 4) for i in range(4)])]
    ppermute x1 -> x7, waiting for transfers between devices: 1.53 us -> 6.71 us  [the longest x3 4.47 us: from_x(): return lax.ppermute(v, X, [(i, (i - k) % 4) for i in range(4)])]
    all_to_all x3 -> x2, starting transfers between devices: 15.8 us -> 10.9 us  [the longest x1 6.62 us: reduce_weights(): got = plus(*lax.all_to_all(sent, YZ, 0, 0))]
    all_to_all x3 -> x2, waiting for transfers between devices: 26.3 us -> 22.1 us  [the longest x1 22.1 us: reduce_weights(): got = plus(*lax.all_to_all(sent, YZ, 0, 0))]
  transfers between devices with their start and end apart: 26 -> 33, of which waited for: 13 -> 18; matrix products, arithmetic and copies ran while one was open for 13% -> 11% of each run, Pallas kernels for 0% -> 0%
where the time goes in v4:
time: 205 us
  starting transfers between devices  65.3 us (32%)
  waiting for transfers between devices  53.6 us (26%)
  Pallas kernels  26.1 us (13%)
  blocking collectives  20.7 us (10%)
  other arithmetic  14.4 us (7%)
  local copies, waits for them, and re-layouts  10.7 us (5%)
  matrix products  7.19 us (4%)
  between operations  6.47 us (3%)
    all_to_all x1, waiting for transfers between devices, reduce_weights(): got = plus(*lax.all_to_all(sent, YZ, 0, 0))  22.1 us
    all_to_all x1, blocking collectives, spread(): return lax.all_to_all(jnp.broadcast_to(v[None], (n,) + v.shape), axes, 0, 0)  20.7 us
    ppermute x9, starting transfers between devices, from_core(): return lax.ppermute(v, 'c', [(0, 1), (1, 0)])  19.5 us
    pallas_call x1, Pallas kernels, block_grads(): pl.pallas_call(grads_kernel, grid=(n // TILE,), in_specs=[pl.BlockSpec(me...  15 us
    ppermute x11, waiting for transfers between devices, from_y(): return lax.ppermute(v, 'y', [(i, (i - k) % 4) for i in range(4)])  14.2 us
    ppermute x11, starting transfers between devices, from_y(): return lax.ppermute(v, 'y', [(i, (i - k) % 4) for i in range(4)])  13.4 us
    pallas_call x1, Pallas kernels, block_logits(): pl.pallas_call(logits_kernel, grid=(n // LTILE,), in_specs=[pl.BlockSpec(...  8.51 us
    ppermute x3, starting transfers between devices, from_mirror(): return lax.ppermute(v, X, [(i, 3 - i) for i in range(4)])  7.55 us
  transfers between devices with their start and end apart: 33, of which 18 were waited for; matrix products, arithmetic and copies ran while one was open for 11% of the time, Pallas kernels for 0%

profile of v4, /device:TPU:1, one launch (start us, length us, event | category | flops | bytes accessed | tf_op | source)
XLA Modules:
  0.0 204.5 jit_solution(8321551087110245352)
XLA Ops:
  0.7 1.4 copy-done
  2.0 1.5 multiply_reduce_fusion.3
  4.4 0.7 multiply_reduce_fusion
  5.1 3.3 %collective-permute-start = (bf16[128,768]{1,0:T(8,128)(2,1)S(1)}, bf16[128,768]{1,0:T(8,128)(2,1)}, u32[]{:S(2)}, u32[]{:S(2)}) collective-permute-start(bf16[128,768]{1,0:T(8,128)(2,1)S(1)} %get-tuple-element.45), channel_id=1, source_target_pairs={{0,72},{8,64},{64,8},{72,0},{1,73},{9,65},{65,9},{73,1},{2,74},{10... | collective-permute-start | bytes 589832 | tf_op jit(solution)/shard_map/ppermute | solution.py:32
  8.4 1.2 broadcast_in_dim.55
  9.7 5.0 %all-to-all-start = ((bf16[8,128,768]{2,1,0:T(8,128)(2,1)}), bf16[8,128,768]{2,1,0:T(8,128)(2,1)S(1)}, u32[]{:S(2)}, u32[]{:S(2)}) async-start(bf16[8,128,768]{2,1,0:T(8,128)(2,1)} %broadcast_in_dim.55), calls=%async_computation | async-start | bytes 3145728 | tf_op jit(solution)/shard_map/all_to_all | solution.py:48
  14.7 1.0 pad_maximum_fusion.1
  15.7 2.8 %collective-permute-start.1 = (bf16[256,768]{1,0:T(8,128)(2,1)S(1)}, bf16[256,768]{1,0:T(8,128)(2,1)S(1)}, u32[]{:S(2)}, u32[]{:S(2)}) collective-permute-start(bf16[256,768]{1,0:T(8,128)(2,1)S(1)} %pad_maximum_fusion.1), channel_id=1, source_target_pairs={{0,48},{16,0},{32,16},{48,32},{1,49},{17,1},{33,17},{49,33},{2,50}... | collective-permute-start | bytes 1179656 | tf_op jit(solution)/shard_map/ppermute | solution.py:40
  18.5 1.0 constant_dynamic-slice_fusion.4
  19.4 1.6 collective-permute-start.5
  21.0 1.0 constant_dynamic-slice_fusion.2
  22.1 0.8 constant_dynamic-update-slice_fusion.4
  24.1 1.5 collective-permute-done.1
  25.6 3.5 %collective-permute-start.2 = (bf16[128,768]{1,0:T(8,128)(2,1)S(1)}, bf16[128,768]{1,0:T(8,128)(2,1)S(1)}, u32[]{:S(2)}, u32[]{:S(2)}) collective-permute-start(bf16[128,768]{1,0:T(8,128)(2,1)S(1)} %slice.122), channel_id=1, source_target_pairs={{0,48},{16,0},{32,16},{48,32},{1,49},{17,1},{33,17},{49,33},{2,50}... | collective-permute-start | bytes 589832 | tf_op jit(solution)/shard_map/ppermute | solution.py:40
  29.1 0.7 pad_maximum_fusion.4
  29.9 0.8 constant_dynamic-update-slice_fusion.3
  30.7 1.0 collective-permute-done.2
  32.4 3.2 %collective-permute-done.4 = bf16[128,768]{1,0:T(8,128)(2,1)S(1)} collective-permute-done((bf16[128,768]{1,0:T(8,128)(2,1)S(1)}, bf16[128,768]{1,0:T(8,128)(2,1)S(1)}, u32[]{:S(2)}, u32[]{:S(2)}) %collective-permute-start.4) | collective-permute-done | bytes 196640 | tf_op jit(solution)/shard_map/ppermute | solution.py:40
  36.4 0.8 constant_dynamic-update-slice_fusion.texts
  37.1 3.6 %collective-permute-start.7 = (bf16[1024,768]{1,0:T(8,128)(2,1)S(1)}, bf16[1024,768]{1,0:T(8,128)(2,1)S(1)}, u32[]{:S(2)}, u32[]{:S(2)}) collective-permute-start(bf16[1024,768]{1,0:T(8,128)(2,1)S(1)} %bitcast.39), channel_id=1, source_target_pairs={{0,1},{1,0},{2,3},{3,2},{4,5},{5,4},{6,7},{7,6},{8,9},{9,8},{10,11... | collective-permute-start | bytes 4718600 | tf_op jit(solution)/shard_map/ppermute | solution.py:28
  40.7 3.0 %collective-permute-done.7.other = bf16[1024,768]{1,0:T(8,128)(2,1)S(1)} collective-permute-done((bf16[1024,768]{1,0:T(8,128)(2,1)S(1)}, bf16[1024,768]{1,0:T(8,128)(2,1)S(1)}, u32[]{:S(2)}, u32[]{:S(2)}) %collective-permute-start.7) | collective-permute-done | bytes 1572896 | tf_op jit(solution)/shard_map/ppermute | solution.py:28
  43.8 1.1 copy-done.17
  44.9 8.5 %block_logits.1 = (f32[2048,1024]{1,0:T(8,128)}, f32[1,2048]{1,0:T(1,128)S(1)}, f32[1,1024]{1,0:T(1,128)S(1)}) custom-call(bf16[1024,768]{1,0:T(8,128)(2,1)S(1)} %bitcast.40, bf16[1024,768]{1,0:T(8,128)(2,1)} %copy-done.17, bf16[1024,768]{1,0:T(8,128)(2,1)} %constant_dynamic-update-slice_fusion.texts), custom_call_target="tpu_custom_call" | custom-call | flops 3221225472 | bytes 13107200 | tf_op jit(solution)/shard_map/block_logits/pallas_call | solution.py:125
  53.8 1.4 collective-permute-start.13
  55.2 2.3 %collective-permute-done.13 = f32[4,2,128]{2,1,0:T(2,128)S(1)} collective-permute-done((f32[4,2,128]{2,1,0:T(2,128)S(1)}, f32[4,2,128]{2,1,0:T(2,128)S(1)}, u32[]{:S(2)}, u32[]{:S(2)}) %collective-permute-start.13) | collective-permute-done | bytes 4128 | tf_op jit(solution)/shard_map/ppermute | solution.py:32
  57.6 0.9 collective-permute-start.14
  59.5 2.0 %collective-permute-done.16 = f32[4,2,128]{2,1,0:T(2,128)S(1)} collective-permute-done((f32[4,2,128]{2,1,0:T(2,128)S(1)}, f32[4,2,128]{2,1,0:T(2,128)S(1)}, u32[]{:S(2)}, u32[]{:S(2)}) %collective-permute-start.16) | collective-permute-done | bytes 4128 | tf_op jit(solution)/shard_map/ppermute | solution.py:40
  62.2 2.7 %collective-permute-start.10 = (f32[1,2048]{1,0:T(1,128)S(1)}, f32[1,2048]{1,0:T(1,128)S(1)}, u32[]{:S(2)}, u32[]{:S(2)}) collective-permute-start(f32[1,2048]{1,0:T(1,128)S(1)} %add.191), channel_id=1, source_target_pairs={{0,6},{2,0},{4,2},{6,4},{1,7},{3,1},{5,3},{7,5},{8,14},{10,8},{12,... | collective-permute-start | bytes 24584 | tf_op jit(solution)/shard_map/ppermute | solution.py:73
  64.9 1.7 collective-permute-start.12
  66.7 1.9 collective-permute-done.11
  68.9 15.0 %block_grads.1 = (bf16[1024,768]{1,0:T(8,128)(2,1)S(1)}, bf16[1024,768]{1,0:T(8,128)(2,1)S(1)}, bf16[1024,768]{1,0:T(8,128)(2,1)S(1)}) custom-call(s32[1]{0:T(128)} %bitcast.1.place, f32[2048,1024]{1,0:T(8,128)} %get-tuple-element.28.logits, f32[1,2048]{1,0:T(1,128)S(1)} %add_add_fusion.1.row_total, f32[1,1024]{1,0:T(1,128)S(1)} %bitcast.42, ...), custom_call_target="tpu_custom_call" | custom-call | flops 6442450944 | bytes 17825792 | tf_op jit(solution)/shard_map/block_grads/pallas_call | solution.py:205
  83.9 4.5 %collective-permute-start.17 = (bf16[1024,768]{1,0:T(8,128)(2,1)S(1)}, bf16[1024,768]{1,0:T(8,128)(2,1)S(1)}, u32[]{:S(2)}, u32[]{:S(2)}) collective-permute-start(bf16[1024,768]{1,0:T(8,128)(2,1)S(1)} %get-tuple-element.32), channel_id=1, source_target_pairs={{0,1},{1,0},{2,3},{3,2},{4,5},{5,4},{6,7},{7,6},{8,9},{9,8},{10,11... | collective-permute-start | bytes 4718600 | tf_op jit(solution)/shard_map/ppermute | solution.py:28
  88.5 0.7 collective-permute-start.19
  89.3 2.0 collective-permute-start.20
  91.3 5.0 %collective-permute-done.19 = bf16[128,768]{1,0:T(8,128)(2,1)S(1)} collective-permute-done((bf16[128,768]{1,0:T(8,128)(2,1)S(1)}, bf16[128,768]{1,0:T(8,128)(2,1)S(1)}, u32[]{:S(2)}, u32[]{:S(2)}) %collective-permute-start.19) | collective-permute-done | bytes 196640 | tf_op jit(solution)/shard_map/ppermute | solution.py:40
  96.4 0.8 pad_maximum_fusion.3
  97.2 1.5 add_convert_fusion
  98.7 4.2 %all-to-all-start.1 = ((bf16[8,128,768]{2,1,0:T(8,128)(2,1)}), bf16[8,128,768]{2,1,0:T(8,128)(2,1)S(1)}, u32[]{:S(2)}, u32[]{:S(2)}) async-start(bf16[8,128,768]{2,1,0:T(8,128)(2,1)} %bitcast.46), calls=%async_computation.1 | async-start | bytes 3145728 | tf_op jit(solution)/shard_map/all_to_all | solution.py:348
  103.0 0.8 pad_maximum_fusion.2
  103.7 0.9 collective-permute-start.21
  104.6 1.8 collective-permute-start.22
  107.0 1.3 fusion.17
  108.2 1.6 collective-permute-start.25
  109.9 1.2 collective-permute-done.25
  114.1 0.7 collective-permute-done.21
  114.8 1.4 convert_add_fusion
  116.2 2.9 %collective-permute-start.23 = (bf16[128,768]{1,0:T(8,128)(2,1)S(1)}, bf16[128,768]{1,0:T(8,128)(2,1)S(1)}, u32[]{:S(2)}, u32[]{:S(2)}) collective-permute-start(bf16[128,768]{1,0:T(8,128)(2,1)S(1)} %slice.167), channel_id=1, source_target_pairs={{0,72},{8,64},{64,8},{72,0},{1,73},{9,65},{65,9},{73,1},{2,74},{10... | collective-permute-start | bytes 589832 | tf_op jit(solution)/shard_map/ppermute | solution.py:32
  119.1 3.3 %collective-permute-done.23 = bf16[128,768]{1,0:T(8,128)(2,1)S(1)} collective-permute-done((bf16[128,768]{1,0:T(8,128)(2,1)S(1)}, bf16[128,768]{1,0:T(8,128)(2,1)S(1)}, u32[]{:S(2)}, u32[]{:S(2)}) %collective-permute-start.23) | collective-permute-done | bytes 196640 | tf_op jit(solution)/shard_map/ppermute | solution.py:32
  122.4 1.2 multiply_reduce_fusion.1
  123.6 0.8 divide_convert_fusion
  124.4 2.9 %collective-permute-start.24 = (bf16[128,768]{1,0:T(8,128)(2,1)}, bf16[128,768]{1,0:T(8,128)(2,1)}, u32[]{:S(2)}, u32[]{:S(2)}) collective-permute-start(bf16[128,768]{1,0:T(8,128)(2,1)} %divide_convert_fusion), channel_id=1, source_target_pairs={{0,1},{1,0},{2,3},{3,2},{4,5},{5,4},{6,7},{7,6},{8,9},{9,8},{10,11... | collective-permute-start | bytes 589832 | tf_op jit(solution)/shard_map/ppermute | solution.py:28
  127.3 0.9 fusion.6
  128.7 1.4 convolution_convert_fusion.1
  130.6 1.3 pad_maximum_fusion
  131.8 6.6 %all-to-all-start.2 = ((bf16[16,64,768]{2,1,0:T(8,128)(2,1)}), bf16[16,64,768]{2,1,0:T(8,128)(2,1)S(1)}, u32[]{:S(2)}, u32[]{:S(2)}) async-start(bf16[16,64,768]{2,1,0:T(8,128)(2,1)} %pad_maximum_fusion), calls=%async_computation.2 | async-start | bytes 3145728 | tf_op jit(solution)/shard_map/all_to_all | solution.py:312
  138.5 22.1 %all-to-all-done.2 = bf16[16,64,768]{2,1,0:T(8,128)(2,1)S(1)} async-done(((bf16[16,64,768]{2,1,0:T(8,128)(2,1)}), bf16[16,64,768]{2,1,0:T(8,128)(2,1)S(1)}, u32[]{:S(2)}, u32[]{:S(2)}) %all-to-all-start.2) | async-done | bytes 1572896 | tf_op jit(solution)/shard_map/all_to_all | solution.py:312
  161.1 2.9 %collective-permute-start.26 = (bf16[64,768]{1,0:T(8,128)(2,1)S(1)}, bf16[64,768]{1,0:T(8,128)(2,1)S(1)}, u32[]{:S(2)}, u32[]{:S(2)}) collective-permute-start(bf16[64,768]{1,0:T(8,128)(2,1)S(1)} %pad_maximum_fusion.6), channel_id=1, source_target_pairs={{0,72},{8,0},{64,8},{72,64},{1,73},{9,1},{65,9},{73,65},{2,74},{10... | collective-permute-start | bytes 294920 | tf_op jit(solution)/shard_map/ppermute | solution.py:36
  163.9 1.3 collective-permute-start.28
  165.6 4.1 %collective-permute-done.27 = bf16[64,768]{1,0:T(8,128)(2,1)S(1)} collective-permute-done((bf16[64,768]{1,0:T(8,128)(2,1)S(1)}, bf16[64,768]{1,0:T(8,128)(2,1)S(1)}, u32[]{:S(2)}, u32[]{:S(2)}) %collective-permute-start.27) | collective-permute-done | bytes 98336 | tf_op jit(solution)/shard_map/ppermute | solution.py:36
  169.9 20.7 %all_to_all.20.mine = bf16[16,56,768]{2,1,0:T(8,128)(2,1)S(1)} all-to-all(bf16[16,56,768]{2,1,0:T(8,128)(2,1)S(1)} %broadcast_in_dim.65), channel_id=1, replica_groups=mesh['xh'=2,'y'=4,'xl'=2,'z'=4,'c'=2] {'y','z'}, dimensions={0} | all-to-all | bytes 2752512 | tf_op jit(solution)/shard_map/all_to_all | solution.py:48
  190.6 4.7 %collective-permute-start.29 = (bf16[16,56,768]{2,1,0:T(8,128)(2,1)S(1)}, bf16[16,56,768]{2,1,0:T(8,128)(2,1)S(1)}, u32[]{:S(2)}, u32[]{:S(2)}) collective-permute-start(bf16[16,56,768]{2,1,0:T(8,128)(2,1)S(1)} %all_to_all.20.mine), channel_id=1, source_target_pairs={{0,1},{1,0},{2,3},{3,2},{4,5},{5,4},{6,7},{7,6},{8,9},{9,8},{10,11... | collective-permute-start | bytes 4128776 | tf_op jit(solution)/shard_map/ppermute | solution.py:28
  195.3 2.1 %convolution_convert_fusion.3 = bf16[128,768]{1,0:T(8,128)(2,1)} fusion(bf16[128,768]{1,0:T(8,128)(2,1)} %divide_convert_fusion, bf16[768,768]{1,0:T(8,128)(2,1)S(1)} %copy-done.7), kind=kOutput, calls=%fused_computation.5 | convolution fusion | flops 151093248 | bytes 1572864 | tf_op jit(solution)/shard_map/dot_general | solution.py:285
  197.5 1.3 convolution_convert_fusion.2
  200.7 2.7 %whole_terms.1 = (f32[1024,768]{1,0:T(8,128)}, f32[768,768]{1,0:T(8,128)}) custom-call(s32[1]{0:T(128)} %bitcast.12.core, bf16[16,56,768]{2,1,0:T(8,128)(2,1)S(1)} %all_to_all.20.mine, bf16[16,56,768]{2,1,0:T(8,128)(2,1)S(1)} %collective-permute-done.29.other), custom_call_target="tpu_custom_call" | custom-call | bytes 8257536 | tf_op jit(solution)/shard_map/whole_terms/pallas_call | solution.py:254
  (102 shorter events, 9.3 us)
Async XLA Ops:
  0.6 1.4 copy-start
  0.6 2.9 %copy-start.11 = (bf16[128,768]{1,0:T(8,128)(2,1)S(1)}, bf16[128,768]{1,0:T(8,128)(2,1)}, u32[]{:S(2)}) copy-start(bf16[128,768]{1,0:T(8,128)(2,1)} %param.5) | copy-start | bytes 589828
  2.0 1.5 copy-start.6
  3.6 0.8 copy-start.2
  4.0 1.1 copy-start.4
  4.0 5.6 %copy-start.13 = (f32[128]{0:T(128)}, f32[128]{0:T(128)S(1)}, u32[]{:S(2)}) copy-start(f32[128]{0:T(128)S(1)} %get-tuple-element.67) | copy-start | bytes 1540
  5.1 9.6 %collective-permute-start = (bf16[128,768]{1,0:T(8,128)(2,1)S(1)}, bf16[128,768]{1,0:T(8,128)(2,1)}, u32[]{:S(2)}, u32[]{:S(2)}) collective-permute-start(bf16[128,768]{1,0:T(8,128)(2,1)S(1)} %get-tuple-element.45), channel_id=1, source_target_pairs={{0,72},{8,64},{64,8},{72,0},{1,73},{9,65},{65,9},{73,1},{2,74},{10... | collective-permute-start | bytes 589832 | tf_op jit(solution)/shard_map/ppermute | solution.py:32
  9.7 27.5 %all-to-all-start = ((bf16[8,128,768]{2,1,0:T(8,128)(2,1)}), bf16[8,128,768]{2,1,0:T(8,128)(2,1)S(1)}, u32[]{:S(2)}, u32[]{:S(2)}) async-start(bf16[8,128,768]{2,1,0:T(8,128)(2,1)} %broadcast_in_dim.55), calls=%async_computation | async-start | bytes 3145728 | tf_op jit(solution)/shard_map/all_to_all | solution.py:48
  15.7 10.0 %collective-permute-start.1 = (bf16[256,768]{1,0:T(8,128)(2,1)S(1)}, bf16[256,768]{1,0:T(8,128)(2,1)S(1)}, u32[]{:S(2)}, u32[]{:S(2)}) collective-permute-start(bf16[256,768]{1,0:T(8,128)(2,1)S(1)} %pad_maximum_fusion.1), channel_id=1, source_target_pairs={{0,48},{16,0},{32,16},{48,32},{1,49},{17,1},{33,17},{49,33},{2,50}... | collective-permute-start | bytes 1179656 | tf_op jit(solution)/shard_map/ppermute | solution.py:40
  18.5 11.4 %collective-permute-start.3 = (bf16[256,768]{1,0:T(8,128)(2,1)S(1)}, bf16[256,768]{1,0:T(8,128)(2,1)S(1)}, u32[]{:S(2)}, u32[]{:S(2)}) collective-permute-start(bf16[256,768]{1,0:T(8,128)(2,1)S(1)} %pad_maximum_fusion.1), channel_id=1, source_target_pairs={{0,16},{16,32},{32,48},{48,0},{1,17},{17,33},{33,49},{49,1},{2,18}... | collective-permute-start | bytes 1179656 | tf_op jit(solution)/shard_map/ppermute | solution.py:40
  19.4 9.7 %collective-permute-start.5 = (bf16[128,512]{1,0:T(8,128)(2,1)S(1)}, bf16[128,512]{1,0:T(8,128)(2,1)S(1)}, u32[]{:S(2)}, u32[]{:S(2)}) collective-permute-start(bf16[128,512]{1,0:T(8,128)(2,1)S(1)} %get-tuple-element.53), channel_id=1, source_target_pairs={{0,1},{1,0},{2,3},{3,2},{4,5},{5,4},{6,7},{7,6},{8,9},{9,8},{10,11... | collective-permute-start | bytes 393224 | tf_op jit(solution)/shard_map/ppermute | solution.py:28
  22.0 1.4 collective-permute-start.6
  25.6 6.1 %collective-permute-start.2 = (bf16[128,768]{1,0:T(8,128)(2,1)S(1)}, bf16[128,768]{1,0:T(8,128)(2,1)S(1)}, u32[]{:S(2)}, u32[]{:S(2)}) collective-permute-start(bf16[128,768]{1,0:T(8,128)(2,1)S(1)} %slice.122), channel_id=1, source_target_pairs={{0,48},{16,0},{32,16},{48,32},{1,49},{17,1},{33,17},{49,33},{2,50}... | collective-permute-start | bytes 589832 | tf_op jit(solution)/shard_map/ppermute | solution.py:40
  29.9 5.8 %collective-permute-start.4 = (bf16[128,768]{1,0:T(8,128)(2,1)S(1)}, bf16[128,768]{1,0:T(8,128)(2,1)S(1)}, u32[]{:S(2)}, u32[]{:S(2)}) collective-permute-start(bf16[128,768]{1,0:T(8,128)(2,1)S(1)} %slice.123), channel_id=1, source_target_pairs={{0,16},{16,32},{32,48},{48,0},{1,17},{17,33},{33,49},{49,1},{2,18}... | collective-permute-start | bytes 589832 | tf_op jit(solution)/shard_map/ppermute | solution.py:40
  37.1 6.6 %collective-permute-start.7 = (bf16[1024,768]{1,0:T(8,128)(2,1)S(1)}, bf16[1024,768]{1,0:T(8,128)(2,1)S(1)}, u32[]{:S(2)}, u32[]{:S(2)}) collective-permute-start(bf16[1024,768]{1,0:T(8,128)(2,1)S(1)} %bitcast.39), channel_id=1, source_target_pairs={{0,1},{1,0},{2,3},{3,2},{4,5},{5,4},{6,7},{7,6},{8,9},{9,8},{10,11... | collective-permute-start | bytes 4718600 | tf_op jit(solution)/shard_map/ppermute | solution.py:28
  43.8 1.1 copy-start.17
  53.4 5.7 %collective-permute-start.8 = (f32[1,2048]{1,0:T(1,128)S(1)}, f32[1,2048]{1,0:T(1,128)S(1)}, u32[]{:S(2)}, u32[]{:S(2)}) collective-permute-start(f32[1,2048]{1,0:T(1,128)S(1)} %get-tuple-element.29), channel_id=1, source_target_pairs={{0,1},{1,0},{2,3},{3,2},{4,5},{5,4},{6,7},{7,6},{8,9},{9,8},{10,11... | collective-permute-start | bytes 24584 | tf_op jit(solution)/shard_map/ppermute | solution.py:28
  53.8 3.7 %collective-permute-start.13 = (f32[4,2,128]{2,1,0:T(2,128)S(1)}, f32[4,2,128]{2,1,0:T(2,128)S(1)}, u32[]{:S(2)}, u32[]{:S(2)}) collective-permute-start(f32[4,2,128]{2,1,0:T(2,128)S(1)} %bitcast.44), channel_id=1, source_target_pairs={{0,72},{8,64},{64,8},{72,0},{1,73},{9,65},{65,9},{73,1},{2,74},{10... | collective-permute-start | bytes 12296 | tf_op jit(solution)/shard_map/ppermute | solution.py:32
  57.5 4.0 %collective-permute-start.16 = (f32[4,2,128]{2,1,0:T(2,128)S(1)}, f32[4,2,128]{2,1,0:T(2,128)S(1)}, u32[]{:S(2)}, u32[]{:S(2)}) collective-permute-start(f32[4,2,128]{2,1,0:T(2,128)S(1)} %add.195), channel_id=1, source_target_pairs={{0,32},{16,48},{32,0},{48,16},{1,33},{17,49},{33,1},{49,17},{2,34}... | collective-permute-start | bytes 12296 | tf_op jit(solution)/shard_map/ppermute | solution.py:40
  57.6 4.0 %collective-permute-start.14 = (f32[4,2,128]{2,1,0:T(2,128)S(1)}, f32[4,2,128]{2,1,0:T(2,128)S(1)}, u32[]{:S(2)}, u32[]{:S(2)}) collective-permute-start(f32[4,2,128]{2,1,0:T(2,128)S(1)} %add.195), channel_id=1, source_target_pairs={{0,48},{16,0},{32,16},{48,32},{1,49},{17,1},{33,17},{49,33},{2,50}... | collective-permute-start | bytes 12296 | tf_op jit(solution)/shard_map/ppermute | solution.py:40
  58.5 3.7 %collective-permute-start.15 = (f32[4,2,128]{2,1,0:T(2,128)S(1)}, f32[4,2,128]{2,1,0:T(2,128)S(1)}, u32[]{:S(2)}, u32[]{:S(2)}) collective-permute-start(f32[4,2,128]{2,1,0:T(2,128)S(1)} %add.195), channel_id=1, source_target_pairs={{0,16},{16,32},{32,48},{48,0},{1,17},{17,33},{33,49},{49,1},{2,18}... | collective-permute-start | bytes 12296 | tf_op jit(solution)/shard_map/ppermute | solution.py:40
  59.1 3.0 %collective-permute-start.9 = (f32[1,2048]{1,0:T(1,128)S(1)}, f32[1,2048]{1,0:T(1,128)S(1)}, u32[]{:S(2)}, u32[]{:S(2)}) collective-permute-start(f32[1,2048]{1,0:T(1,128)S(1)} %maximum_add_fusion), channel_id=1, source_target_pairs={{0,8},{8,0},{1,9},{9,1},{2,10},{10,2},{3,11},{11,3},{4,12},{12,4},... | collective-permute-start | bytes 24584 | tf_op jit(solution)/shard_map/ppermute | solution.py:72
  62.2 4.5 %collective-permute-start.10 = (f32[1,2048]{1,0:T(1,128)S(1)}, f32[1,2048]{1,0:T(1,128)S(1)}, u32[]{:S(2)}, u32[]{:S(2)}) collective-permute-start(f32[1,2048]{1,0:T(1,128)S(1)} %add.191), channel_id=1, source_target_pairs={{0,6},{2,0},{4,2},{6,4},{1,7},{3,1},{5,3},{7,5},{8,14},{10,8},{12,... | collective-permute-start | bytes 24584 | tf_op jit(solution)/shard_map/ppermute | solution.py:73
  64.9 3.7 %collective-permute-start.11 = (f32[1,2048]{1,0:T(1,128)S(1)}, f32[1,2048]{1,0:T(1,128)S(1)}, u32[]{:S(2)}, u32[]{:S(2)}) collective-permute-start(f32[1,2048]{1,0:T(1,128)S(1)} %add.191), channel_id=1, source_target_pairs={{0,2},{2,4},{4,6},{6,0},{1,3},{3,5},{5,7},{7,1},{8,10},{10,12},{12... | collective-permute-start | bytes 24584 | tf_op jit(solution)/shard_map/ppermute | solution.py:73
  64.9 4.0 %collective-permute-start.12 = (f32[1,2048]{1,0:T(1,128)S(1)}, f32[1,2048]{1,0:T(1,128)S(1)}, u32[]{:S(2)}, u32[]{:S(2)}) collective-permute-start(f32[1,2048]{1,0:T(1,128)S(1)} %add.191), channel_id=1, source_target_pairs={{0,4},{2,6},{4,0},{6,2},{1,5},{3,7},{5,1},{7,3},{8,12},{10,14},{12... | collective-permute-start | bytes 24584 | tf_op jit(solution)/shard_map/ppermute | solution.py:73
  83.9 13.3 %copy-start.1 = (bf16[1024,768]{1,0:T(8,128)(2,1)}, bf16[1024,768]{1,0:T(8,128)(2,1)S(1)}, u32[]{:S(2)}) copy-start(bf16[1024,768]{1,0:T(8,128)(2,1)S(1)} %get-tuple-element.34) | copy-start | bytes 4718596
  83.9 13.3 %collective-permute-start.17 = (bf16[1024,768]{1,0:T(8,128)(2,1)S(1)}, bf16[1024,768]{1,0:T(8,128)(2,1)S(1)}, u32[]{:S(2)}, u32[]{:S(2)}) collective-permute-start(bf16[1024,768]{1,0:T(8,128)(2,1)S(1)} %get-tuple-element.32), channel_id=1, source_target_pairs={{0,1},{1,0},{2,3},{3,2},{4,5},{5,4},{6,7},{7,6},{8,9},{9,8},{10,11... | collective-permute-start | bytes 4718600 | tf_op jit(solution)/shard_map/ppermute | solution.py:28
  88.5 7.8 %collective-permute-start.19 = (bf16[128,768]{1,0:T(8,128)(2,1)S(1)}, bf16[128,768]{1,0:T(8,128)(2,1)S(1)}, u32[]{:S(2)}, u32[]{:S(2)}) collective-permute-start(bf16[128,768]{1,0:T(8,128)(2,1)S(1)} %get-tuple-element.49), channel_id=1, source_target_pairs={{0,16},{16,32},{32,48},{48,0},{1,17},{17,33},{33,49},{49,1},{2,18}... | collective-permute-start | bytes 589832 | tf_op jit(solution)/shard_map/ppermute | solution.py:40
  89.3 7.1 %collective-permute-start.20 = (bf16[128,768]{1,0:T(8,128)(2,1)S(1)}, bf16[128,768]{1,0:T(8,128)(2,1)S(1)}, u32[]{:S(2)}, u32[]{:S(2)}) collective-permute-start(bf16[128,768]{1,0:T(8,128)(2,1)S(1)} %get-tuple-element.47), channel_id=1, source_target_pairs={{0,48},{16,0},{32,16},{48,32},{1,49},{17,1},{33,17},{49,33},{2,50}... | collective-permute-start | bytes 589832 | tf_op jit(solution)/shard_map/ppermute | solution.py:40
  98.7 28.6 %all-to-all-start.1 = ((bf16[8,128,768]{2,1,0:T(8,128)(2,1)}), bf16[8,128,768]{2,1,0:T(8,128)(2,1)S(1)}, u32[]{:S(2)}, u32[]{:S(2)}) async-start(bf16[8,128,768]{2,1,0:T(8,128)(2,1)} %bitcast.46), calls=%async_computation.1 | async-start | bytes 3145728 | tf_op jit(solution)/shard_map/all_to_all | solution.py:348
  103.7 11.1 %collective-permute-start.21 = (bf16[256,768]{1,0:T(8,128)(2,1)}, bf16[256,768]{1,0:T(8,128)(2,1)}, u32[]{:S(2)}, u32[]{:S(2)}) collective-permute-start(bf16[256,768]{1,0:T(8,128)(2,1)} %pad_maximum_fusion.2), channel_id=1, source_target_pairs={{0,16},{16,32},{32,48},{48,0},{1,17},{17,33},{33,49},{49,1},{2,18}... | collective-permute-start | bytes 1179656 | tf_op jit(solution)/shard_map/ppermute | solution.py:40
  104.6 10.2 %collective-permute-start.22 = (bf16[256,768]{1,0:T(8,128)(2,1)}, bf16[256,768]{1,0:T(8,128)(2,1)}, u32[]{:S(2)}, u32[]{:S(2)}) collective-permute-start(bf16[256,768]{1,0:T(8,128)(2,1)} %pad_maximum_fusion.3), channel_id=1, source_target_pairs={{0,48},{16,0},{32,16},{48,32},{1,49},{17,1},{33,17},{49,33},{2,50}... | collective-permute-start | bytes 1179656 | tf_op jit(solution)/shard_map/ppermute | solution.py:40
  108.2 2.8 %collective-permute-start.25 = (f32[]{:T(128)}, f32[]{:T(128)}, u32[]{:S(2)}, u32[]{:S(2)}) collective-permute-start(f32[]{:T(128)} %fusion.17), channel_id=1, source_target_pairs={{0,1},{1,0},{2,3},{3,2},{4,5},{5,4},{6,7},{7,6},{8,9},{9,8},{10,11... | collective-permute-start | bytes 20 | tf_op jit(solution)/shard_map/ppermute | solution.py:28
  114.0 5.0 %copy-start.15 = (pred[768]{0:T(1024)(128)(4,1)S(1)}, pred[768]{0:T(1024)(128)(4,1)}, u32[]{:S(2)}) copy-start(pred[768]{0:T(1024)(128)(4,1)} %iota_compare_fusion.1) | copy-start | bytes 2308
  114.0 9.6 %copy-start.5 = (f32[128,768]{1,0:T(8,128)S(1)}, f32[128,768]{1,0:T(8,128)}, u32[]{:S(2)}) copy-start(f32[128,768]{1,0:T(8,128)} %copy-done.4) | copy-start | bytes 1179652
  116.2 11.1 %copy-start.3 = (f32[128,768]{1,0:T(8,128)S(1)}, f32[128,768]{1,0:T(8,128)}, u32[]{:S(2)}) copy-start(f32[128,768]{1,0:T(8,128)} %copy-done.2) | copy-start | bytes 1179652
  116.2 6.2 %collective-permute-start.23 = (bf16[128,768]{1,0:T(8,128)(2,1)S(1)}, bf16[128,768]{1,0:T(8,128)(2,1)S(1)}, u32[]{:S(2)}, u32[]{:S(2)}) collective-permute-start(bf16[128,768]{1,0:T(8,128)(2,1)S(1)} %slice.167), channel_id=1, source_target_pairs={{0,72},{8,64},{64,8},{72,0},{1,73},{9,65},{65,9},{73,1},{2,74},{10... | collective-permute-start | bytes 589832 | tf_op jit(solution)/shard_map/ppermute | solution.py:32
  124.4 3.8 %copy-start.14 = (f32[128]{0:T(128)S(1)}, f32[128]{0:T(128)}, u32[]{:S(2)}) copy-start(f32[128]{0:T(128)} %copy-done.13) | copy-start | bytes 1540
  124.4 4.3 %collective-permute-start.24 = (bf16[128,768]{1,0:T(8,128)(2,1)}, bf16[128,768]{1,0:T(8,128)(2,1)}, u32[]{:S(2)}, u32[]{:S(2)}) collective-permute-start(bf16[128,768]{1,0:T(8,128)(2,1)} %divide_convert_fusion), channel_id=1, source_target_pairs={{0,1},{1,0},{2,3},{3,2},{4,5},{5,4},{6,7},{7,6},{8,9},{9,8},{10,11... | collective-permute-start | bytes 589832 | tf_op jit(solution)/shard_map/ppermute | solution.py:28
  127.3 1.4 copy-start.12
  128.2 1.9 copy-start.10
  128.4 1.7 copy-start.8
  128.4 1.7 collective-permute-start.18
  131.8 28.7 %all-to-all-start.2 = ((bf16[16,64,768]{2,1,0:T(8,128)(2,1)}), bf16[16,64,768]{2,1,0:T(8,128)(2,1)S(1)}, u32[]{:S(2)}, u32[]{:S(2)}) async-start(bf16[16,64,768]{2,1,0:T(8,128)(2,1)} %pad_maximum_fusion), calls=%async_computation.2 | async-start | bytes 3145728 | tf_op jit(solution)/shard_map/all_to_all | solution.py:312
  138.5 22.5 %copy-start.16 = (pred[768]{0:T(1024)(128)(4,1)S(1)}, pred[768]{0:T(1024)(128)(4,1)}, u32[]{:S(2)}) copy-start(pred[768]{0:T(1024)(128)(4,1)} %iota_compare_fusion.1) | copy-start | bytes 2308
  161.1 4.5 %collective-permute-start.26 = (bf16[64,768]{1,0:T(8,128)(2,1)S(1)}, bf16[64,768]{1,0:T(8,128)(2,1)S(1)}, u32[]{:S(2)}, u32[]{:S(2)}) collective-permute-start(bf16[64,768]{1,0:T(8,128)(2,1)S(1)} %pad_maximum_fusion.6), channel_id=1, source_target_pairs={{0,72},{8,0},{64,8},{72,64},{1,73},{9,1},{65,9},{73,65},{2,74},{10... | collective-permute-start | bytes 294920 | tf_op jit(solution)/shard_map/ppermute | solution.py:36
  163.9 5.7 %collective-permute-start.27 = (bf16[64,768]{1,0:T(8,128)(2,1)S(1)}, bf16[64,768]{1,0:T(8,128)(2,1)S(1)}, u32[]{:S(2)}, u32[]{:S(2)}) collective-permute-start(bf16[64,768]{1,0:T(8,128)(2,1)S(1)} %pad_maximum_fusion.6), channel_id=1, source_target_pairs={{0,8},{8,64},{64,72},{72,0},{1,9},{9,65},{65,73},{73,1},{2,10},{10... | collective-permute-start | bytes 294920 | tf_op jit(solution)/shard_map/ppermute | solution.py:36
  163.9 5.7 %collective-permute-start.28 = (bf16[64,768]{1,0:T(8,128)(2,1)S(1)}, bf16[64,768]{1,0:T(8,128)(2,1)S(1)}, u32[]{:S(2)}, u32[]{:S(2)}) collective-permute-start(bf16[64,768]{1,0:T(8,128)(2,1)S(1)} %pad_maximum_fusion.6), channel_id=1, source_target_pairs={{0,64},{8,72},{64,0},{72,8},{1,65},{9,73},{65,1},{73,9},{2,66},{10... | collective-permute-start | bytes 294920 | tf_op jit(solution)/shard_map/ppermute | solution.py:36
  169.9 25.5 %copy-start.7 = (bf16[768,768]{1,0:T(8,128)(2,1)S(1)}, bf16[768,768]{1,0:T(8,128)(2,1)}, u32[]{:S(2)}) copy-start(bf16[768,768]{1,0:T(8,128)(2,1)} %param.7) | copy-start | bytes 3538948
  169.9 27.6 %copy-start.9 = (bf16[128,768]{1,0:T(8,128)(2,1)S(1)}, bf16[128,768]{1,0:T(8,128)(2,1)}, u32[]{:S(2)}) copy-start(bf16[128,768]{1,0:T(8,128)(2,1)} %copy-done.8) | copy-start | bytes 589828
  190.6 10.1 %collective-permute-start.29 = (bf16[16,56,768]{2,1,0:T(8,128)(2,1)S(1)}, bf16[16,56,768]{2,1,0:T(8,128)(2,1)S(1)}, u32[]{:S(2)}, u32[]{:S(2)}) collective-permute-start(bf16[16,56,768]{2,1,0:T(8,128)(2,1)S(1)} %all_to_all.20.mine), channel_id=1, source_target_pairs={{0,1},{1,0},{2,3},{3,2},{4,5},{5,4},{6,7},{7,6},{8,9},{9,8},{10,11... | collective-permute-start | bytes 4128776 | tf_op jit(solution)/shard_map/ppermute | solution.py:28

commit v5 on v4

--- a/solution.py
+++ b/solution.py
@@ -1,3 +1,5 @@
+import math
+
 import jax
 import jax.numpy as jnp
 from jax import lax
@@ -12,8 +14,7 @@
 YZ = ("y", "z")
 ALL = ("xh", "y", "xl", "z", "c")
 TILE = 512
-LTILE = 512
-GRADS_MIB = 40
+LOG2 = sharpness_factor * math.log2(math.e)
 f32 = jnp.float32
 bf16 = jnp.bfloat16
 
@@ -67,9 +68,13 @@
 
 def row_totals(part):
     n = part.shape[1] // 2
-    other = from_core(part)
-    part = part + jnp.concatenate([other[:, n:], other[:, :n]], axis=1)
-    part = part + lax.ppermute(part, "xl", [(0, 1), (1, 0)])
+    flipped = jnp.concatenate([part[:, n:], part[:, :n]], axis=1)
+
+    def from_pair(v, xl, c):
+        pairs = [(i, i ^ (2 * xl + c)) for i in range(4)]
+        return lax.ppermute(v, ("xl", "c"), pairs)
+
+    part = part + from_pair(part, 1, 0) + from_pair(flipped, 1, 1) + from_pair(flipped, 0, 1)
     return part + sum(lax.ppermute(part, "z", [(i, (i - k) % 4) for i in range(4)]) for k in (1, 3, 2))
 
 
@@ -97,42 +102,35 @@
 def logits_kernel(mine, other, texts, logits, row_sum, column_sum):
     i = pl.program_id(0)
     images = jnp.where(i < pl.num_programs(0) // 2, mine[...], other[...])
-    value = sharpness_factor * lax.dot_general(
+    value = lax.dot_general(
         images, texts[...], (((1,), (1,)), ((), ())), preferred_element_type=f32
     )
     logits[...] = value
-    e = jnp.exp(value - sharpness_factor)
+    e = jnp.exp2(value * LOG2 - LOG2)
     by_lane = e[:, :128]
     for k in range(1, e.shape[1] // 128):
         by_lane = by_lane + e[:, k * 128 : (k + 1) * 128]
     row_sum[...] = jnp.sum(by_lane.T, axis=0, keepdims=True)
-    by_column = jnp.sum(e, axis=0, keepdims=True)
-
-    @pl.when(i == 0)
-    def _():
-        column_sum[...] = by_column
-
-    @pl.when(i > 0)
-    def _():
-        column_sum[...] += by_column
+    column_sum[...] = jnp.where(i == 0, 0.0, column_sum[...]) + jnp.sum(e, axis=0, keepdims=True)
 
 
 def block_logits(mine, other, texts):
-    n, width = mine.shape
-    half = n // LTILE
-    n = 2 * n
+    rows, width = mine.shape
+    n = 2 * rows
     m = texts.shape[0]
+    steps = n // TILE
+    half = steps // 2
     return pl.pallas_call(
         logits_kernel,
-        grid=(n // LTILE,),
+        grid=(steps,),
         in_specs=[
-            pl.BlockSpec((LTILE, width), lambda i: (jnp.minimum(i, half - 1), 0)),
-            pl.BlockSpec((LTILE, width), lambda i: (jnp.maximum(i - half, 0), 0)),
+            pl.BlockSpec((TILE, width), lambda i: (jnp.minimum(i, half - 1), 0)),
+            pl.BlockSpec((TILE, width), lambda i: (jnp.maximum(i - half, 0), 0)),
             pl.BlockSpec((m, width), lambda i: (0, 0)),
         ],
         out_specs=[
-            pl.BlockSpec((LTILE, m), lambda i: (i, 0)),
-            pl.BlockSpec((1, LTILE), lambda i: (0, i)),
+            pl.BlockSpec((TILE, m), lambda i: (i, 0)),
+            pl.BlockSpec((1, TILE), lambda i: (0, i)),
             pl.BlockSpec((1, m), lambda i: (0, 0)),
         ],
         out_shape=[
@@ -149,46 +147,38 @@
 
 
 def grads_kernel(
-    place, logits, row_total, column_total, mine, other, texts, own, part_mine, part_other, text_part, total
+    place, logits, row_total, column_total, mine, other, texts, own, part_mine, part_other, text_part, total, last
 ):
     i = pl.program_id(0)
-    half = pl.num_programs(0) // 2
-    images = jnp.where(i < half, mine[...], other[...])
-    row_lse = jnp.log(row_total[...]) + sharpness_factor
-    column_lse = jnp.log(column_total[...]) + sharpness_factor
-    value = logits[...]
+    half = (pl.num_programs(0) - 1) // 2
+    before = jnp.where(i == 0, jnp.zeros((), bf16), last[...])
+    images = jnp.where(i <= half, mine[...], other[...])
+    part = jnp.dot(before, texts[...], preferred_element_type=f32)
+    share = lax.dot_general(
+        before, images, (((0,), (0,)), ((), ())), preferred_element_type=f32
+    )
+    shift = LOG2 - math.log2(0.5 * sharpness_factor)
+    value = logits[...] * LOG2
     rows, columns = value.shape
+    row_lse = jnp.log2(row_total[...]) + shift
+    column_lse = jnp.log2(column_total[...]) + shift
     by_row = jnp.broadcast_to(row_lse, (128, rows)).T
     by_row = jnp.concatenate([by_row] * (columns // 128), axis=1)
-    weights = (
-        0.5 * sharpness_factor * (jnp.exp(value - by_row) + jnp.exp(value - column_lse))
-    ).astype(bf16)
-    part = jnp.dot(weights, texts[...], preferred_element_type=f32)
+    last[...] = (jnp.exp2(value - by_row) + jnp.exp2(value - column_lse)).astype(bf16)
+    total[...] = jnp.where(i == 0, 0.0, total[...]) + share
     per = rows // 128
 
-    @pl.when(i < half)
+    @pl.when(i <= half)
     def _():
         for k in range(per):
-            here = jnp.where(place[0] == i * per + k, sharpness_factor, 0.0)
+            here = jnp.where(place[0] == (i - 1) * per + k, sharpness_factor, 0.0)
             part_mine[k * 128 : (k + 1) * 128, :] = (
                 part[k * 128 : (k + 1) * 128] - here * texts[:128, :].astype(f32)
             ).astype(bf16)
 
-    @pl.when(i >= half)
+    @pl.when(i > half)
     def _():
         part_other[...] = part.astype(bf16)
-
-    share = lax.dot_general(
-        weights, images, (((0,), (0,)), ((), ())), preferred_element_type=f32
-    )
-
-    @pl.when(i == 0)
-    def _():
-        total[...] = share
-
-    @pl.when(i > 0)
-    def _():
-        total[...] += share
 
     @pl.when(i == pl.num_programs(0) - 1)
     def _():
@@ -199,30 +189,35 @@
 def block_grads(place, logits, row_total, column_total, mine, other, texts, own):
     n, m = logits.shape
     width = texts.shape[1]
-    half = n // TILE // 2
-    first = pl.BlockSpec((TILE, width), lambda i: (jnp.minimum(i, half - 1), 0))
-    second = pl.BlockSpec((TILE, width), lambda i: (jnp.maximum(i - half, 0), 0))
+    steps = n // TILE
+    half = steps // 2
+    first = pl.BlockSpec((TILE, width), lambda i: (jnp.clip(i - 1, 0, half - 1), 0))
+    second = pl.BlockSpec((TILE, width), lambda i: (jnp.clip(i - 1 - half, 0, half - 1), 0))
     return pl.pallas_call(
         grads_kernel,
-        grid=(n // TILE,),
+        grid=(steps + 1,),
         in_specs=[
             pl.BlockSpec(memory_space=pltpu.SMEM),
-            pl.BlockSpec((TILE, m), lambda i: (i, 0)),
-            pl.BlockSpec((1, TILE), lambda i: (0, i)),
+            pl.BlockSpec((TILE, m), lambda i: (jnp.minimum(i, steps - 1), 0)),
+            pl.BlockSpec((1, TILE), lambda i: (0, jnp.minimum(i, steps - 1))),
             pl.BlockSpec((1, m), lambda i: (0, 0)),
             first,
             second,
             pl.BlockSpec((m, width), lambda i: (0, 0)),
             pl.BlockSpec(own.shape, lambda i: (0, 0)),
         ],
-        out_specs=[first, second, pl.BlockSpec((m, width), lambda i: (0, 0))],
+        out_specs=[
+            first,
+            second,
+            pl.BlockSpec((m, width), lambda i: (0, 0)),
+        ],
         out_shape=[
             jax.ShapeDtypeStruct((n // 2, width), bf16),
             jax.ShapeDtypeStruct((n // 2, width), bf16),
             jax.ShapeDtypeStruct((m, width), bf16),
         ],
-        scratch_shapes=[pltpu.VMEM((m, width), f32)],
-        compiler_params=params(GRADS_MIB),
+        scratch_shapes=[pltpu.VMEM((m, width), f32), pltpu.VMEM((TILE, m), bf16)],
+        compiler_params=params(),
         cost_estimate=pl.CostEstimate(
             flops=4 * n * m * width,
             bytes_accessed=4 * n * m + 4 * (n + m) * width,

time: 205 us -> 203 us (level)
  waiting for transfers between devices: 53.6 us -> 50.9 us
    ppermute x11, waiting for transfers between devices: 14.2 us -> 11.8 us  [from_y(): return lax.ppermute(v, 'y', [(i, (i - k) % 4) for i in range(4)])]
    ppermute x9 -> x8, starting transfers between devices: 19.5 us -> 18.5 us  [from_core(): return lax.ppermute(v, 'c', [(0, 1), (1, 0)])]
    ppermute x9 -> x8, waiting for transfers between devices: 4.92 us -> 4.75 us  [from_core(): return lax.ppermute(v, 'c', [(0, 1), (1, 0)])]
  transfers between devices with their start and end apart: 33 -> 34, of which waited for: 18 -> 17; matrix products, arithmetic and copies ran while one was open for 11% -> 11% of each run, Pallas kernels for 0% -> 0%
where the time goes in v5:
time: 203 us; the launch traced here: 202 us
  starting transfers between devices  65.9 us (32%)
  waiting for transfers between devices  50.9 us (25%)
  Pallas kernels  25.6 us (13%)
  blocking collectives  20.6 us (10%)
  other arithmetic  14.5 us (7%)
  local copies, waits for them, and re-layouts  10.7 us (5%)
  matrix products  7.19 us (4%)
  between operations  6.62 us (3%)
    all_to_all x1, waiting for transfers between devices, reduce_weights(): got = plus(*lax.all_to_all(sent, YZ, 0, 0))  22.1 us
    all_to_all x1, blocking collectives, spread(): return lax.all_to_all(jnp.broadcast_to(v[None], (n,) + v.shape), axes, 0, 0)  20.6 us
    ppermute x8, starting transfers between devices, from_core(): return lax.ppermute(v, 'c', [(0, 1), (1, 0)])  18.5 us
    pallas_call x1, Pallas kernels, block_grads(): pl.pallas_call(grads_kernel, grid=(steps + 1,), in_specs=[pl.BlockSpec(me...  14.7 us
    ppermute x11, starting transfers between devices, from_y(): return lax.ppermute(v, 'y', [(i, (i - k) % 4) for i in range(4)])  13.4 us
    ppermute x11, waiting for transfers between devices, from_y(): return lax.ppermute(v, 'y', [(i, (i - k) % 4) for i in range(4)])  11.8 us
    pallas_call x1, Pallas kernels, block_logits(): pl.pallas_call(logits_kernel, grid=(steps,), in_specs=[pl.BlockSpec((TILE...  8.29 us
    ppermute x3, starting transfers between devices, from_mirror(): return lax.ppermute(v, X, [(i, 3 - i) for i in range(4)])  7.51 us
  transfers between devices with their start and end apart: 34, of which 17 were waited for; matrix products, arithmetic and copies ran while one was open for 11% of the time, Pallas kernels for 0%

profile of v5, /device:TPU:1, one launch (start us, length us, event | category | flops | bytes accessed | tf_op | source)
XLA Modules:
  0.0 202.1 jit_solution(6197573227832295167)
XLA Ops:
  0.7 1.4 copy-done
  2.0 1.5 multiply_reduce_fusion.3
  4.3 0.7 multiply_reduce_fusion
  5.1 3.3 %collective-permute-start = (bf16[128,768]{1,0:T(8,128)(2,1)S(1)}, bf16[128,768]{1,0:T(8,128)(2,1)}, u32[]{:S(2)}, u32[]{:S(2)}) collective-permute-start(bf16[128,768]{1,0:T(8,128)(2,1)S(1)} %get-tuple-element.45), channel_id=1, source_target_pairs={{0,72},{8,64},{64,8},{72,0},{1,73},{9,65},{65,9},{73,1},{2,74},{10... | collective-permute-start | bytes 589832 | tf_op jit(solution)/shard_map/ppermute | solution.py:33
  8.4 1.2 broadcast_in_dim.55
  9.6 5.0 %all-to-all-start = ((bf16[8,128,768]{2,1,0:T(8,128)(2,1)}), bf16[8,128,768]{2,1,0:T(8,128)(2,1)S(1)}, u32[]{:S(2)}, u32[]{:S(2)}) async-start(bf16[8,128,768]{2,1,0:T(8,128)(2,1)} %broadcast_in_dim.55), calls=%async_computation | async-start | bytes 3145728 | tf_op jit(solution)/shard_map/all_to_all | solution.py:49
  14.7 1.0 pad_maximum_fusion.1
  15.6 2.8 %collective-permute-start.1 = (bf16[256,768]{1,0:T(8,128)(2,1)S(1)}, bf16[256,768]{1,0:T(8,128)(2,1)S(1)}, u32[]{:S(2)}, u32[]{:S(2)}) collective-permute-start(bf16[256,768]{1,0:T(8,128)(2,1)S(1)} %pad_maximum_fusion.1), channel_id=1, source_target_pairs={{0,48},{16,0},{32,16},{48,32},{1,49},{17,1},{33,17},{49,33},{2,50}... | collective-permute-start | bytes 1179656 | tf_op jit(solution)/shard_map/ppermute | solution.py:41
  18.5 1.0 constant_dynamic-slice_fusion.4
  19.4 1.6 collective-permute-start.5
  21.0 1.0 constant_dynamic-slice_fusion.2
  22.1 0.8 constant_dynamic-update-slice_fusion.4
  24.1 1.5 collective-permute-done.1
  25.6 3.5 %collective-permute-start.2 = (bf16[128,768]{1,0:T(8,128)(2,1)S(1)}, bf16[128,768]{1,0:T(8,128)(2,1)S(1)}, u32[]{:S(2)}, u32[]{:S(2)}) collective-permute-start(bf16[128,768]{1,0:T(8,128)(2,1)S(1)} %slice.122), channel_id=1, source_target_pairs={{0,48},{16,0},{32,16},{48,32},{1,49},{17,1},{33,17},{49,33},{2,50}... | collective-permute-start | bytes 589832 | tf_op jit(solution)/shard_map/ppermute | solution.py:41
  29.1 0.7 pad_maximum_fusion.4
  29.9 0.8 constant_dynamic-update-slice_fusion.3
  30.7 1.0 collective-permute-done.2
  32.4 3.2 %collective-permute-done.4 = bf16[128,768]{1,0:T(8,128)(2,1)S(1)} collective-permute-done((bf16[128,768]{1,0:T(8,128)(2,1)S(1)}, bf16[128,768]{1,0:T(8,128)(2,1)S(1)}, u32[]{:S(2)}, u32[]{:S(2)}) %collective-permute-start.4) | collective-permute-done | bytes 196640 | tf_op jit(solution)/shard_map/ppermute | solution.py:41
  36.4 0.8 constant_dynamic-update-slice_fusion.texts
  37.1 3.6 %collective-permute-start.7 = (bf16[1024,768]{1,0:T(8,128)(2,1)S(1)}, bf16[1024,768]{1,0:T(8,128)(2,1)S(1)}, u32[]{:S(2)}, u32[]{:S(2)}) collective-permute-start(bf16[1024,768]{1,0:T(8,128)(2,1)S(1)} %bitcast.39), channel_id=1, source_target_pairs={{0,1},{1,0},{2,3},{3,2},{4,5},{5,4},{6,7},{7,6},{8,9},{9,8},{10,11... | collective-permute-start | bytes 4718600 | tf_op jit(solution)/shard_map/ppermute | solution.py:29
  40.7 3.0 %collective-permute-done.7.other = bf16[1024,768]{1,0:T(8,128)(2,1)S(1)} collective-permute-done((bf16[1024,768]{1,0:T(8,128)(2,1)S(1)}, bf16[1024,768]{1,0:T(8,128)(2,1)S(1)}, u32[]{:S(2)}, u32[]{:S(2)}) %collective-permute-start.7) | collective-permute-done | bytes 1572896 | tf_op jit(solution)/shard_map/ppermute | solution.py:29
  43.8 1.1 copy-done.17
  44.9 8.3 %block_logits.1 = (f32[2048,1024]{1,0:T(8,128)}, f32[1,2048]{1,0:T(1,128)S(1)}, f32[1,1024]{1,0:T(1,128)S(1)}) custom-call(bf16[1024,768]{1,0:T(8,128)(2,1)S(1)} %bitcast.40, bf16[1024,768]{1,0:T(8,128)(2,1)} %copy-done.17, bf16[1024,768]{1,0:T(8,128)(2,1)} %constant_dynamic-update-slice_fusion.texts), custom_call_target="tpu_custom_call" | custom-call | flops 3221225472 | bytes 13107200 | tf_op jit(solution)/shard_map/block_logits/pallas_call | solution.py:123
  53.6 1.5 collective-permute-start.9
  55.2 1.4 collective-permute-start.14
  56.5 2.3 %collective-permute-done.14 = f32[4,2,128]{2,1,0:T(2,128)S(1)} collective-permute-done((f32[4,2,128]{2,1,0:T(2,128)S(1)}, f32[4,2,128]{2,1,0:T(2,128)S(1)}, u32[]{:S(2)}, u32[]{:S(2)}) %collective-permute-start.14) | collective-permute-done | bytes 4128 | tf_op jit(solution)/shard_map/ppermute | solution.py:33
  59.0 0.9 collective-permute-start.15
  60.5 2.7 %collective-permute-start.11 = (f32[1,2048]{1,0:T(1,128)S(1)}, f32[1,2048]{1,0:T(1,128)S(1)}, u32[]{:S(2)}, u32[]{:S(2)}) collective-permute-start(f32[1,2048]{1,0:T(1,128)S(1)} %add_add_fusion.2), channel_id=1, source_target_pairs={{0,6},{2,0},{4,2},{6,4},{1,7},{3,1},{5,3},{7,5},{8,14},{10,8},{12,... | collective-permute-start | bytes 24584 | tf_op jit(solution)/shard_map/ppermute | solution.py:78
  63.3 1.8 collective-permute-start.13
  65.1 1.9 collective-permute-done.12
  67.3 14.7 %block_grads.1 = (bf16[1024,768]{1,0:T(8,128)(2,1)S(1)}, bf16[1024,768]{1,0:T(8,128)(2,1)S(1)}, bf16[1024,768]{1,0:T(8,128)(2,1)S(1)}) custom-call(s32[1]{0:T(128)} %bitcast.1.place, f32[2048,1024]{1,0:T(8,128)} %get-tuple-element.28.logits, f32[1,2048]{1,0:T(1,128)S(1)} %add_add_fusion.1.row_total, f32[1,1024]{1,0:T(1,128)S(1)} %bitcast.42, ...), custom_call_target="tpu_custom_call" | custom-call | flops 6442450944 | bytes 17825792 | tf_op jit(solution)/shard_map/block_grads/pallas_call | solution.py:196
  82.0 3.9 %collective-permute-start.18 = (bf16[1024,768]{1,0:T(8,128)(2,1)S(1)}, bf16[1024,768]{1,0:T(8,128)(2,1)S(1)}, u32[]{:S(2)}, u32[]{:S(2)}) collective-permute-start(bf16[1024,768]{1,0:T(8,128)(2,1)S(1)} %get-tuple-element.32), channel_id=1, source_target_pairs={{0,1},{1,0},{2,3},{3,2},{4,5},{5,4},{6,7},{7,6},{8,9},{9,8},{10,11... | collective-permute-start | bytes 4718600 | tf_op jit(solution)/shard_map/ppermute | solution.py:29
  85.9 1.2 collective-permute-start.20
  87.1 1.6 collective-permute-start.21
  88.7 5.0 %collective-permute-done.20 = bf16[128,768]{1,0:T(8,128)(2,1)S(1)} collective-permute-done((bf16[128,768]{1,0:T(8,128)(2,1)S(1)}, bf16[128,768]{1,0:T(8,128)(2,1)S(1)}, u32[]{:S(2)}, u32[]{:S(2)}) %collective-permute-start.20) | collective-permute-done | bytes 196640 | tf_op jit(solution)/shard_map/ppermute | solution.py:41
  94.0 0.8 pad_maximum_fusion.3
  94.8 1.5 add_convert_fusion
  96.3 4.2 %all-to-all-start.1 = ((bf16[8,128,768]{2,1,0:T(8,128)(2,1)}), bf16[8,128,768]{2,1,0:T(8,128)(2,1)S(1)}, u32[]{:S(2)}, u32[]{:S(2)}) async-start(bf16[8,128,768]{2,1,0:T(8,128)(2,1)} %bitcast.46), calls=%async_computation.1 | async-start | bytes 3145728 | tf_op jit(solution)/shard_map/all_to_all | solution.py:343
  100.5 0.8 pad_maximum_fusion.2
  101.3 1.1 collective-permute-start.22
  102.5 1.5 collective-permute-start.23
  104.5 1.3 fusion.17
  105.8 1.6 collective-permute-start.26
  107.4 1.0 collective-permute-done.26
  111.6 0.7 collective-permute-done.22
  112.4 1.4 convert_add_fusion
  113.8 2.8 %collective-permute-start.24 = (bf16[128,768]{1,0:T(8,128)(2,1)S(1)}, bf16[128,768]{1,0:T(8,128)(2,1)S(1)}, u32[]{:S(2)}, u32[]{:S(2)}) collective-permute-start(bf16[128,768]{1,0:T(8,128)(2,1)S(1)} %slice.165), channel_id=1, source_target_pairs={{0,72},{8,64},{64,8},{72,0},{1,73},{9,65},{65,9},{73,1},{2,74},{10... | collective-permute-start | bytes 589832 | tf_op jit(solution)/shard_map/ppermute | solution.py:33
  116.7 3.3 %collective-permute-done.24 = bf16[128,768]{1,0:T(8,128)(2,1)S(1)} collective-permute-done((bf16[128,768]{1,0:T(8,128)(2,1)S(1)}, bf16[128,768]{1,0:T(8,128)(2,1)S(1)}, u32[]{:S(2)}, u32[]{:S(2)}) %collective-permute-start.24) | collective-permute-done | bytes 196640 | tf_op jit(solution)/shard_map/ppermute | solution.py:33
  120.0 1.2 multiply_reduce_fusion.1
  121.2 0.8 divide_convert_fusion
  122.0 2.9 %collective-permute-start.25 = (bf16[128,768]{1,0:T(8,128)(2,1)}, bf16[128,768]{1,0:T(8,128)(2,1)}, u32[]{:S(2)}, u32[]{:S(2)}) collective-permute-start(bf16[128,768]{1,0:T(8,128)(2,1)} %divide_convert_fusion), channel_id=1, source_target_pairs={{0,1},{1,0},{2,3},{3,2},{4,5},{5,4},{6,7},{7,6},{8,9},{9,8},{10,11... | collective-permute-start | bytes 589832 | tf_op jit(solution)/shard_map/ppermute | solution.py:29
  124.9 1.0 fusion.6
  126.3 1.4 convolution_convert_fusion.1
  128.1 1.3 pad_maximum_fusion
  129.4 6.6 %all-to-all-start.2 = ((bf16[16,64,768]{2,1,0:T(8,128)(2,1)}), bf16[16,64,768]{2,1,0:T(8,128)(2,1)S(1)}, u32[]{:S(2)}, u32[]{:S(2)}) async-start(bf16[16,64,768]{2,1,0:T(8,128)(2,1)} %pad_maximum_fusion), calls=%async_computation.2 | async-start | bytes 3145728 | tf_op jit(solution)/shard_map/all_to_all | solution.py:307
  136.1 22.1 %all-to-all-done.2 = bf16[16,64,768]{2,1,0:T(8,128)(2,1)S(1)} async-done(((bf16[16,64,768]{2,1,0:T(8,128)(2,1)}), bf16[16,64,768]{2,1,0:T(8,128)(2,1)S(1)}, u32[]{:S(2)}, u32[]{:S(2)}) %all-to-all-start.2) | async-done | bytes 1572896 | tf_op jit(solution)/shard_map/all_to_all | solution.py:307
  158.7 3.0 %collective-permute-start.27 = (bf16[64,768]{1,0:T(8,128)(2,1)S(1)}, bf16[64,768]{1,0:T(8,128)(2,1)S(1)}, u32[]{:S(2)}, u32[]{:S(2)}) collective-permute-start(bf16[64,768]{1,0:T(8,128)(2,1)S(1)} %pad_maximum_fusion.6), channel_id=1, source_target_pairs={{0,72},{8,0},{64,8},{72,64},{1,73},{9,1},{65,9},{73,65},{2,74},{10... | collective-permute-start | bytes 294920 | tf_op jit(solution)/shard_map/ppermute | solution.py:37
  161.6 1.3 collective-permute-start.29
  163.3 4.1 %collective-permute-done.28 = bf16[64,768]{1,0:T(8,128)(2,1)S(1)} collective-permute-done((bf16[64,768]{1,0:T(8,128)(2,1)S(1)}, bf16[64,768]{1,0:T(8,128)(2,1)S(1)}, u32[]{:S(2)}, u32[]{:S(2)}) %collective-permute-start.28) | collective-permute-done | bytes 98336 | tf_op jit(solution)/shard_map/ppermute | solution.py:37
  167.6 20.6 %all_to_all.20.mine = bf16[16,56,768]{2,1,0:T(8,128)(2,1)S(1)} all-to-all(bf16[16,56,768]{2,1,0:T(8,128)(2,1)S(1)} %broadcast_in_dim.65), channel_id=1, replica_groups=mesh['xh'=2,'y'=4,'xl'=2,'z'=4,'c'=2] {'y','z'}, dimensions={0} | all-to-all | bytes 2752512 | tf_op jit(solution)/shard_map/all_to_all | solution.py:49
  188.2 4.7 %collective-permute-start.30 = (bf16[16,56,768]{2,1,0:T(8,128)(2,1)S(1)}, bf16[16,56,768]{2,1,0:T(8,128)(2,1)S(1)}, u32[]{:S(2)}, u32[]{:S(2)}) collective-permute-start(bf16[16,56,768]{2,1,0:T(8,128)(2,1)S(1)} %all_to_all.20.mine), channel_id=1, source_target_pairs={{0,1},{1,0},{2,3},{3,2},{4,5},{5,4},{6,7},{7,6},{8,9},{9,8},{10,11... | collective-permute-start | bytes 4128776 | tf_op jit(solution)/shard_map/ppermute | solution.py:29
  192.9 2.1 %convolution_convert_fusion.3 = bf16[128,768]{1,0:T(8,128)(2,1)} fusion(bf16[128,768]{1,0:T(8,128)(2,1)} %divide_convert_fusion, bf16[768,768]{1,0:T(8,128)(2,1)S(1)} %copy-done.7), kind=kOutput, calls=%fused_computation.5 | convolution fusion | flops 151093248 | bytes 1572864 | tf_op jit(solution)/shard_map/dot_general | solution.py:280
  195.1 1.3 convolution_convert_fusion.2
  198.3 2.7 %whole_terms.1 = (f32[1024,768]{1,0:T(8,128)}, f32[768,768]{1,0:T(8,128)}) custom-call(s32[1]{0:T(128)} %bitcast.12.core, bf16[16,56,768]{2,1,0:T(8,128)(2,1)S(1)} %all_to_all.20.mine, bf16[16,56,768]{2,1,0:T(8,128)(2,1)S(1)} %collective-permute-done.30.other), custom_call_target="tpu_custom_call" | custom-call | bytes 8257536 | tf_op jit(solution)/shard_map/whole_terms/pallas_call | solution.py:249
  (104 shorter events, 8.6 us)
Async XLA Ops:
  0.6 1.4 copy-start
  0.6 2.9 %copy-start.11 = (bf16[128,768]{1,0:T(8,128)(2,1)S(1)}, bf16[128,768]{1,0:T(8,128)(2,1)}, u32[]{:S(2)}) copy-start(bf16[128,768]{1,0:T(8,128)(2,1)} %param.5) | copy-start | bytes 589828
  2.0 1.5 copy-start.6
  3.6 0.8 copy-start.2
  4.0 1.1 copy-start.4
  4.0 5.6 %copy-start.13 = (f32[128]{0:T(128)}, f32[128]{0:T(128)S(1)}, u32[]{:S(2)}) copy-start(f32[128]{0:T(128)S(1)} %get-tuple-element.67) | copy-start | bytes 1540
  5.1 9.6 %collective-permute-start = (bf16[128,768]{1,0:T(8,128)(2,1)S(1)}, bf16[128,768]{1,0:T(8,128)(2,1)}, u32[]{:S(2)}, u32[]{:S(2)}) collective-permute-start(bf16[128,768]{1,0:T(8,128)(2,1)S(1)} %get-tuple-element.45), channel_id=1, source_target_pairs={{0,72},{8,64},{64,8},{72,0},{1,73},{9,65},{65,9},{73,1},{2,74},{10... | collective-permute-start | bytes 589832 | tf_op jit(solution)/shard_map/ppermute | solution.py:33
  9.6 27.5 %all-to-all-start = ((bf16[8,128,768]{2,1,0:T(8,128)(2,1)}), bf16[8,128,768]{2,1,0:T(8,128)(2,1)S(1)}, u32[]{:S(2)}, u32[]{:S(2)}) async-start(bf16[8,128,768]{2,1,0:T(8,128)(2,1)} %broadcast_in_dim.55), calls=%async_computation | async-start | bytes 3145728 | tf_op jit(solution)/shard_map/all_to_all | solution.py:49
  15.6 10.0 %collective-permute-start.1 = (bf16[256,768]{1,0:T(8,128)(2,1)S(1)}, bf16[256,768]{1,0:T(8,128)(2,1)S(1)}, u32[]{:S(2)}, u32[]{:S(2)}) collective-permute-start(bf16[256,768]{1,0:T(8,128)(2,1)S(1)} %pad_maximum_fusion.1), channel_id=1, source_target_pairs={{0,48},{16,0},{32,16},{48,32},{1,49},{17,1},{33,17},{49,33},{2,50}... | collective-permute-start | bytes 1179656 | tf_op jit(solution)/shard_map/ppermute | solution.py:41
  18.4 11.4 %collective-permute-start.3 = (bf16[256,768]{1,0:T(8,128)(2,1)S(1)}, bf16[256,768]{1,0:T(8,128)(2,1)S(1)}, u32[]{:S(2)}, u32[]{:S(2)}) collective-permute-start(bf16[256,768]{1,0:T(8,128)(2,1)S(1)} %pad_maximum_fusion.1), channel_id=1, source_target_pairs={{0,16},{16,32},{32,48},{48,0},{1,17},{17,33},{33,49},{49,1},{2,18}... | collective-permute-start | bytes 1179656 | tf_op jit(solution)/shard_map/ppermute | solution.py:41
  19.4 9.7 %collective-permute-start.5 = (bf16[128,512]{1,0:T(8,128)(2,1)S(1)}, bf16[128,512]{1,0:T(8,128)(2,1)S(1)}, u32[]{:S(2)}, u32[]{:S(2)}) collective-permute-start(bf16[128,512]{1,0:T(8,128)(2,1)S(1)} %get-tuple-element.53), channel_id=1, source_target_pairs={{0,1},{1,0},{2,3},{3,2},{4,5},{5,4},{6,7},{7,6},{8,9},{9,8},{10,11... | collective-permute-start | bytes 393224 | tf_op jit(solution)/shard_map/ppermute | solution.py:29
  22.0 1.4 collective-permute-start.6
  25.6 6.1 %collective-permute-start.2 = (bf16[128,768]{1,0:T(8,128)(2,1)S(1)}, bf16[128,768]{1,0:T(8,128)(2,1)S(1)}, u32[]{:S(2)}, u32[]{:S(2)}) collective-permute-start(bf16[128,768]{1,0:T(8,128)(2,1)S(1)} %slice.122), channel_id=1, source_target_pairs={{0,48},{16,0},{32,16},{48,32},{1,49},{17,1},{33,17},{49,33},{2,50}... | collective-permute-start | bytes 589832 | tf_op jit(solution)/shard_map/ppermute | solution.py:41
  29.9 5.8 %collective-permute-start.4 = (bf16[128,768]{1,0:T(8,128)(2,1)S(1)}, bf16[128,768]{1,0:T(8,128)(2,1)S(1)}, u32[]{:S(2)}, u32[]{:S(2)}) collective-permute-start(bf16[128,768]{1,0:T(8,128)(2,1)S(1)} %slice.123), channel_id=1, source_target_pairs={{0,16},{16,32},{32,48},{48,0},{1,17},{17,33},{33,49},{49,1},{2,18}... | collective-permute-start | bytes 589832 | tf_op jit(solution)/shard_map/ppermute | solution.py:41
  37.1 6.6 %collective-permute-start.7 = (bf16[1024,768]{1,0:T(8,128)(2,1)S(1)}, bf16[1024,768]{1,0:T(8,128)(2,1)S(1)}, u32[]{:S(2)}, u32[]{:S(2)}) collective-permute-start(bf16[1024,768]{1,0:T(8,128)(2,1)S(1)} %bitcast.39), channel_id=1, source_target_pairs={{0,1},{1,0},{2,3},{3,2},{4,5},{5,4},{6,7},{7,6},{8,9},{9,8},{10,11... | collective-permute-start | bytes 4718600 | tf_op jit(solution)/shard_map/ppermute | solution.py:29
  43.8 1.1 copy-start.17
  53.2 6.7 %collective-permute-start.10 = (f32[1,2048]{1,0:T(1,128)S(1)}, f32[1,2048]{1,0:T(1,128)S(1)}, u32[]{:S(2)}, u32[]{:S(2)}) collective-permute-start(f32[1,2048]{1,0:T(1,128)S(1)} %pad_maximum_fusion.7), channel_id=1, source_target_pairs={{0,1},{1,0},{8,9},{9,8},{2,3},{3,2},{10,11},{11,10},{4,5},{5,4},{1... | collective-permute-start | bytes 24584 | tf_op jit(solution)/shard_map/ppermute | solution.py:75
  53.6 6.9 %collective-permute-start.9 = (f32[1,2048]{1,0:T(1,128)S(1)}, f32[1,2048]{1,0:T(1,128)S(1)}, u32[]{:S(2)}, u32[]{:S(2)}) collective-permute-start(f32[1,2048]{1,0:T(1,128)S(1)} %pad_maximum_fusion.7), channel_id=1, source_target_pairs={{0,9},{1,8},{8,1},{9,0},{2,11},{3,10},{10,3},{11,2},{4,13},{5,12},... | collective-permute-start | bytes 24584 | tf_op jit(solution)/shard_map/ppermute | solution.py:75
  55.1 5.4 %collective-permute-start.8 = (f32[1,2048]{1,0:T(1,128)S(1)}, f32[1,2048]{1,0:T(1,128)S(1)}, u32[]{:S(2)}, u32[]{:S(2)}) collective-permute-start(f32[1,2048]{1,0:T(1,128)S(1)} %get-tuple-element.29), channel_id=1, source_target_pairs={{0,8},{1,9},{8,0},{9,1},{2,10},{3,11},{10,2},{11,3},{4,12},{5,13},... | collective-permute-start | bytes 24584 | tf_op jit(solution)/shard_map/ppermute | solution.py:75
  55.2 3.7 %collective-permute-start.14 = (f32[4,2,128]{2,1,0:T(2,128)S(1)}, f32[4,2,128]{2,1,0:T(2,128)S(1)}, u32[]{:S(2)}, u32[]{:S(2)}) collective-permute-start(f32[4,2,128]{2,1,0:T(2,128)S(1)} %bitcast.44), channel_id=1, source_target_pairs={{0,72},{8,64},{64,8},{72,0},{1,73},{9,65},{65,9},{73,1},{2,74},{10... | collective-permute-start | bytes 12296 | tf_op jit(solution)/shard_map/ppermute | solution.py:33
  58.9 6.2 %collective-permute-start.17 = (f32[4,2,128]{2,1,0:T(2,128)S(1)}, f32[4,2,128]{2,1,0:T(2,128)S(1)}, u32[]{:S(2)}, u32[]{:S(2)}) collective-permute-start(f32[4,2,128]{2,1,0:T(2,128)S(1)} %add.199), channel_id=1, source_target_pairs={{0,32},{16,48},{32,0},{48,16},{1,33},{17,49},{33,1},{49,17},{2,34}... | collective-permute-start | bytes 12296 | tf_op jit(solution)/shard_map/ppermute | solution.py:41
  59.0 4.3 %collective-permute-start.15 = (f32[4,2,128]{2,1,0:T(2,128)S(1)}, f32[4,2,128]{2,1,0:T(2,128)S(1)}, u32[]{:S(2)}, u32[]{:S(2)}) collective-permute-start(f32[4,2,128]{2,1,0:T(2,128)S(1)} %add.199), channel_id=1, source_target_pairs={{0,48},{16,0},{32,16},{48,32},{1,49},{17,1},{33,17},{49,33},{2,50}... | collective-permute-start | bytes 12296 | tf_op jit(solution)/shard_map/ppermute | solution.py:41
  59.9 5.2 %collective-permute-start.16 = (f32[4,2,128]{2,1,0:T(2,128)S(1)}, f32[4,2,128]{2,1,0:T(2,128)S(1)}, u32[]{:S(2)}, u32[]{:S(2)}) collective-permute-start(f32[4,2,128]{2,1,0:T(2,128)S(1)} %add.199), channel_id=1, source_target_pairs={{0,16},{16,32},{32,48},{48,0},{1,17},{17,33},{33,49},{49,1},{2,18}... | collective-permute-start | bytes 12296 | tf_op jit(solution)/shard_map/ppermute | solution.py:41
  60.5 4.6 %collective-permute-start.11 = (f32[1,2048]{1,0:T(1,128)S(1)}, f32[1,2048]{1,0:T(1,128)S(1)}, u32[]{:S(2)}, u32[]{:S(2)}) collective-permute-start(f32[1,2048]{1,0:T(1,128)S(1)} %add_add_fusion.2), channel_id=1, source_target_pairs={{0,6},{2,0},{4,2},{6,4},{1,7},{3,1},{5,3},{7,5},{8,14},{10,8},{12,... | collective-permute-start | bytes 24584 | tf_op jit(solution)/shard_map/ppermute | solution.py:78
  63.3 3.7 %collective-permute-start.12 = (f32[1,2048]{1,0:T(1,128)S(1)}, f32[1,2048]{1,0:T(1,128)S(1)}, u32[]{:S(2)}, u32[]{:S(2)}) collective-permute-start(f32[1,2048]{1,0:T(1,128)S(1)} %add_add_fusion.2), channel_id=1, source_target_pairs={{0,2},{2,4},{4,6},{6,0},{1,3},{3,5},{5,7},{7,1},{8,10},{10,12},{12... | collective-permute-start | bytes 24584 | tf_op jit(solution)/shard_map/ppermute | solution.py:78
  63.3 4.0 %collective-permute-start.13 = (f32[1,2048]{1,0:T(1,128)S(1)}, f32[1,2048]{1,0:T(1,128)S(1)}, u32[]{:S(2)}, u32[]{:S(2)}) collective-permute-start(f32[1,2048]{1,0:T(1,128)S(1)} %add_add_fusion.2), channel_id=1, source_target_pairs={{0,4},{2,6},{4,0},{6,2},{1,5},{3,7},{5,1},{7,3},{8,12},{10,14},{12... | collective-permute-start | bytes 24584 | tf_op jit(solution)/shard_map/ppermute | solution.py:78
  82.0 12.8 %copy-start.1 = (bf16[1024,768]{1,0:T(8,128)(2,1)}, bf16[1024,768]{1,0:T(8,128)(2,1)S(1)}, u32[]{:S(2)}) copy-start(bf16[1024,768]{1,0:T(8,128)(2,1)S(1)} %get-tuple-element.34) | copy-start | bytes 4718596
  82.0 12.8 %collective-permute-start.18 = (bf16[1024,768]{1,0:T(8,128)(2,1)S(1)}, bf16[1024,768]{1,0:T(8,128)(2,1)S(1)}, u32[]{:S(2)}, u32[]{:S(2)}) collective-permute-start(bf16[1024,768]{1,0:T(8,128)(2,1)S(1)} %get-tuple-element.32), channel_id=1, source_target_pairs={{0,1},{1,0},{2,3},{3,2},{4,5},{5,4},{6,7},{7,6},{8,9},{9,8},{10,11... | collective-permute-start | bytes 4718600 | tf_op jit(solution)/shard_map/ppermute | solution.py:29
  85.9 7.8 %collective-permute-start.20 = (bf16[128,768]{1,0:T(8,128)(2,1)S(1)}, bf16[128,768]{1,0:T(8,128)(2,1)S(1)}, u32[]{:S(2)}, u32[]{:S(2)}) collective-permute-start(bf16[128,768]{1,0:T(8,128)(2,1)S(1)} %get-tuple-element.49), channel_id=1, source_target_pairs={{0,16},{16,32},{32,48},{48,0},{1,17},{17,33},{33,49},{49,1},{2,18}... | collective-permute-start | bytes 589832 | tf_op jit(solution)/shard_map/ppermute | solution.py:41
  87.1 6.8 %collective-permute-start.21 = (bf16[128,768]{1,0:T(8,128)(2,1)S(1)}, bf16[128,768]{1,0:T(8,128)(2,1)S(1)}, u32[]{:S(2)}, u32[]{:S(2)}) collective-permute-start(bf16[128,768]{1,0:T(8,128)(2,1)S(1)} %get-tuple-element.47), channel_id=1, source_target_pairs={{0,48},{16,0},{32,16},{48,32},{1,49},{17,1},{33,17},{49,33},{2,50}... | collective-permute-start | bytes 589832 | tf_op jit(solution)/shard_map/ppermute | solution.py:41
  96.3 28.6 %all-to-all-start.1 = ((bf16[8,128,768]{2,1,0:T(8,128)(2,1)}), bf16[8,128,768]{2,1,0:T(8,128)(2,1)S(1)}, u32[]{:S(2)}, u32[]{:S(2)}) async-start(bf16[8,128,768]{2,1,0:T(8,128)(2,1)} %bitcast.46), calls=%async_computation.1 | async-start | bytes 3145728 | tf_op jit(solution)/shard_map/all_to_all | solution.py:343
  101.3 11.1 %collective-permute-start.22 = (bf16[256,768]{1,0:T(8,128)(2,1)}, bf16[256,768]{1,0:T(8,128)(2,1)}, u32[]{:S(2)}, u32[]{:S(2)}) collective-permute-start(bf16[256,768]{1,0:T(8,128)(2,1)} %pad_maximum_fusion.2), channel_id=1, source_target_pairs={{0,16},{16,32},{32,48},{48,0},{1,17},{17,33},{33,49},{49,1},{2,18}... | collective-permute-start | bytes 1179656 | tf_op jit(solution)/shard_map/ppermute | solution.py:41
  102.5 9.9 %collective-permute-start.23 = (bf16[256,768]{1,0:T(8,128)(2,1)}, bf16[256,768]{1,0:T(8,128)(2,1)}, u32[]{:S(2)}, u32[]{:S(2)}) collective-permute-start(bf16[256,768]{1,0:T(8,128)(2,1)} %pad_maximum_fusion.3), channel_id=1, source_target_pairs={{0,48},{16,0},{32,16},{48,32},{1,49},{17,1},{33,17},{49,33},{2,50}... | collective-permute-start | bytes 1179656 | tf_op jit(solution)/shard_map/ppermute | solution.py:41
  105.8 2.7 %collective-permute-start.26 = (f32[]{:T(128)}, f32[]{:T(128)}, u32[]{:S(2)}, u32[]{:S(2)}) collective-permute-start(f32[]{:T(128)} %fusion.17), channel_id=1, source_target_pairs={{0,1},{1,0},{2,3},{3,2},{4,5},{5,4},{6,7},{7,6},{8,9},{9,8},{10,11... | collective-permute-start | bytes 20 | tf_op jit(solution)/shard_map/ppermute | solution.py:29
  111.6 5.0 %copy-start.15 = (pred[768]{0:T(1024)(128)(4,1)S(1)}, pred[768]{0:T(1024)(128)(4,1)}, u32[]{:S(2)}) copy-start(pred[768]{0:T(1024)(128)(4,1)} %iota_compare_fusion.1) | copy-start | bytes 2308
  111.6 9.6 %copy-start.5 = (f32[128,768]{1,0:T(8,128)S(1)}, f32[128,768]{1,0:T(8,128)}, u32[]{:S(2)}) copy-start(f32[128,768]{1,0:T(8,128)} %copy-done.4) | copy-start | bytes 1179652
  113.8 11.1 %copy-start.3 = (f32[128,768]{1,0:T(8,128)S(1)}, f32[128,768]{1,0:T(8,128)}, u32[]{:S(2)}) copy-start(f32[128,768]{1,0:T(8,128)} %copy-done.2) | copy-start | bytes 1179652
  113.8 6.2 %collective-permute-start.24 = (bf16[128,768]{1,0:T(8,128)(2,1)S(1)}, bf16[128,768]{1,0:T(8,128)(2,1)S(1)}, u32[]{:S(2)}, u32[]{:S(2)}) collective-permute-start(bf16[128,768]{1,0:T(8,128)(2,1)S(1)} %slice.165), channel_id=1, source_target_pairs={{0,72},{8,64},{64,8},{72,0},{1,73},{9,65},{65,9},{73,1},{2,74},{10... | collective-permute-start | bytes 589832 | tf_op jit(solution)/shard_map/ppermute | solution.py:33
  122.0 3.8 %copy-start.14 = (f32[128]{0:T(128)S(1)}, f32[128]{0:T(128)}, u32[]{:S(2)}) copy-start(f32[128]{0:T(128)} %copy-done.13) | copy-start | bytes 1540
  122.0 4.3 %collective-permute-start.25 = (bf16[128,768]{1,0:T(8,128)(2,1)}, bf16[128,768]{1,0:T(8,128)(2,1)}, u32[]{:S(2)}, u32[]{:S(2)}) collective-permute-start(bf16[128,768]{1,0:T(8,128)(2,1)} %divide_convert_fusion), channel_id=1, source_target_pairs={{0,1},{1,0},{2,3},{3,2},{4,5},{5,4},{6,7},{7,6},{8,9},{9,8},{10,11... | collective-permute-start | bytes 589832 | tf_op jit(solution)/shard_map/ppermute | solution.py:29
  124.9 1.4 copy-start.12
  125.8 1.9 copy-start.10
  126.0 1.7 copy-start.8
  126.0 1.7 collective-permute-start.19
  129.4 28.8 %all-to-all-start.2 = ((bf16[16,64,768]{2,1,0:T(8,128)(2,1)}), bf16[16,64,768]{2,1,0:T(8,128)(2,1)S(1)}, u32[]{:S(2)}, u32[]{:S(2)}) async-start(bf16[16,64,768]{2,1,0:T(8,128)(2,1)} %pad_maximum_fusion), calls=%async_computation.2 | async-start | bytes 3145728 | tf_op jit(solution)/shard_map/all_to_all | solution.py:307
  136.1 22.5 %copy-start.16 = (pred[768]{0:T(1024)(128)(4,1)S(1)}, pred[768]{0:T(1024)(128)(4,1)}, u32[]{:S(2)}) copy-start(pred[768]{0:T(1024)(128)(4,1)} %iota_compare_fusion.1) | copy-start | bytes 2308
  158.7 4.6 %collective-permute-start.27 = (bf16[64,768]{1,0:T(8,128)(2,1)S(1)}, bf16[64,768]{1,0:T(8,128)(2,1)S(1)}, u32[]{:S(2)}, u32[]{:S(2)}) collective-permute-start(bf16[64,768]{1,0:T(8,128)(2,1)S(1)} %pad_maximum_fusion.6), channel_id=1, source_target_pairs={{0,72},{8,0},{64,8},{72,64},{1,73},{9,1},{65,9},{73,65},{2,74},{10... | collective-permute-start | bytes 294920 | tf_op jit(solution)/shard_map/ppermute | solution.py:37
  161.6 5.7 %collective-permute-start.28 = (bf16[64,768]{1,0:T(8,128)(2,1)S(1)}, bf16[64,768]{1,0:T(8,128)(2,1)S(1)}, u32[]{:S(2)}, u32[]{:S(2)}) collective-permute-start(bf16[64,768]{1,0:T(8,128)(2,1)S(1)} %pad_maximum_fusion.6), channel_id=1, source_target_pairs={{0,8},{8,64},{64,72},{72,0},{1,9},{9,65},{65,73},{73,1},{2,10},{10... | collective-permute-start | bytes 294920 | tf_op jit(solution)/shard_map/ppermute | solution.py:37
  161.6 5.7 %collective-permute-start.29 = (bf16[64,768]{1,0:T(8,128)(2,1)S(1)}, bf16[64,768]{1,0:T(8,128)(2,1)S(1)}, u32[]{:S(2)}, u32[]{:S(2)}) collective-permute-start(bf16[64,768]{1,0:T(8,128)(2,1)S(1)} %pad_maximum_fusion.6), channel_id=1, source_target_pairs={{0,64},{8,72},{64,0},{72,8},{1,65},{9,73},{65,1},{73,9},{2,66},{10... | collective-permute-start | bytes 294920 | tf_op jit(solution)/shard_map/ppermute | solution.py:37
  167.5 25.4 %copy-start.7 = (bf16[768,768]{1,0:T(8,128)(2,1)S(1)}, bf16[768,768]{1,0:T(8,128)(2,1)}, u32[]{:S(2)}) copy-start(bf16[768,768]{1,0:T(8,128)(2,1)} %param.7) | copy-start | bytes 3538948
  167.6 27.5 %copy-start.9 = (bf16[128,768]{1,0:T(8,128)(2,1)S(1)}, bf16[128,768]{1,0:T(8,128)(2,1)}, u32[]{:S(2)}) copy-start(bf16[128,768]{1,0:T(8,128)(2,1)} %copy-done.8) | copy-start | bytes 589828
  188.2 10.1 %collective-permute-start.30 = (bf16[16,56,768]{2,1,0:T(8,128)(2,1)S(1)}, bf16[16,56,768]{2,1,0:T(8,128)(2,1)S(1)}, u32[]{:S(2)}, u32[]{:S(2)}) collective-permute-start(bf16[16,56,768]{2,1,0:T(8,128)(2,1)S(1)} %all_to_all.20.mine), channel_id=1, source_target_pairs={{0,1},{1,0},{2,3},{3,2},{4,5},{5,4},{6,7},{7,6},{8,9},{9,8},{10,11... | collective-permute-start | bytes 4128776 | tf_op jit(solution)/shard_map/ppermute | solution.py:29

commit v6 on v5

--- a/solution.py
+++ b/solution.py
@@ -82,7 +82,7 @@
     return sum(p.astype(f32) for p in parts)
 
 
-def scatter_text(g):
+def scatter_text(g, image_part):
     b = g.shape[0] // 4
     h = b // 2
     g0, g1, g2, g3 = (g[k * b : (k + 1) * b] for k in range(4))
@@ -90,9 +90,9 @@
     high = from_y(g2[h:], 1)
     g1 = jnp.concatenate([plus(g1[:h], low).astype(bf16), g1[h:]], axis=0)
     g3 = jnp.concatenate([g3[:h], plus(g3[h:], high).astype(bf16)], axis=0)
-    g1, g3 = lax.optimization_barrier((g1, g3))
+    g1, g3, image_part = lax.optimization_barrier((g1, g3, image_part))
     g0 = plus(g0, from_y(g1, 3), from_y(g3, 1))
-    return g0[:h] + from_mirror(g0[h:].astype(bf16)).astype(f32)
+    return g0[:h] + from_mirror(g0[h:].astype(bf16)).astype(f32), image_part
 
 
 def params(mib=40):
@@ -340,8 +340,8 @@
         place.reshape(1), logits, row_total, column_total, images, images_other, texts, image_emb
     )
     image_part = plus(image_part, from_core(other_part)).astype(bf16)
+    text_emb_grad, image_part = scatter_text(text_part, image_part)
     image_emb_grad = plus(*lax.all_to_all(image_part.reshape(8, own, width), PAIR_Z, 0, 0))
-    text_emb_grad = scatter_text(text_part)
     matched = sharpness_factor * jnp.sum(image_emb.astype(f32) * text_emb.astype(f32), axis=1)
     own_rows = lax.dynamic_slice_in_dim(row_total[0], place * own, own)
     loss_part = jnp.sum(

time: 203 us -> 203 us (level)
  no operation moved by 1% of the time
where the time goes in v6:
time: 203 us; the launch traced here: 202 us
  starting transfers between devices  65.8 us (32%)
  waiting for transfers between devices  51.8 us (26%)
  Pallas kernels  25.6 us (13%)
  blocking collectives  20.6 us (10%)
  other arithmetic  13.3 us (7%)
  local copies, waits for them, and re-layouts  10.9 us (5%)
  matrix products  7.19 us (4%)
  between operations  6.58 us (3%)
    all_to_all x1, waiting for transfers between devices, reduce_weights(): got = plus(*lax.all_to_all(sent, YZ, 0, 0))  22.2 us
    all_to_all x1, blocking collectives, spread(): return lax.all_to_all(jnp.broadcast_to(v[None], (n,) + v.shape), axes, 0, 0)  20.6 us
    ppermute x8, starting transfers between devices, from_core(): return lax.ppermute(v, 'c', [(0, 1), (1, 0)])  18.5 us
    pallas_call x1, Pallas kernels, block_grads(): pl.pallas_call(grads_kernel, grid=(steps + 1,), in_specs=[pl.BlockSpec(me...  14.7 us
    ppermute x11, starting transfers between devices, from_y(): return lax.ppermute(v, 'y', [(i, (i - k) % 4) for i in range(4)])  13.4 us
    ppermute x11, waiting for transfers between devices, from_y(): return lax.ppermute(v, 'y', [(i, (i - k) % 4) for i in range(4)])  12.4 us
    pallas_call x1, Pallas kernels, block_logits(): pl.pallas_call(logits_kernel, grid=(steps,), in_specs=[pl.BlockSpec((TILE...  8.29 us
    ppermute x3, starting transfers between devices, from_mirror(): return lax.ppermute(v, X, [(i, 3 - i) for i in range(4)])  7.51 us
  transfers between devices with their start and end apart: 34, of which 17 were waited for; matrix products, arithmetic and copies ran while one was open for 11% of the time, Pallas kernels for 0%

profile of v6, /device:TPU:1, one launch (start us, length us, event | category | flops | bytes accessed | tf_op | source)
XLA Modules:
  0.0 201.8 jit_solution(2893756116325854584)
XLA Ops:
  0.7 1.4 copy-done
  2.0 1.5 multiply_reduce_fusion.3
  4.8 3.3 %collective-permute-start = (bf16[128,768]{1,0:T(8,128)(2,1)S(1)}, bf16[128,768]{1,0:T(8,128)(2,1)}, u32[]{:S(2)}, u32[]{:S(2)}) collective-permute-start(bf16[128,768]{1,0:T(8,128)(2,1)S(1)} %get-tuple-element.47), channel_id=1, source_target_pairs={{0,72},{8,64},{64,8},{72,0},{1,73},{9,65},{65,9},{73,1},{2,74},{10... | collective-permute-start | bytes 589832 | tf_op jit(solution)/shard_map/ppermute | solution.py:33
  8.1 1.2 broadcast_in_dim.55
  9.3 5.0 %all-to-all-start = ((bf16[8,128,768]{2,1,0:T(8,128)(2,1)}), bf16[8,128,768]{2,1,0:T(8,128)(2,1)S(1)}, u32[]{:S(2)}, u32[]{:S(2)}) async-start(bf16[8,128,768]{2,1,0:T(8,128)(2,1)} %broadcast_in_dim.55), calls=%async_computation | async-start | bytes 3145728 | tf_op jit(solution)/shard_map/all_to_all | solution.py:49
  14.4 1.0 pad_maximum_fusion.1
  15.3 2.8 %collective-permute-start.1 = (bf16[256,768]{1,0:T(8,128)(2,1)S(1)}, bf16[256,768]{1,0:T(8,128)(2,1)S(1)}, u32[]{:S(2)}, u32[]{:S(2)}) collective-permute-start(bf16[256,768]{1,0:T(8,128)(2,1)S(1)} %pad_maximum_fusion.1), channel_id=1, source_target_pairs={{0,48},{16,0},{32,16},{48,32},{1,49},{17,1},{33,17},{49,33},{2,50}... | collective-permute-start | bytes 1179656 | tf_op jit(solution)/shard_map/ppermute | solution.py:41
  18.1 1.0 constant_dynamic-slice_fusion.4
  19.1 1.6 collective-permute-start.5
  20.7 1.0 constant_dynamic-slice_fusion.2
  21.8 0.8 constant_dynamic-update-slice_fusion.4
  23.1 0.7 pad_maximum_fusion.5
  23.8 1.5 collective-permute-done.1
  25.3 3.5 %collective-permute-start.2 = (bf16[128,768]{1,0:T(8,128)(2,1)S(1)}, bf16[128,768]{1,0:T(8,128)(2,1)S(1)}, u32[]{:S(2)}, u32[]{:S(2)}) collective-permute-start(bf16[128,768]{1,0:T(8,128)(2,1)S(1)} %slice.122), channel_id=1, source_target_pairs={{0,48},{16,0},{32,16},{48,32},{1,49},{17,1},{33,17},{49,33},{2,50}... | collective-permute-start | bytes 589832 | tf_op jit(solution)/shard_map/ppermute | solution.py:41
  28.8 0.7 pad_maximum_fusion.4
  29.6 0.8 constant_dynamic-update-slice_fusion.3
  30.4 1.0 collective-permute-done.2
  32.1 3.2 %collective-permute-done.4 = bf16[128,768]{1,0:T(8,128)(2,1)S(1)} collective-permute-done((bf16[128,768]{1,0:T(8,128)(2,1)S(1)}, bf16[128,768]{1,0:T(8,128)(2,1)S(1)}, u32[]{:S(2)}, u32[]{:S(2)}) %collective-permute-start.4) | collective-permute-done | bytes 196640 | tf_op jit(solution)/shard_map/ppermute | solution.py:41
  35.3 0.7 constant_dynamic-update-slice_fusion.1
  36.0 0.8 constant_dynamic-update-slice_fusion.texts
  36.8 3.6 %collective-permute-start.7 = (bf16[1024,768]{1,0:T(8,128)(2,1)S(1)}, bf16[1024,768]{1,0:T(8,128)(2,1)S(1)}, u32[]{:S(2)}, u32[]{:S(2)}) collective-permute-start(bf16[1024,768]{1,0:T(8,128)(2,1)S(1)} %bitcast.39), channel_id=1, source_target_pairs={{0,1},{1,0},{2,3},{3,2},{4,5},{5,4},{6,7},{7,6},{8,9},{9,8},{10,11... | collective-permute-start | bytes 4718600 | tf_op jit(solution)/shard_map/ppermute | solution.py:29
  40.4 3.0 %collective-permute-done.7.other = bf16[1024,768]{1,0:T(8,128)(2,1)S(1)} collective-permute-done((bf16[1024,768]{1,0:T(8,128)(2,1)S(1)}, bf16[1024,768]{1,0:T(8,128)(2,1)S(1)}, u32[]{:S(2)}, u32[]{:S(2)}) %collective-permute-start.7) | collective-permute-done | bytes 1572896 | tf_op jit(solution)/shard_map/ppermute | solution.py:29
  43.4 1.1 copy-done.17
  44.6 8.3 %block_logits.1 = (f32[2048,1024]{1,0:T(8,128)}, f32[1,2048]{1,0:T(1,128)S(1)}, f32[1,1024]{1,0:T(1,128)S(1)}) custom-call(bf16[1024,768]{1,0:T(8,128)(2,1)S(1)} %bitcast.40, bf16[1024,768]{1,0:T(8,128)(2,1)} %copy-done.17, bf16[1024,768]{1,0:T(8,128)(2,1)} %constant_dynamic-update-slice_fusion.texts), custom_call_target="tpu_custom_call" | custom-call | flops 3221225472 | bytes 13107200 | tf_op jit(solution)/shard_map/block_logits/pallas_call | solution.py:123
  53.3 1.5 collective-permute-start.9
  54.9 1.4 collective-permute-start.14
  56.2 2.3 %collective-permute-done.14 = f32[4,2,128]{2,1,0:T(2,128)S(1)} collective-permute-done((f32[4,2,128]{2,1,0:T(2,128)S(1)}, f32[4,2,128]{2,1,0:T(2,128)S(1)}, u32[]{:S(2)}, u32[]{:S(2)}) %collective-permute-start.14) | collective-permute-done | bytes 4128 | tf_op jit(solution)/shard_map/ppermute | solution.py:33
  58.6 0.9 collective-permute-start.15
  60.2 2.7 %collective-permute-start.11 = (f32[1,2048]{1,0:T(1,128)S(1)}, f32[1,2048]{1,0:T(1,128)S(1)}, u32[]{:S(2)}, u32[]{:S(2)}) collective-permute-start(f32[1,2048]{1,0:T(1,128)S(1)} %add_add_fusion.2), channel_id=1, source_target_pairs={{0,6},{2,0},{4,2},{6,4},{1,7},{3,1},{5,3},{7,5},{8,14},{10,8},{12,... | collective-permute-start | bytes 24584 | tf_op jit(solution)/shard_map/ppermute | solution.py:78
  62.9 1.8 collective-permute-start.13
  64.8 1.9 collective-permute-done.12
  67.0 14.7 %block_grads.1 = (bf16[1024,768]{1,0:T(8,128)(2,1)S(1)}, bf16[1024,768]{1,0:T(8,128)(2,1)S(1)}, bf16[1024,768]{1,0:T(8,128)(2,1)S(1)}) custom-call(s32[1]{0:T(128)} %bitcast.1.place, f32[2048,1024]{1,0:T(8,128)} %get-tuple-element.29.logits, f32[1,2048]{1,0:T(1,128)S(1)} %add_add_fusion.1.row_total, f32[1,1024]{1,0:T(1,128)S(1)} %bitcast.42, ...), custom_call_target="tpu_custom_call" | custom-call | flops 6442450944 | bytes 17825792 | tf_op jit(solution)/shard_map/block_grads/pallas_call | solution.py:196
  81.7 3.9 %collective-permute-start.20 = (bf16[1024,768]{1,0:T(8,128)(2,1)S(1)}, bf16[1024,768]{1,0:T(8,128)(2,1)S(1)}, u32[]{:S(2)}, u32[]{:S(2)}) collective-permute-start(bf16[1024,768]{1,0:T(8,128)(2,1)S(1)} %get-tuple-element.34), channel_id=1, source_target_pairs={{0,1},{1,0},{2,3},{3,2},{4,5},{5,4},{6,7},{7,6},{8,9},{9,8},{10,11... | collective-permute-start | bytes 4718600 | tf_op jit(solution)/shard_map/ppermute | solution.py:29
  85.6 1.2 collective-permute-start.18
  86.8 1.6 collective-permute-start.19
  88.3 5.0 %collective-permute-done.18 = bf16[128,768]{1,0:T(8,128)(2,1)S(1)} collective-permute-done((bf16[128,768]{1,0:T(8,128)(2,1)S(1)}, bf16[128,768]{1,0:T(8,128)(2,1)S(1)}, u32[]{:S(2)}, u32[]{:S(2)}) %collective-permute-start.18) | collective-permute-done | bytes 196640 | tf_op jit(solution)/shard_map/ppermute | solution.py:41
  93.7 0.8 pad_maximum_fusion.3
  94.4 0.8 pad_maximum_fusion.2
  95.2 1.5 add_convert_fusion
  96.8 4.2 %all-to-all-start.1 = ((bf16[8,128,768]{2,1,0:T(8,128)(2,1)}), bf16[8,128,768]{2,1,0:T(8,128)(2,1)S(1)}, u32[]{:S(2)}, u32[]{:S(2)}) async-start(bf16[8,128,768]{2,1,0:T(8,128)(2,1)} %bitcast.46), calls=%async_computation.1 | async-start | bytes 3145728 | tf_op jit(solution)/shard_map/all_to_all | solution.py:344
  101.0 1.1 collective-permute-start.22
  102.1 1.5 collective-permute-start.23
  104.8 1.6 collective-permute-start.26
  106.4 1.1 collective-permute-done.26
  110.6 1.4 collective-permute-done.22
  112.0 1.4 convert_add_fusion
  113.5 2.9 %collective-permute-start.24 = (bf16[128,768]{1,0:T(8,128)(2,1)S(1)}, bf16[128,768]{1,0:T(8,128)(2,1)S(1)}, u32[]{:S(2)}, u32[]{:S(2)}) collective-permute-start(bf16[128,768]{1,0:T(8,128)(2,1)S(1)} %slice.165), channel_id=1, source_target_pairs={{0,72},{8,64},{64,8},{72,0},{1,73},{9,65},{65,9},{73,1},{2,74},{10... | collective-permute-start | bytes 589832 | tf_op jit(solution)/shard_map/ppermute | solution.py:33
  116.3 3.3 %collective-permute-done.24 = bf16[128,768]{1,0:T(8,128)(2,1)S(1)} collective-permute-done((bf16[128,768]{1,0:T(8,128)(2,1)S(1)}, bf16[128,768]{1,0:T(8,128)(2,1)S(1)}, u32[]{:S(2)}, u32[]{:S(2)}) %collective-permute-start.24) | collective-permute-done | bytes 196640 | tf_op jit(solution)/shard_map/ppermute | solution.py:33
  119.7 1.2 multiply_reduce_fusion.1
  120.9 0.8 divide_convert_fusion
  121.7 2.9 %collective-permute-start.25 = (bf16[128,768]{1,0:T(8,128)(2,1)}, bf16[128,768]{1,0:T(8,128)(2,1)}, u32[]{:S(2)}, u32[]{:S(2)}) collective-permute-start(bf16[128,768]{1,0:T(8,128)(2,1)} %divide_convert_fusion), channel_id=1, source_target_pairs={{0,1},{1,0},{2,3},{3,2},{4,5},{5,4},{6,7},{7,6},{8,9},{9,8},{10,11... | collective-permute-start | bytes 589832 | tf_op jit(solution)/shard_map/ppermute | solution.py:29
  124.5 1.0 fusion.6
  126.0 1.4 convolution_convert_fusion.1
  127.8 1.3 pad_maximum_fusion
  129.1 6.6 %all-to-all-start.2 = ((bf16[16,64,768]{2,1,0:T(8,128)(2,1)}), bf16[16,64,768]{2,1,0:T(8,128)(2,1)S(1)}, u32[]{:S(2)}, u32[]{:S(2)}) async-start(bf16[16,64,768]{2,1,0:T(8,128)(2,1)} %pad_maximum_fusion), calls=%async_computation.2 | async-start | bytes 3145728 | tf_op jit(solution)/shard_map/all_to_all | solution.py:307
  135.7 22.2 %all-to-all-done.2 = bf16[16,64,768]{2,1,0:T(8,128)(2,1)S(1)} async-done(((bf16[16,64,768]{2,1,0:T(8,128)(2,1)}), bf16[16,64,768]{2,1,0:T(8,128)(2,1)S(1)}, u32[]{:S(2)}, u32[]{:S(2)}) %all-to-all-start.2) | async-done | bytes 1572896 | tf_op jit(solution)/shard_map/all_to_all | solution.py:307
  158.5 2.8 %collective-permute-start.27 = (bf16[64,768]{1,0:T(8,128)(2,1)S(1)}, bf16[64,768]{1,0:T(8,128)(2,1)S(1)}, u32[]{:S(2)}, u32[]{:S(2)}) collective-permute-start(bf16[64,768]{1,0:T(8,128)(2,1)S(1)} %pad_maximum_fusion.6), channel_id=1, source_target_pairs={{0,72},{8,0},{64,8},{72,64},{1,73},{9,1},{65,9},{73,65},{2,74},{10... | collective-permute-start | bytes 294920 | tf_op jit(solution)/shard_map/ppermute | solution.py:37
  161.3 1.3 collective-permute-start.29
  162.9 4.1 %collective-permute-done.28 = bf16[64,768]{1,0:T(8,128)(2,1)S(1)} collective-permute-done((bf16[64,768]{1,0:T(8,128)(2,1)S(1)}, bf16[64,768]{1,0:T(8,128)(2,1)S(1)}, u32[]{:S(2)}, u32[]{:S(2)}) %collective-permute-start.28) | collective-permute-done | bytes 98336 | tf_op jit(solution)/shard_map/ppermute | solution.py:37
  167.2 20.6 %all_to_all.20.mine = bf16[16,56,768]{2,1,0:T(8,128)(2,1)S(1)} all-to-all(bf16[16,56,768]{2,1,0:T(8,128)(2,1)S(1)} %broadcast_in_dim.65), channel_id=1, replica_groups=mesh['xh'=2,'y'=4,'xl'=2,'z'=4,'c'=2] {'y','z'}, dimensions={0} | all-to-all | bytes 2752512 | tf_op jit(solution)/shard_map/all_to_all | solution.py:49
  187.9 4.7 %collective-permute-start.30 = (bf16[16,56,768]{2,1,0:T(8,128)(2,1)S(1)}, bf16[16,56,768]{2,1,0:T(8,128)(2,1)S(1)}, u32[]{:S(2)}, u32[]{:S(2)}) collective-permute-start(bf16[16,56,768]{2,1,0:T(8,128)(2,1)S(1)} %all_to_all.20.mine), channel_id=1, source_target_pairs={{0,1},{1,0},{2,3},{3,2},{4,5},{5,4},{6,7},{7,6},{8,9},{9,8},{10,11... | collective-permute-start | bytes 4128776 | tf_op jit(solution)/shard_map/ppermute | solution.py:29
  192.6 2.1 %convolution_convert_fusion.3 = bf16[128,768]{1,0:T(8,128)(2,1)} fusion(bf16[128,768]{1,0:T(8,128)(2,1)} %divide_convert_fusion, bf16[768,768]{1,0:T(8,128)(2,1)S(1)} %copy-done.7), kind=kOutput, calls=%fused_computation.5 | convolution fusion | flops 151093248 | bytes 1572864 | tf_op jit(solution)/shard_map/dot_general | solution.py:280
  194.7 1.3 convolution_convert_fusion.2
  198.0 2.7 %whole_terms.1 = (f32[1024,768]{1,0:T(8,128)}, f32[768,768]{1,0:T(8,128)}) custom-call(s32[1]{0:T(128)} %bitcast.12.core, bf16[16,56,768]{2,1,0:T(8,128)(2,1)S(1)} %all_to_all.20.mine, bf16[16,56,768]{2,1,0:T(8,128)(2,1)S(1)} %collective-permute-done.30.other), custom_call_target="tpu_custom_call" | custom-call | bytes 8257536 | tf_op jit(solution)/shard_map/whole_terms/pallas_call | solution.py:249
  (104 shorter events, 8.2 us)
Async XLA Ops:
  0.6 1.4 copy-start
  0.6 2.9 %copy-start.11 = (bf16[128,768]{1,0:T(8,128)(2,1)S(1)}, bf16[128,768]{1,0:T(8,128)(2,1)}, u32[]{:S(2)}) copy-start(bf16[128,768]{1,0:T(8,128)(2,1)} %param.5) | copy-start | bytes 589828
  2.0 1.5 copy-start.6
  3.6 0.8 copy-start.2
  4.0 0.8 copy-start.4
  4.0 5.3 %copy-start.13 = (f32[128]{0:T(128)}, f32[128]{0:T(128)S(1)}, u32[]{:S(2)}) copy-start(f32[128]{0:T(128)S(1)} %get-tuple-element.69) | copy-start | bytes 1540
  4.8 9.6 %collective-permute-start = (bf16[128,768]{1,0:T(8,128)(2,1)S(1)}, bf16[128,768]{1,0:T(8,128)(2,1)}, u32[]{:S(2)}, u32[]{:S(2)}) collective-permute-start(bf16[128,768]{1,0:T(8,128)(2,1)S(1)} %get-tuple-element.47), channel_id=1, source_target_pairs={{0,72},{8,64},{64,8},{72,0},{1,73},{9,65},{65,9},{73,1},{2,74},{10... | collective-permute-start | bytes 589832 | tf_op jit(solution)/shard_map/ppermute | solution.py:33
  9.3 27.5 %all-to-all-start = ((bf16[8,128,768]{2,1,0:T(8,128)(2,1)}), bf16[8,128,768]{2,1,0:T(8,128)(2,1)S(1)}, u32[]{:S(2)}, u32[]{:S(2)}) async-start(bf16[8,128,768]{2,1,0:T(8,128)(2,1)} %broadcast_in_dim.55), calls=%async_computation | async-start | bytes 3145728 | tf_op jit(solution)/shard_map/all_to_all | solution.py:49
  15.3 10.0 %collective-permute-start.1 = (bf16[256,768]{1,0:T(8,128)(2,1)S(1)}, bf16[256,768]{1,0:T(8,128)(2,1)S(1)}, u32[]{:S(2)}, u32[]{:S(2)}) collective-permute-start(bf16[256,768]{1,0:T(8,128)(2,1)S(1)} %pad_maximum_fusion.1), channel_id=1, source_target_pairs={{0,48},{16,0},{32,16},{48,32},{1,49},{17,1},{33,17},{49,33},{2,50}... | collective-permute-start | bytes 1179656 | tf_op jit(solution)/shard_map/ppermute | solution.py:41
  18.1 11.4 %collective-permute-start.3 = (bf16[256,768]{1,0:T(8,128)(2,1)S(1)}, bf16[256,768]{1,0:T(8,128)(2,1)S(1)}, u32[]{:S(2)}, u32[]{:S(2)}) collective-permute-start(bf16[256,768]{1,0:T(8,128)(2,1)S(1)} %pad_maximum_fusion.1), channel_id=1, source_target_pairs={{0,16},{16,32},{32,48},{48,0},{1,17},{17,33},{33,49},{49,1},{2,18}... | collective-permute-start | bytes 1179656 | tf_op jit(solution)/shard_map/ppermute | solution.py:41
  19.1 9.7 %collective-permute-start.5 = (bf16[128,512]{1,0:T(8,128)(2,1)S(1)}, bf16[128,512]{1,0:T(8,128)(2,1)S(1)}, u32[]{:S(2)}, u32[]{:S(2)}) collective-permute-start(bf16[128,512]{1,0:T(8,128)(2,1)S(1)} %get-tuple-element.55), channel_id=1, source_target_pairs={{0,1},{1,0},{2,3},{3,2},{4,5},{5,4},{6,7},{7,6},{8,9},{9,8},{10,11... | collective-permute-start | bytes 393224 | tf_op jit(solution)/shard_map/ppermute | solution.py:29
  21.7 1.4 collective-permute-start.6
  25.3 6.1 %collective-permute-start.2 = (bf16[128,768]{1,0:T(8,128)(2,1)S(1)}, bf16[128,768]{1,0:T(8,128)(2,1)S(1)}, u32[]{:S(2)}, u32[]{:S(2)}) collective-permute-start(bf16[128,768]{1,0:T(8,128)(2,1)S(1)} %slice.122), channel_id=1, source_target_pairs={{0,48},{16,0},{32,16},{48,32},{1,49},{17,1},{33,17},{49,33},{2,50}... | collective-permute-start | bytes 589832 | tf_op jit(solution)/shard_map/ppermute | solution.py:41
  29.5 5.8 %collective-permute-start.4 = (bf16[128,768]{1,0:T(8,128)(2,1)S(1)}, bf16[128,768]{1,0:T(8,128)(2,1)S(1)}, u32[]{:S(2)}, u32[]{:S(2)}) collective-permute-start(bf16[128,768]{1,0:T(8,128)(2,1)S(1)} %slice.123), channel_id=1, source_target_pairs={{0,16},{16,32},{32,48},{48,0},{1,17},{17,33},{33,49},{49,1},{2,18}... | collective-permute-start | bytes 589832 | tf_op jit(solution)/shard_map/ppermute | solution.py:41
  36.8 6.6 %collective-permute-start.7 = (bf16[1024,768]{1,0:T(8,128)(2,1)S(1)}, bf16[1024,768]{1,0:T(8,128)(2,1)S(1)}, u32[]{:S(2)}, u32[]{:S(2)}) collective-permute-start(bf16[1024,768]{1,0:T(8,128)(2,1)S(1)} %bitcast.39), channel_id=1, source_target_pairs={{0,1},{1,0},{2,3},{3,2},{4,5},{5,4},{6,7},{7,6},{8,9},{9,8},{10,11... | collective-permute-start | bytes 4718600 | tf_op jit(solution)/shard_map/ppermute | solution.py:29
  43.4 1.1 copy-start.17
  52.9 6.7 %collective-permute-start.10 = (f32[1,2048]{1,0:T(1,128)S(1)}, f32[1,2048]{1,0:T(1,128)S(1)}, u32[]{:S(2)}, u32[]{:S(2)}) collective-permute-start(f32[1,2048]{1,0:T(1,128)S(1)} %pad_maximum_fusion.7), channel_id=1, source_target_pairs={{0,1},{1,0},{8,9},{9,8},{2,3},{3,2},{10,11},{11,10},{4,5},{5,4},{1... | collective-permute-start | bytes 24584 | tf_op jit(solution)/shard_map/ppermute | solution.py:75
  53.3 6.9 %collective-permute-start.9 = (f32[1,2048]{1,0:T(1,128)S(1)}, f32[1,2048]{1,0:T(1,128)S(1)}, u32[]{:S(2)}, u32[]{:S(2)}) collective-permute-start(f32[1,2048]{1,0:T(1,128)S(1)} %pad_maximum_fusion.7), channel_id=1, source_target_pairs={{0,9},{1,8},{8,1},{9,0},{2,11},{3,10},{10,3},{11,2},{4,13},{5,12},... | collective-permute-start | bytes 24584 | tf_op jit(solution)/shard_map/ppermute | solution.py:75
  54.8 5.4 %collective-permute-start.8 = (f32[1,2048]{1,0:T(1,128)S(1)}, f32[1,2048]{1,0:T(1,128)S(1)}, u32[]{:S(2)}, u32[]{:S(2)}) collective-permute-start(f32[1,2048]{1,0:T(1,128)S(1)} %get-tuple-element.30), channel_id=1, source_target_pairs={{0,8},{1,9},{8,0},{9,1},{2,10},{3,11},{10,2},{11,3},{4,12},{5,13},... | collective-permute-start | bytes 24584 | tf_op jit(solution)/shard_map/ppermute | solution.py:75
  54.9 3.7 %collective-permute-start.14 = (f32[4,2,128]{2,1,0:T(2,128)S(1)}, f32[4,2,128]{2,1,0:T(2,128)S(1)}, u32[]{:S(2)}, u32[]{:S(2)}) collective-permute-start(f32[4,2,128]{2,1,0:T(2,128)S(1)} %bitcast.44), channel_id=1, source_target_pairs={{0,72},{8,64},{64,8},{72,0},{1,73},{9,65},{65,9},{73,1},{2,74},{10... | collective-permute-start | bytes 12296 | tf_op jit(solution)/shard_map/ppermute | solution.py:33
  58.6 6.2 %collective-permute-start.17 = (f32[4,2,128]{2,1,0:T(2,128)S(1)}, f32[4,2,128]{2,1,0:T(2,128)S(1)}, u32[]{:S(2)}, u32[]{:S(2)}) collective-permute-start(f32[4,2,128]{2,1,0:T(2,128)S(1)} %add.199), channel_id=1, source_target_pairs={{0,32},{16,48},{32,0},{48,16},{1,33},{17,49},{33,1},{49,17},{2,34}... | collective-permute-start | bytes 12296 | tf_op jit(solution)/shard_map/ppermute | solution.py:41
  58.6 4.3 %collective-permute-start.15 = (f32[4,2,128]{2,1,0:T(2,128)S(1)}, f32[4,2,128]{2,1,0:T(2,128)S(1)}, u32[]{:S(2)}, u32[]{:S(2)}) collective-permute-start(f32[4,2,128]{2,1,0:T(2,128)S(1)} %add.199), channel_id=1, source_target_pairs={{0,48},{16,0},{32,16},{48,32},{1,49},{17,1},{33,17},{49,33},{2,50}... | collective-permute-start | bytes 12296 | tf_op jit(solution)/shard_map/ppermute | solution.py:41
  59.5 5.2 %collective-permute-start.16 = (f32[4,2,128]{2,1,0:T(2,128)S(1)}, f32[4,2,128]{2,1,0:T(2,128)S(1)}, u32[]{:S(2)}, u32[]{:S(2)}) collective-permute-start(f32[4,2,128]{2,1,0:T(2,128)S(1)} %add.199), channel_id=1, source_target_pairs={{0,16},{16,32},{32,48},{48,0},{1,17},{17,33},{33,49},{49,1},{2,18}... | collective-permute-start | bytes 12296 | tf_op jit(solution)/shard_map/ppermute | solution.py:41
  60.2 4.5 %collective-permute-start.11 = (f32[1,2048]{1,0:T(1,128)S(1)}, f32[1,2048]{1,0:T(1,128)S(1)}, u32[]{:S(2)}, u32[]{:S(2)}) collective-permute-start(f32[1,2048]{1,0:T(1,128)S(1)} %add_add_fusion.2), channel_id=1, source_target_pairs={{0,6},{2,0},{4,2},{6,4},{1,7},{3,1},{5,3},{7,5},{8,14},{10,8},{12,... | collective-permute-start | bytes 24584 | tf_op jit(solution)/shard_map/ppermute | solution.py:78
  62.9 3.7 %collective-permute-start.12 = (f32[1,2048]{1,0:T(1,128)S(1)}, f32[1,2048]{1,0:T(1,128)S(1)}, u32[]{:S(2)}, u32[]{:S(2)}) collective-permute-start(f32[1,2048]{1,0:T(1,128)S(1)} %add_add_fusion.2), channel_id=1, source_target_pairs={{0,2},{2,4},{4,6},{6,0},{1,3},{3,5},{5,7},{7,1},{8,10},{10,12},{12... | collective-permute-start | bytes 24584 | tf_op jit(solution)/shard_map/ppermute | solution.py:78
  62.9 4.0 %collective-permute-start.13 = (f32[1,2048]{1,0:T(1,128)S(1)}, f32[1,2048]{1,0:T(1,128)S(1)}, u32[]{:S(2)}, u32[]{:S(2)}) collective-permute-start(f32[1,2048]{1,0:T(1,128)S(1)} %add_add_fusion.2), channel_id=1, source_target_pairs={{0,4},{2,6},{4,0},{6,2},{1,5},{3,7},{5,1},{7,3},{8,12},{10,14},{12... | collective-permute-start | bytes 24584 | tf_op jit(solution)/shard_map/ppermute | solution.py:78
  81.7 12.8 %copy-start.1 = (bf16[1024,768]{1,0:T(8,128)(2,1)}, bf16[1024,768]{1,0:T(8,128)(2,1)S(1)}, u32[]{:S(2)}) copy-start(bf16[1024,768]{1,0:T(8,128)(2,1)S(1)} %get-tuple-element.32) | copy-start | bytes 4718596
  81.7 13.6 %collective-permute-start.20 = (bf16[1024,768]{1,0:T(8,128)(2,1)S(1)}, bf16[1024,768]{1,0:T(8,128)(2,1)S(1)}, u32[]{:S(2)}, u32[]{:S(2)}) collective-permute-start(bf16[1024,768]{1,0:T(8,128)(2,1)S(1)} %get-tuple-element.34), channel_id=1, source_target_pairs={{0,1},{1,0},{2,3},{3,2},{4,5},{5,4},{6,7},{7,6},{8,9},{9,8},{10,11... | collective-permute-start | bytes 4718600 | tf_op jit(solution)/shard_map/ppermute | solution.py:29
  85.6 7.8 %collective-permute-start.18 = (bf16[128,768]{1,0:T(8,128)(2,1)S(1)}, bf16[128,768]{1,0:T(8,128)(2,1)S(1)}, u32[]{:S(2)}, u32[]{:S(2)}) collective-permute-start(bf16[128,768]{1,0:T(8,128)(2,1)S(1)} %get-tuple-element.51), channel_id=1, source_target_pairs={{0,16},{16,32},{32,48},{48,0},{1,17},{17,33},{33,49},{49,1},{2,18}... | collective-permute-start | bytes 589832 | tf_op jit(solution)/shard_map/ppermute | solution.py:41
  86.8 6.8 %collective-permute-start.19 = (bf16[128,768]{1,0:T(8,128)(2,1)S(1)}, bf16[128,768]{1,0:T(8,128)(2,1)S(1)}, u32[]{:S(2)}, u32[]{:S(2)}) collective-permute-start(bf16[128,768]{1,0:T(8,128)(2,1)S(1)} %get-tuple-element.49), channel_id=1, source_target_pairs={{0,48},{16,0},{32,16},{48,32},{1,49},{17,1},{33,17},{49,33},{2,50}... | collective-permute-start | bytes 589832 | tf_op jit(solution)/shard_map/ppermute | solution.py:41
  96.8 27.8 %all-to-all-start.1 = ((bf16[8,128,768]{2,1,0:T(8,128)(2,1)}), bf16[8,128,768]{2,1,0:T(8,128)(2,1)S(1)}, u32[]{:S(2)}, u32[]{:S(2)}) async-start(bf16[8,128,768]{2,1,0:T(8,128)(2,1)} %bitcast.46), calls=%async_computation.1 | async-start | bytes 3145728 | tf_op jit(solution)/shard_map/all_to_all | solution.py:344
  101.0 11.1 %collective-permute-start.22 = (bf16[256,768]{1,0:T(8,128)(2,1)}, bf16[256,768]{1,0:T(8,128)(2,1)}, u32[]{:S(2)}, u32[]{:S(2)}) collective-permute-start(bf16[256,768]{1,0:T(8,128)(2,1)} %pad_maximum_fusion.2), channel_id=1, source_target_pairs={{0,16},{16,32},{32,48},{48,0},{1,17},{17,33},{33,49},{49,1},{2,18}... | collective-permute-start | bytes 1179656 | tf_op jit(solution)/shard_map/ppermute | solution.py:41
  102.1 9.9 %collective-permute-start.23 = (bf16[256,768]{1,0:T(8,128)(2,1)}, bf16[256,768]{1,0:T(8,128)(2,1)}, u32[]{:S(2)}, u32[]{:S(2)}) collective-permute-start(bf16[256,768]{1,0:T(8,128)(2,1)} %pad_maximum_fusion.3), channel_id=1, source_target_pairs={{0,48},{16,0},{32,16},{48,32},{1,49},{17,1},{33,17},{49,33},{2,50}... | collective-permute-start | bytes 1179656 | tf_op jit(solution)/shard_map/ppermute | solution.py:41
  104.8 2.7 %collective-permute-start.26 = (f32[]{:T(128)}, f32[]{:T(128)}, u32[]{:S(2)}, u32[]{:S(2)}) collective-permute-start(f32[]{:T(128)} %fusion.17), channel_id=1, source_target_pairs={{0,1},{1,0},{2,3},{3,2},{4,5},{5,4},{6,7},{7,6},{8,9},{9,8},{10,11... | collective-permute-start | bytes 20 | tf_op jit(solution)/shard_map/ppermute | solution.py:29
  110.6 5.7 %copy-start.15 = (pred[768]{0:T(1024)(128)(4,1)S(1)}, pred[768]{0:T(1024)(128)(4,1)}, u32[]{:S(2)}) copy-start(pred[768]{0:T(1024)(128)(4,1)} %iota_compare_fusion.1) | copy-start | bytes 2308
  110.6 10.2 %copy-start.5 = (f32[128,768]{1,0:T(8,128)S(1)}, f32[128,768]{1,0:T(8,128)}, u32[]{:S(2)}) copy-start(f32[128,768]{1,0:T(8,128)} %copy-done.4) | copy-start | bytes 1179652
  113.4 11.1 %copy-start.3 = (f32[128,768]{1,0:T(8,128)S(1)}, f32[128,768]{1,0:T(8,128)}, u32[]{:S(2)}) copy-start(f32[128,768]{1,0:T(8,128)} %copy-done.2) | copy-start | bytes 1179652
  113.5 6.2 %collective-permute-start.24 = (bf16[128,768]{1,0:T(8,128)(2,1)S(1)}, bf16[128,768]{1,0:T(8,128)(2,1)S(1)}, u32[]{:S(2)}, u32[]{:S(2)}) collective-permute-start(bf16[128,768]{1,0:T(8,128)(2,1)S(1)} %slice.165), channel_id=1, source_target_pairs={{0,72},{8,64},{64,8},{72,0},{1,73},{9,65},{65,9},{73,1},{2,74},{10... | collective-permute-start | bytes 589832 | tf_op jit(solution)/shard_map/ppermute | solution.py:33
  121.7 3.8 %copy-start.14 = (f32[128]{0:T(128)S(1)}, f32[128]{0:T(128)}, u32[]{:S(2)}) copy-start(f32[128]{0:T(128)} %copy-done.13) | copy-start | bytes 1540
  121.7 4.3 %collective-permute-start.25 = (bf16[128,768]{1,0:T(8,128)(2,1)}, bf16[128,768]{1,0:T(8,128)(2,1)}, u32[]{:S(2)}, u32[]{:S(2)}) collective-permute-start(bf16[128,768]{1,0:T(8,128)(2,1)} %divide_convert_fusion), channel_id=1, source_target_pairs={{0,1},{1,0},{2,3},{3,2},{4,5},{5,4},{6,7},{7,6},{8,9},{9,8},{10,11... | collective-permute-start | bytes 589832 | tf_op jit(solution)/shard_map/ppermute | solution.py:29
  124.5 1.4 copy-start.12
  125.5 1.9 copy-start.10
  125.7 1.7 copy-start.8
  125.7 1.7 collective-permute-start.21
  129.1 28.9 %all-to-all-start.2 = ((bf16[16,64,768]{2,1,0:T(8,128)(2,1)}), bf16[16,64,768]{2,1,0:T(8,128)(2,1)S(1)}, u32[]{:S(2)}, u32[]{:S(2)}) async-start(bf16[16,64,768]{2,1,0:T(8,128)(2,1)} %pad_maximum_fusion), calls=%async_computation.2 | async-start | bytes 3145728 | tf_op jit(solution)/shard_map/all_to_all | solution.py:307
  135.7 22.6 %copy-start.16 = (pred[768]{0:T(1024)(128)(4,1)S(1)}, pred[768]{0:T(1024)(128)(4,1)}, u32[]{:S(2)}) copy-start(pred[768]{0:T(1024)(128)(4,1)} %iota_compare_fusion.1) | copy-start | bytes 2308
  158.5 4.5 %collective-permute-start.27 = (bf16[64,768]{1,0:T(8,128)(2,1)S(1)}, bf16[64,768]{1,0:T(8,128)(2,1)S(1)}, u32[]{:S(2)}, u32[]{:S(2)}) collective-permute-start(bf16[64,768]{1,0:T(8,128)(2,1)S(1)} %pad_maximum_fusion.6), channel_id=1, source_target_pairs={{0,72},{8,0},{64,8},{72,64},{1,73},{9,1},{65,9},{73,65},{2,74},{10... | collective-permute-start | bytes 294920 | tf_op jit(solution)/shard_map/ppermute | solution.py:37
  161.3 5.7 %collective-permute-start.28 = (bf16[64,768]{1,0:T(8,128)(2,1)S(1)}, bf16[64,768]{1,0:T(8,128)(2,1)S(1)}, u32[]{:S(2)}, u32[]{:S(2)}) collective-permute-start(bf16[64,768]{1,0:T(8,128)(2,1)S(1)} %pad_maximum_fusion.6), channel_id=1, source_target_pairs={{0,8},{8,64},{64,72},{72,0},{1,9},{9,65},{65,73},{73,1},{2,10},{10... | collective-permute-start | bytes 294920 | tf_op jit(solution)/shard_map/ppermute | solution.py:37
  161.3 5.7 %collective-permute-start.29 = (bf16[64,768]{1,0:T(8,128)(2,1)S(1)}, bf16[64,768]{1,0:T(8,128)(2,1)S(1)}, u32[]{:S(2)}, u32[]{:S(2)}) collective-permute-start(bf16[64,768]{1,0:T(8,128)(2,1)S(1)} %pad_maximum_fusion.6), channel_id=1, source_target_pairs={{0,64},{8,72},{64,0},{72,8},{1,65},{9,73},{65,1},{73,9},{2,66},{10... | collective-permute-start | bytes 294920 | tf_op jit(solution)/shard_map/ppermute | solution.py:37
  167.2 25.4 %copy-start.7 = (bf16[768,768]{1,0:T(8,128)(2,1)S(1)}, bf16[768,768]{1,0:T(8,128)(2,1)}, u32[]{:S(2)}) copy-start(bf16[768,768]{1,0:T(8,128)(2,1)} %param.7) | copy-start | bytes 3538948
  167.2 27.5 %copy-start.9 = (bf16[128,768]{1,0:T(8,128)(2,1)S(1)}, bf16[128,768]{1,0:T(8,128)(2,1)}, u32[]{:S(2)}) copy-start(bf16[128,768]{1,0:T(8,128)(2,1)} %copy-done.8) | copy-start | bytes 589828
  187.9 10.1 %collective-permute-start.30 = (bf16[16,56,768]{2,1,0:T(8,128)(2,1)S(1)}, bf16[16,56,768]{2,1,0:T(8,128)(2,1)S(1)}, u32[]{:S(2)}, u32[]{:S(2)}) collective-permute-start(bf16[16,56,768]{2,1,0:T(8,128)(2,1)S(1)} %all_to_all.20.mine), channel_id=1, source_target_pairs={{0,1},{1,0},{2,3},{3,2},{4,5},{5,4},{6,7},{7,6},{8,9},{9,8},{10,11... | collective-permute-start | bytes 4128776 | tf_op jit(solution)/shard_map/ppermute | solution.py:29

commit v7 on v6

--- a/solution.py
+++ b/solution.py
@@ -332,7 +332,6 @@
         (images, gather_text(pair), image_halves, text_halves)
     )
     images_other = hbm(from_core(images))
-    texts = hbm(texts)
     logits, row_part, column_part = block_logits(images, images_other, texts)
     row_total = row_totals(row_part)
     column_total = column_totals(column_part)

time: 203 us -> 204 us (level)
    unnamed x40 -> x46, local copies, waits for them, and re-layouts: 6.04 us -> 7.13 us
  transfers between devices with their start and end apart: 34 -> 34, of which waited for: 17 -> 17; matrix products, arithmetic and copies ran while one was open for 11% -> 9% of each run, Pallas kernels for 0% -> 0%
where the time goes in v7:
time: 204 us; the launch traced here: 203 us
  starting transfers between devices  65.8 us (32%)
  waiting for transfers between devices  53.8 us (26%)
  Pallas kernels  24.6 us (12%)
  blocking collectives  20.6 us (10%)
  other arithmetic  13.4 us (7%)
  local copies, waits for them, and re-layouts  11.2 us (5%)
  matrix products  7.19 us (4%)
  between operations  6.67 us (3%)
    all_to_all x1, waiting for transfers between devices, reduce_weights(): got = plus(*lax.all_to_all(sent, YZ, 0, 0))  22.2 us
    all_to_all x1, blocking collectives, spread(): return lax.all_to_all(jnp.broadcast_to(v[None], (n,) + v.shape), axes, 0, 0)  20.6 us
    ppermute x8, starting transfers between devices, from_core(): return lax.ppermute(v, 'c', [(0, 1), (1, 0)])  18.5 us
    pallas_call x1, Pallas kernels, block_grads(): pl.pallas_call(grads_kernel, grid=(steps + 1,), in_specs=[pl.BlockSpec(me...  14.1 us
    ppermute x11, waiting for transfers between devices, from_y(): return lax.ppermute(v, 'y', [(i, (i - k) % 4) for i in range(4)])  13.9 us
    ppermute x11, starting transfers between devices, from_y(): return lax.ppermute(v, 'y', [(i, (i - k) % 4) for i in range(4)])  13.4 us
    pallas_call x1, Pallas kernels, block_logits(): pl.pallas_call(logits_kernel, grid=(steps,), in_specs=[pl.BlockSpec((TILE...  7.75 us
    ppermute x3, starting transfers between devices, from_mirror(): return lax.ppermute(v, X, [(i, 3 - i) for i in range(4)])  7.52 us
  transfers between devices with their start and end apart: 34, of which 17 were waited for; matrix products, arithmetic and copies ran while one was open for 9% of the time, Pallas kernels for 0%

profile of v7, /device:TPU:1, one launch (start us, length us, event | category | flops | bytes accessed | tf_op | source)
XLA Modules:
  0.0 203.3 jit_solution(16586052964205784353)
XLA Ops:
  0.7 1.4 copy-done
  2.0 1.5 multiply_reduce_fusion.3
  4.7 3.3 %collective-permute-start = (bf16[128,768]{1,0:T(8,128)(2,1)S(1)}, bf16[128,768]{1,0:T(8,128)(2,1)}, u32[]{:S(2)}, u32[]{:S(2)}) collective-permute-start(bf16[128,768]{1,0:T(8,128)(2,1)S(1)} %get-tuple-element.47), channel_id=1, source_target_pairs={{0,72},{8,64},{64,8},{72,0},{1,73},{9,65},{65,9},{73,1},{2,74},{10... | collective-permute-start | bytes 589832 | tf_op jit(solution)/shard_map/ppermute | solution.py:33
  8.1 1.2 broadcast_in_dim.55
  9.3 5.0 %all-to-all-start = ((bf16[8,128,768]{2,1,0:T(8,128)(2,1)}), bf16[8,128,768]{2,1,0:T(8,128)(2,1)S(1)}, u32[]{:S(2)}, u32[]{:S(2)}) async-start(bf16[8,128,768]{2,1,0:T(8,128)(2,1)} %broadcast_in_dim.55), calls=%async_computation | async-start | bytes 3145728 | tf_op jit(solution)/shard_map/all_to_all | solution.py:49
  14.4 1.0 pad_maximum_fusion.1
  15.3 2.8 %collective-permute-start.1 = (bf16[256,768]{1,0:T(8,128)(2,1)S(1)}, bf16[256,768]{1,0:T(8,128)(2,1)S(1)}, u32[]{:S(2)}, u32[]{:S(2)}) collective-permute-start(bf16[256,768]{1,0:T(8,128)(2,1)S(1)} %pad_maximum_fusion.1), channel_id=1, source_target_pairs={{0,48},{16,0},{32,16},{48,32},{1,49},{17,1},{33,17},{49,33},{2,50}... | collective-permute-start | bytes 1179656 | tf_op jit(solution)/shard_map/ppermute | solution.py:41
  18.1 1.0 constant_dynamic-slice_fusion.4
  19.1 1.6 collective-permute-start.5
  20.7 1.0 constant_dynamic-slice_fusion.2
  21.8 1.2 collective-permute-done.6
  23.0 0.7 pad_maximum_fusion.5
  23.7 1.5 collective-permute-done.1
  25.3 3.5 %collective-permute-start.2 = (bf16[128,768]{1,0:T(8,128)(2,1)S(1)}, bf16[128,768]{1,0:T(8,128)(2,1)S(1)}, u32[]{:S(2)}, u32[]{:S(2)}) collective-permute-start(bf16[128,768]{1,0:T(8,128)(2,1)S(1)} %slice.122), channel_id=1, source_target_pairs={{0,48},{16,0},{32,16},{48,32},{1,49},{17,1},{33,17},{49,33},{2,50}... | collective-permute-start | bytes 589832 | tf_op jit(solution)/shard_map/ppermute | solution.py:41
  28.8 0.7 pad_maximum_fusion.4
  29.6 1.8 collective-permute-done.2
  31.4 3.9 %collective-permute-done.4 = bf16[128,768]{1,0:T(8,128)(2,1)S(1)} collective-permute-done((bf16[128,768]{1,0:T(8,128)(2,1)S(1)}, bf16[128,768]{1,0:T(8,128)(2,1)S(1)}, u32[]{:S(2)}, u32[]{:S(2)}) %collective-permute-start.4) | collective-permute-done | bytes 196640 | tf_op jit(solution)/shard_map/ppermute | solution.py:41
  35.4 1.1 copy-done.2
  36.5 3.6 %collective-permute-start.7 = (bf16[1024,768]{1,0:T(8,128)(2,1)S(1)}, bf16[1024,768]{1,0:T(8,128)(2,1)S(1)}, u32[]{:S(2)}, u32[]{:S(2)}) collective-permute-start(bf16[1024,768]{1,0:T(8,128)(2,1)S(1)} %bitcast.39), channel_id=1, source_target_pairs={{0,1},{1,0},{2,3},{3,2},{4,5},{5,4},{6,7},{7,6},{8,9},{9,8},{10,11... | collective-permute-start | bytes 4718600 | tf_op jit(solution)/shard_map/ppermute | solution.py:29
  40.1 3.0 %collective-permute-done.7.other = bf16[1024,768]{1,0:T(8,128)(2,1)S(1)} collective-permute-done((bf16[1024,768]{1,0:T(8,128)(2,1)S(1)}, bf16[1024,768]{1,0:T(8,128)(2,1)S(1)}, u32[]{:S(2)}, u32[]{:S(2)}) %collective-permute-start.7) | collective-permute-done | bytes 1572896 | tf_op jit(solution)/shard_map/ppermute | solution.py:29
  43.2 1.1 copy-done.20
  44.3 1.4 copy-done.3
  45.7 7.8 %block_logits.1 = (f32[2048,1024]{1,0:T(8,128)}, f32[1,2048]{1,0:T(1,128)S(1)}, f32[1,1024]{1,0:T(1,128)S(1)}) custom-call(bf16[1024,768]{1,0:T(8,128)(2,1)S(1)} %bitcast.40, bf16[1024,768]{1,0:T(8,128)(2,1)} %copy-done.20, bf16[1024,768]{1,0:T(8,128)(2,1)S(1)} %copy-done.3), custom_call_target="tpu_custom_call" | custom-call | flops 3221225472 | bytes 13107200 | tf_op jit(solution)/shard_map/block_logits/pallas_call | solution.py:123
  53.9 1.5 collective-permute-start.9
  55.4 1.4 collective-permute-start.14
  56.8 2.3 %collective-permute-done.14 = f32[4,2,128]{2,1,0:T(2,128)S(1)} collective-permute-done((f32[4,2,128]{2,1,0:T(2,128)S(1)}, f32[4,2,128]{2,1,0:T(2,128)S(1)}, u32[]{:S(2)}, u32[]{:S(2)}) %collective-permute-start.14) | collective-permute-done | bytes 4128 | tf_op jit(solution)/shard_map/ppermute | solution.py:33
  59.2 0.9 collective-permute-start.15
  60.8 2.7 %collective-permute-start.11 = (f32[1,2048]{1,0:T(1,128)S(1)}, f32[1,2048]{1,0:T(1,128)S(1)}, u32[]{:S(2)}, u32[]{:S(2)}) collective-permute-start(f32[1,2048]{1,0:T(1,128)S(1)} %add_add_fusion.2), channel_id=1, source_target_pairs={{0,6},{2,0},{4,2},{6,4},{1,7},{3,1},{5,3},{7,5},{8,14},{10,8},{12,... | collective-permute-start | bytes 24584 | tf_op jit(solution)/shard_map/ppermute | solution.py:78
  63.5 1.8 collective-permute-start.13
  65.4 1.9 collective-permute-done.12
  67.6 1.4 copy-done.4
  69.0 14.1 %block_grads.1 = (bf16[1024,768]{1,0:T(8,128)(2,1)S(1)}, bf16[1024,768]{1,0:T(8,128)(2,1)S(1)}, bf16[1024,768]{1,0:T(8,128)(2,1)S(1)}) custom-call(s32[1]{0:T(128)} %bitcast.1.place, f32[2048,1024]{1,0:T(8,128)} %get-tuple-element.29.logits, f32[1,2048]{1,0:T(1,128)S(1)} %add_add_fusion.1.row_total, f32[1,1024]{1,0:T(1,128)S(1)} %bitcast.42, ...), custom_call_target="tpu_custom_call" | custom-call | flops 6442450944 | bytes 17825792 | tf_op jit(solution)/shard_map/block_grads/pallas_call | solution.py:196
  83.2 3.9 %collective-permute-start.20 = (bf16[1024,768]{1,0:T(8,128)(2,1)S(1)}, bf16[1024,768]{1,0:T(8,128)(2,1)S(1)}, u32[]{:S(2)}, u32[]{:S(2)}) collective-permute-start(bf16[1024,768]{1,0:T(8,128)(2,1)S(1)} %get-tuple-element.34), channel_id=1, source_target_pairs={{0,1},{1,0},{2,3},{3,2},{4,5},{5,4},{6,7},{7,6},{8,9},{9,8},{10,11... | collective-permute-start | bytes 4718600 | tf_op jit(solution)/shard_map/ppermute | solution.py:29
  87.1 1.2 collective-permute-start.18
  88.2 1.6 collective-permute-start.19
  89.8 5.0 %collective-permute-done.18 = bf16[128,768]{1,0:T(8,128)(2,1)S(1)} collective-permute-done((bf16[128,768]{1,0:T(8,128)(2,1)S(1)}, bf16[128,768]{1,0:T(8,128)(2,1)S(1)}, u32[]{:S(2)}, u32[]{:S(2)}) %collective-permute-start.18) | collective-permute-done | bytes 196640 | tf_op jit(solution)/shard_map/ppermute | solution.py:41
  95.1 0.8 pad_maximum_fusion.3
  95.9 0.8 pad_maximum_fusion.2
  96.7 1.5 add_convert_fusion
  98.2 4.2 %all-to-all-start.1 = ((bf16[8,128,768]{2,1,0:T(8,128)(2,1)}), bf16[8,128,768]{2,1,0:T(8,128)(2,1)S(1)}, u32[]{:S(2)}, u32[]{:S(2)}) async-start(bf16[8,128,768]{2,1,0:T(8,128)(2,1)} %bitcast.46), calls=%async_computation.1 | async-start | bytes 3145728 | tf_op jit(solution)/shard_map/all_to_all | solution.py:343
  102.5 1.1 collective-permute-start.22
  103.6 1.5 collective-permute-start.23
  106.3 1.6 collective-permute-start.26
  108.0 1.0 collective-permute-done.26
  112.1 1.4 collective-permute-done.22
  113.5 1.4 convert_add_fusion
  114.9 2.8 %collective-permute-start.24 = (bf16[128,768]{1,0:T(8,128)(2,1)S(1)}, bf16[128,768]{1,0:T(8,128)(2,1)S(1)}, u32[]{:S(2)}, u32[]{:S(2)}) collective-permute-start(bf16[128,768]{1,0:T(8,128)(2,1)S(1)} %slice.165), channel_id=1, source_target_pairs={{0,72},{8,64},{64,8},{72,0},{1,73},{9,65},{65,9},{73,1},{2,74},{10... | collective-permute-start | bytes 589832 | tf_op jit(solution)/shard_map/ppermute | solution.py:33
  117.8 3.3 %collective-permute-done.24 = bf16[128,768]{1,0:T(8,128)(2,1)S(1)} collective-permute-done((bf16[128,768]{1,0:T(8,128)(2,1)S(1)}, bf16[128,768]{1,0:T(8,128)(2,1)S(1)}, u32[]{:S(2)}, u32[]{:S(2)}) %collective-permute-start.24) | collective-permute-done | bytes 196640 | tf_op jit(solution)/shard_map/ppermute | solution.py:33
  121.1 1.2 multiply_reduce_fusion.1
  122.3 0.8 divide_convert_fusion
  123.2 2.9 %collective-permute-start.25 = (bf16[128,768]{1,0:T(8,128)(2,1)}, bf16[128,768]{1,0:T(8,128)(2,1)}, u32[]{:S(2)}, u32[]{:S(2)}) collective-permute-start(bf16[128,768]{1,0:T(8,128)(2,1)} %divide_convert_fusion), channel_id=1, source_target_pairs={{0,1},{1,0},{2,3},{3,2},{4,5},{5,4},{6,7},{7,6},{8,9},{9,8},{10,11... | collective-permute-start | bytes 589832 | tf_op jit(solution)/shard_map/ppermute | solution.py:29
  126.0 1.0 fusion.6
  127.4 1.4 convolution_convert_fusion.1
  129.3 1.3 pad_maximum_fusion
  130.6 6.6 %all-to-all-start.2 = ((bf16[16,64,768]{2,1,0:T(8,128)(2,1)}), bf16[16,64,768]{2,1,0:T(8,128)(2,1)S(1)}, u32[]{:S(2)}, u32[]{:S(2)}) async-start(bf16[16,64,768]{2,1,0:T(8,128)(2,1)} %pad_maximum_fusion), calls=%async_computation.2 | async-start | bytes 3145728 | tf_op jit(solution)/shard_map/all_to_all | solution.py:307
  137.2 22.2 %all-to-all-done.2 = bf16[16,64,768]{2,1,0:T(8,128)(2,1)S(1)} async-done(((bf16[16,64,768]{2,1,0:T(8,128)(2,1)}), bf16[16,64,768]{2,1,0:T(8,128)(2,1)S(1)}, u32[]{:S(2)}, u32[]{:S(2)}) %all-to-all-start.2) | async-done | bytes 1572896 | tf_op jit(solution)/shard_map/all_to_all | solution.py:307
  160.0 2.8 %collective-permute-start.27 = (bf16[64,768]{1,0:T(8,128)(2,1)S(1)}, bf16[64,768]{1,0:T(8,128)(2,1)S(1)}, u32[]{:S(2)}, u32[]{:S(2)}) collective-permute-start(bf16[64,768]{1,0:T(8,128)(2,1)S(1)} %pad_maximum_fusion.6), channel_id=1, source_target_pairs={{0,72},{8,0},{64,8},{72,64},{1,73},{9,1},{65,9},{73,65},{2,74},{10... | collective-permute-start | bytes 294920 | tf_op jit(solution)/shard_map/ppermute | solution.py:37
  162.8 1.3 collective-permute-start.29
  164.4 4.1 %collective-permute-done.28 = bf16[64,768]{1,0:T(8,128)(2,1)S(1)} collective-permute-done((bf16[64,768]{1,0:T(8,128)(2,1)S(1)}, bf16[64,768]{1,0:T(8,128)(2,1)S(1)}, u32[]{:S(2)}, u32[]{:S(2)}) %collective-permute-start.28) | collective-permute-done | bytes 98336 | tf_op jit(solution)/shard_map/ppermute | solution.py:37
  168.7 20.6 %all_to_all.20.mine = bf16[16,56,768]{2,1,0:T(8,128)(2,1)S(1)} all-to-all(bf16[16,56,768]{2,1,0:T(8,128)(2,1)S(1)} %broadcast_in_dim.65), channel_id=1, replica_groups=mesh['xh'=2,'y'=4,'xl'=2,'z'=4,'c'=2] {'y','z'}, dimensions={0} | all-to-all | bytes 2752512 | tf_op jit(solution)/shard_map/all_to_all | solution.py:49
  189.4 4.7 %collective-permute-start.30 = (bf16[16,56,768]{2,1,0:T(8,128)(2,1)S(1)}, bf16[16,56,768]{2,1,0:T(8,128)(2,1)S(1)}, u32[]{:S(2)}, u32[]{:S(2)}) collective-permute-start(bf16[16,56,768]{2,1,0:T(8,128)(2,1)S(1)} %all_to_all.20.mine), channel_id=1, source_target_pairs={{0,1},{1,0},{2,3},{3,2},{4,5},{5,4},{6,7},{7,6},{8,9},{9,8},{10,11... | collective-permute-start | bytes 4128776 | tf_op jit(solution)/shard_map/ppermute | solution.py:29
  194.1 2.1 %convolution_convert_fusion.3 = bf16[128,768]{1,0:T(8,128)(2,1)} fusion(bf16[128,768]{1,0:T(8,128)(2,1)} %divide_convert_fusion, bf16[768,768]{1,0:T(8,128)(2,1)S(1)} %copy-done.10), kind=kOutput, calls=%fused_computation.5 | convolution fusion | flops 151093248 | bytes 1572864 | tf_op jit(solution)/shard_map/dot_general | solution.py:280
  196.2 1.3 convolution_convert_fusion.2
  199.5 2.7 %whole_terms.1 = (f32[1024,768]{1,0:T(8,128)}, f32[768,768]{1,0:T(8,128)}) custom-call(s32[1]{0:T(128)} %bitcast.12.core, bf16[16,56,768]{2,1,0:T(8,128)(2,1)S(1)} %all_to_all.20.mine, bf16[16,56,768]{2,1,0:T(8,128)(2,1)S(1)} %collective-permute-done.30.other), custom_call_target="tpu_custom_call" | custom-call | bytes 8257536 | tf_op jit(solution)/shard_map/whole_terms/pallas_call | solution.py:249
  (110 shorter events, 7.1 us)
Async XLA Ops:
  0.6 1.4 copy-start
  0.6 2.9 %copy-start.14 = (bf16[128,768]{1,0:T(8,128)(2,1)S(1)}, bf16[128,768]{1,0:T(8,128)(2,1)}, u32[]{:S(2)}) copy-start(bf16[128,768]{1,0:T(8,128)(2,1)} %param.5) | copy-start | bytes 589828
  2.0 1.5 copy-start.9
  3.6 0.8 copy-start.5
  4.0 0.8 copy-start.7
  4.0 5.3 %copy-start.16 = (f32[128]{0:T(128)}, f32[128]{0:T(128)S(1)}, u32[]{:S(2)}) copy-start(f32[128]{0:T(128)S(1)} %get-tuple-element.69) | copy-start | bytes 1540
  4.7 9.6 %collective-permute-start = (bf16[128,768]{1,0:T(8,128)(2,1)S(1)}, bf16[128,768]{1,0:T(8,128)(2,1)}, u32[]{:S(2)}, u32[]{:S(2)}) collective-permute-start(bf16[128,768]{1,0:T(8,128)(2,1)S(1)} %get-tuple-element.47), channel_id=1, source_target_pairs={{0,72},{8,64},{64,8},{72,0},{1,73},{9,65},{65,9},{73,1},{2,74},{10... | collective-permute-start | bytes 589832 | tf_op jit(solution)/shard_map/ppermute | solution.py:33
  9.3 27.2 %all-to-all-start = ((bf16[8,128,768]{2,1,0:T(8,128)(2,1)}), bf16[8,128,768]{2,1,0:T(8,128)(2,1)S(1)}, u32[]{:S(2)}, u32[]{:S(2)}) async-start(bf16[8,128,768]{2,1,0:T(8,128)(2,1)} %broadcast_in_dim.55), calls=%async_computation | async-start | bytes 3145728 | tf_op jit(solution)/shard_map/all_to_all | solution.py:49
  15.3 10.0 %collective-permute-start.1 = (bf16[256,768]{1,0:T(8,128)(2,1)S(1)}, bf16[256,768]{1,0:T(8,128)(2,1)S(1)}, u32[]{:S(2)}, u32[]{:S(2)}) collective-permute-start(bf16[256,768]{1,0:T(8,128)(2,1)S(1)} %pad_maximum_fusion.1), channel_id=1, source_target_pairs={{0,48},{16,0},{32,16},{48,32},{1,49},{17,1},{33,17},{49,33},{2,50}... | collective-permute-start | bytes 1179656 | tf_op jit(solution)/shard_map/ppermute | solution.py:41
  18.1 11.4 %collective-permute-start.3 = (bf16[256,768]{1,0:T(8,128)(2,1)S(1)}, bf16[256,768]{1,0:T(8,128)(2,1)S(1)}, u32[]{:S(2)}, u32[]{:S(2)}) collective-permute-start(bf16[256,768]{1,0:T(8,128)(2,1)S(1)} %pad_maximum_fusion.1), channel_id=1, source_target_pairs={{0,16},{16,32},{32,48},{48,0},{1,17},{17,33},{33,49},{49,1},{2,18}... | collective-permute-start | bytes 1179656 | tf_op jit(solution)/shard_map/ppermute | solution.py:41
  19.1 9.7 %collective-permute-start.5 = (bf16[128,512]{1,0:T(8,128)(2,1)S(1)}, bf16[128,512]{1,0:T(8,128)(2,1)S(1)}, u32[]{:S(2)}, u32[]{:S(2)}) collective-permute-start(bf16[128,512]{1,0:T(8,128)(2,1)S(1)} %get-tuple-element.55), channel_id=1, source_target_pairs={{0,1},{1,0},{2,3},{3,2},{4,5},{5,4},{6,7},{7,6},{8,9},{9,8},{10,11... | collective-permute-start | bytes 393224 | tf_op jit(solution)/shard_map/ppermute | solution.py:29
  21.7 1.4 collective-permute-start.6
  25.3 6.1 %collective-permute-start.2 = (bf16[128,768]{1,0:T(8,128)(2,1)S(1)}, bf16[128,768]{1,0:T(8,128)(2,1)S(1)}, u32[]{:S(2)}, u32[]{:S(2)}) collective-permute-start(bf16[128,768]{1,0:T(8,128)(2,1)S(1)} %slice.122), channel_id=1, source_target_pairs={{0,48},{16,0},{32,16},{48,32},{1,49},{17,1},{33,17},{49,33},{2,50}... | collective-permute-start | bytes 589832 | tf_op jit(solution)/shard_map/ppermute | solution.py:41
  29.5 5.8 %collective-permute-start.4 = (bf16[128,768]{1,0:T(8,128)(2,1)S(1)}, bf16[128,768]{1,0:T(8,128)(2,1)S(1)}, u32[]{:S(2)}, u32[]{:S(2)}) collective-permute-start(bf16[128,768]{1,0:T(8,128)(2,1)S(1)} %slice.123), channel_id=1, source_target_pairs={{0,16},{16,32},{32,48},{48,0},{1,17},{17,33},{33,49},{49,1},{2,18}... | collective-permute-start | bytes 589832 | tf_op jit(solution)/shard_map/ppermute | solution.py:41
  35.4 1.1 copy-start.2
  36.5 6.6 %collective-permute-start.7 = (bf16[1024,768]{1,0:T(8,128)(2,1)S(1)}, bf16[1024,768]{1,0:T(8,128)(2,1)S(1)}, u32[]{:S(2)}, u32[]{:S(2)}) collective-permute-start(bf16[1024,768]{1,0:T(8,128)(2,1)S(1)} %bitcast.39), channel_id=1, source_target_pairs={{0,1},{1,0},{2,3},{3,2},{4,5},{5,4},{6,7},{7,6},{8,9},{9,8},{10,11... | collective-permute-start | bytes 4718600 | tf_op jit(solution)/shard_map/ppermute | solution.py:29
  43.2 1.1 copy-start.20
  44.3 1.4 copy-start.3
  53.5 6.7 %collective-permute-start.10 = (f32[1,2048]{1,0:T(1,128)S(1)}, f32[1,2048]{1,0:T(1,128)S(1)}, u32[]{:S(2)}, u32[]{:S(2)}) collective-permute-start(f32[1,2048]{1,0:T(1,128)S(1)} %pad_maximum_fusion.7), channel_id=1, source_target_pairs={{0,1},{1,0},{8,9},{9,8},{2,3},{3,2},{10,11},{11,10},{4,5},{5,4},{1... | collective-permute-start | bytes 24584 | tf_op jit(solution)/shard_map/ppermute | solution.py:75
  53.9 6.9 %collective-permute-start.9 = (f32[1,2048]{1,0:T(1,128)S(1)}, f32[1,2048]{1,0:T(1,128)S(1)}, u32[]{:S(2)}, u32[]{:S(2)}) collective-permute-start(f32[1,2048]{1,0:T(1,128)S(1)} %pad_maximum_fusion.7), channel_id=1, source_target_pairs={{0,9},{1,8},{8,1},{9,0},{2,11},{3,10},{10,3},{11,2},{4,13},{5,12},... | collective-permute-start | bytes 24584 | tf_op jit(solution)/shard_map/ppermute | solution.py:75
  55.4 5.4 %collective-permute-start.8 = (f32[1,2048]{1,0:T(1,128)S(1)}, f32[1,2048]{1,0:T(1,128)S(1)}, u32[]{:S(2)}, u32[]{:S(2)}) collective-permute-start(f32[1,2048]{1,0:T(1,128)S(1)} %get-tuple-element.30), channel_id=1, source_target_pairs={{0,8},{1,9},{8,0},{9,1},{2,10},{3,11},{10,2},{11,3},{4,12},{5,13},... | collective-permute-start | bytes 24584 | tf_op jit(solution)/shard_map/ppermute | solution.py:75
  55.4 3.7 %collective-permute-start.14 = (f32[4,2,128]{2,1,0:T(2,128)S(1)}, f32[4,2,128]{2,1,0:T(2,128)S(1)}, u32[]{:S(2)}, u32[]{:S(2)}) collective-permute-start(f32[4,2,128]{2,1,0:T(2,128)S(1)} %bitcast.44), channel_id=1, source_target_pairs={{0,72},{8,64},{64,8},{72,0},{1,73},{9,65},{65,9},{73,1},{2,74},{10... | collective-permute-start | bytes 12296 | tf_op jit(solution)/shard_map/ppermute | solution.py:33
  59.2 6.2 %collective-permute-start.17 = (f32[4,2,128]{2,1,0:T(2,128)S(1)}, f32[4,2,128]{2,1,0:T(2,128)S(1)}, u32[]{:S(2)}, u32[]{:S(2)}) collective-permute-start(f32[4,2,128]{2,1,0:T(2,128)S(1)} %add.199), channel_id=1, source_target_pairs={{0,32},{16,48},{32,0},{48,16},{1,33},{17,49},{33,1},{49,17},{2,34}... | collective-permute-start | bytes 12296 | tf_op jit(solution)/shard_map/ppermute | solution.py:41
  59.2 4.3 %collective-permute-start.15 = (f32[4,2,128]{2,1,0:T(2,128)S(1)}, f32[4,2,128]{2,1,0:T(2,128)S(1)}, u32[]{:S(2)}, u32[]{:S(2)}) collective-permute-start(f32[4,2,128]{2,1,0:T(2,128)S(1)} %add.199), channel_id=1, source_target_pairs={{0,48},{16,0},{32,16},{48,32},{1,49},{17,1},{33,17},{49,33},{2,50}... | collective-permute-start | bytes 12296 | tf_op jit(solution)/shard_map/ppermute | solution.py:41
  60.1 5.2 %collective-permute-start.16 = (f32[4,2,128]{2,1,0:T(2,128)S(1)}, f32[4,2,128]{2,1,0:T(2,128)S(1)}, u32[]{:S(2)}, u32[]{:S(2)}) collective-permute-start(f32[4,2,128]{2,1,0:T(2,128)S(1)} %add.199), channel_id=1, source_target_pairs={{0,16},{16,32},{32,48},{48,0},{1,17},{17,33},{33,49},{49,1},{2,18}... | collective-permute-start | bytes 12296 | tf_op jit(solution)/shard_map/ppermute | solution.py:41
  60.8 4.6 %collective-permute-start.11 = (f32[1,2048]{1,0:T(1,128)S(1)}, f32[1,2048]{1,0:T(1,128)S(1)}, u32[]{:S(2)}, u32[]{:S(2)}) collective-permute-start(f32[1,2048]{1,0:T(1,128)S(1)} %add_add_fusion.2), channel_id=1, source_target_pairs={{0,6},{2,0},{4,2},{6,4},{1,7},{3,1},{5,3},{7,5},{8,14},{10,8},{12,... | collective-permute-start | bytes 24584 | tf_op jit(solution)/shard_map/ppermute | solution.py:78
  63.5 3.7 %collective-permute-start.12 = (f32[1,2048]{1,0:T(1,128)S(1)}, f32[1,2048]{1,0:T(1,128)S(1)}, u32[]{:S(2)}, u32[]{:S(2)}) collective-permute-start(f32[1,2048]{1,0:T(1,128)S(1)} %add_add_fusion.2), channel_id=1, source_target_pairs={{0,2},{2,4},{4,6},{6,0},{1,3},{3,5},{5,7},{7,1},{8,10},{10,12},{12... | collective-permute-start | bytes 24584 | tf_op jit(solution)/shard_map/ppermute | solution.py:78
  63.5 4.0 %collective-permute-start.13 = (f32[1,2048]{1,0:T(1,128)S(1)}, f32[1,2048]{1,0:T(1,128)S(1)}, u32[]{:S(2)}, u32[]{:S(2)}) collective-permute-start(f32[1,2048]{1,0:T(1,128)S(1)} %add_add_fusion.2), channel_id=1, source_target_pairs={{0,4},{2,6},{4,0},{6,2},{1,5},{3,7},{5,1},{7,3},{8,12},{10,14},{12... | collective-permute-start | bytes 24584 | tf_op jit(solution)/shard_map/ppermute | solution.py:78
  67.6 1.4 copy-start.4
  83.1 12.8 %copy-start.1 = (bf16[1024,768]{1,0:T(8,128)(2,1)}, bf16[1024,768]{1,0:T(8,128)(2,1)S(1)}, u32[]{:S(2)}) copy-start(bf16[1024,768]{1,0:T(8,128)(2,1)S(1)} %get-tuple-element.32) | copy-start | bytes 4718596
  83.2 13.6 %collective-permute-start.20 = (bf16[1024,768]{1,0:T(8,128)(2,1)S(1)}, bf16[1024,768]{1,0:T(8,128)(2,1)S(1)}, u32[]{:S(2)}, u32[]{:S(2)}) collective-permute-start(bf16[1024,768]{1,0:T(8,128)(2,1)S(1)} %get-tuple-element.34), channel_id=1, source_target_pairs={{0,1},{1,0},{2,3},{3,2},{4,5},{5,4},{6,7},{7,6},{8,9},{9,8},{10,11... | collective-permute-start | bytes 4718600 | tf_op jit(solution)/shard_map/ppermute | solution.py:29
  87.1 7.8 %collective-permute-start.18 = (bf16[128,768]{1,0:T(8,128)(2,1)S(1)}, bf16[128,768]{1,0:T(8,128)(2,1)S(1)}, u32[]{:S(2)}, u32[]{:S(2)}) collective-permute-start(bf16[128,768]{1,0:T(8,128)(2,1)S(1)} %get-tuple-element.51), channel_id=1, source_target_pairs={{0,16},{16,32},{32,48},{48,0},{1,17},{17,33},{33,49},{49,1},{2,18}... | collective-permute-start | bytes 589832 | tf_op jit(solution)/shard_map/ppermute | solution.py:41
  88.2 6.8 %collective-permute-start.19 = (bf16[128,768]{1,0:T(8,128)(2,1)S(1)}, bf16[128,768]{1,0:T(8,128)(2,1)S(1)}, u32[]{:S(2)}, u32[]{:S(2)}) collective-permute-start(bf16[128,768]{1,0:T(8,128)(2,1)S(1)} %get-tuple-element.49), channel_id=1, source_target_pairs={{0,48},{16,0},{32,16},{48,32},{1,49},{17,1},{33,17},{49,33},{2,50}... | collective-permute-start | bytes 589832 | tf_op jit(solution)/shard_map/ppermute | solution.py:41
  98.2 27.8 %all-to-all-start.1 = ((bf16[8,128,768]{2,1,0:T(8,128)(2,1)}), bf16[8,128,768]{2,1,0:T(8,128)(2,1)S(1)}, u32[]{:S(2)}, u32[]{:S(2)}) async-start(bf16[8,128,768]{2,1,0:T(8,128)(2,1)} %bitcast.46), calls=%async_computation.1 | async-start | bytes 3145728 | tf_op jit(solution)/shard_map/all_to_all | solution.py:343
  102.5 11.1 %collective-permute-start.22 = (bf16[256,768]{1,0:T(8,128)(2,1)}, bf16[256,768]{1,0:T(8,128)(2,1)}, u32[]{:S(2)}, u32[]{:S(2)}) collective-permute-start(bf16[256,768]{1,0:T(8,128)(2,1)} %pad_maximum_fusion.2), channel_id=1, source_target_pairs={{0,16},{16,32},{32,48},{48,0},{1,17},{17,33},{33,49},{49,1},{2,18}... | collective-permute-start | bytes 1179656 | tf_op jit(solution)/shard_map/ppermute | solution.py:41
  103.6 9.9 %collective-permute-start.23 = (bf16[256,768]{1,0:T(8,128)(2,1)}, bf16[256,768]{1,0:T(8,128)(2,1)}, u32[]{:S(2)}, u32[]{:S(2)}) collective-permute-start(bf16[256,768]{1,0:T(8,128)(2,1)} %pad_maximum_fusion.3), channel_id=1, source_target_pairs={{0,48},{16,0},{32,16},{48,32},{1,49},{17,1},{33,17},{49,33},{2,50}... | collective-permute-start | bytes 1179656 | tf_op jit(solution)/shard_map/ppermute | solution.py:41
  106.3 2.6 %collective-permute-start.26 = (f32[]{:T(128)}, f32[]{:T(128)}, u32[]{:S(2)}, u32[]{:S(2)}) collective-permute-start(f32[]{:T(128)} %fusion.17), channel_id=1, source_target_pairs={{0,1},{1,0},{2,3},{3,2},{4,5},{5,4},{6,7},{7,6},{8,9},{9,8},{10,11... | collective-permute-start | bytes 20 | tf_op jit(solution)/shard_map/ppermute | solution.py:29
  112.0 5.7 %copy-start.18 = (pred[768]{0:T(1024)(128)(4,1)S(1)}, pred[768]{0:T(1024)(128)(4,1)}, u32[]{:S(2)}) copy-start(pred[768]{0:T(1024)(128)(4,1)} %iota_compare_fusion.1) | copy-start | bytes 2308
  112.1 10.2 %copy-start.8 = (f32[128,768]{1,0:T(8,128)S(1)}, f32[128,768]{1,0:T(8,128)}, u32[]{:S(2)}) copy-start(f32[128,768]{1,0:T(8,128)} %copy-done.7) | copy-start | bytes 1179652
  114.9 11.1 %copy-start.6 = (f32[128,768]{1,0:T(8,128)S(1)}, f32[128,768]{1,0:T(8,128)}, u32[]{:S(2)}) copy-start(f32[128,768]{1,0:T(8,128)} %copy-done.5) | copy-start | bytes 1179652
  114.9 6.2 %collective-permute-start.24 = (bf16[128,768]{1,0:T(8,128)(2,1)S(1)}, bf16[128,768]{1,0:T(8,128)(2,1)S(1)}, u32[]{:S(2)}, u32[]{:S(2)}) collective-permute-start(bf16[128,768]{1,0:T(8,128)(2,1)S(1)} %slice.165), channel_id=1, source_target_pairs={{0,72},{8,64},{64,8},{72,0},{1,73},{9,65},{65,9},{73,1},{2,74},{10... | collective-permute-start | bytes 589832 | tf_op jit(solution)/shard_map/ppermute | solution.py:33
  123.2 3.9 %copy-start.17 = (f32[128]{0:T(128)S(1)}, f32[128]{0:T(128)}, u32[]{:S(2)}) copy-start(f32[128]{0:T(128)} %copy-done.16) | copy-start | bytes 1540
  123.2 4.3 %collective-permute-start.25 = (bf16[128,768]{1,0:T(8,128)(2,1)}, bf16[128,768]{1,0:T(8,128)(2,1)}, u32[]{:S(2)}, u32[]{:S(2)}) collective-permute-start(bf16[128,768]{1,0:T(8,128)(2,1)} %divide_convert_fusion), channel_id=1, source_target_pairs={{0,1},{1,0},{2,3},{3,2},{4,5},{5,4},{6,7},{7,6},{8,9},{9,8},{10,11... | collective-permute-start | bytes 589832 | tf_op jit(solution)/shard_map/ppermute | solution.py:29
  126.0 1.4 copy-start.15
  127.0 1.8 copy-start.13
  127.2 1.6 copy-start.11
  127.2 1.6 collective-permute-start.21
  130.6 28.9 %all-to-all-start.2 = ((bf16[16,64,768]{2,1,0:T(8,128)(2,1)}), bf16[16,64,768]{2,1,0:T(8,128)(2,1)S(1)}, u32[]{:S(2)}, u32[]{:S(2)}) async-start(bf16[16,64,768]{2,1,0:T(8,128)(2,1)} %pad_maximum_fusion), calls=%async_computation.2 | async-start | bytes 3145728 | tf_op jit(solution)/shard_map/all_to_all | solution.py:307
  137.2 22.6 %copy-start.19 = (pred[768]{0:T(1024)(128)(4,1)S(1)}, pred[768]{0:T(1024)(128)(4,1)}, u32[]{:S(2)}) copy-start(pred[768]{0:T(1024)(128)(4,1)} %iota_compare_fusion.1) | copy-start | bytes 2308
  160.0 4.5 %collective-permute-start.27 = (bf16[64,768]{1,0:T(8,128)(2,1)S(1)}, bf16[64,768]{1,0:T(8,128)(2,1)S(1)}, u32[]{:S(2)}, u32[]{:S(2)}) collective-permute-start(bf16[64,768]{1,0:T(8,128)(2,1)S(1)} %pad_maximum_fusion.6), channel_id=1, source_target_pairs={{0,72},{8,0},{64,8},{72,64},{1,73},{9,1},{65,9},{73,65},{2,74},{10... | collective-permute-start | bytes 294920 | tf_op jit(solution)/shard_map/ppermute | solution.py:37
  162.8 5.7 %collective-permute-start.28 = (bf16[64,768]{1,0:T(8,128)(2,1)S(1)}, bf16[64,768]{1,0:T(8,128)(2,1)S(1)}, u32[]{:S(2)}, u32[]{:S(2)}) collective-permute-start(bf16[64,768]{1,0:T(8,128)(2,1)S(1)} %pad_maximum_fusion.6), channel_id=1, source_target_pairs={{0,8},{8,64},{64,72},{72,0},{1,9},{9,65},{65,73},{73,1},{2,10},{10... | collective-permute-start | bytes 294920 | tf_op jit(solution)/shard_map/ppermute | solution.py:37
  162.8 5.7 %collective-permute-start.29 = (bf16[64,768]{1,0:T(8,128)(2,1)S(1)}, bf16[64,768]{1,0:T(8,128)(2,1)S(1)}, u32[]{:S(2)}, u32[]{:S(2)}) collective-permute-start(bf16[64,768]{1,0:T(8,128)(2,1)S(1)} %pad_maximum_fusion.6), channel_id=1, source_target_pairs={{0,64},{8,72},{64,0},{72,8},{1,65},{9,73},{65,1},{73,9},{2,66},{10... | collective-permute-start | bytes 294920 | tf_op jit(solution)/shard_map/ppermute | solution.py:37
  168.7 25.4 %copy-start.10 = (bf16[768,768]{1,0:T(8,128)(2,1)S(1)}, bf16[768,768]{1,0:T(8,128)(2,1)}, u32[]{:S(2)}) copy-start(bf16[768,768]{1,0:T(8,128)(2,1)} %param.7) | copy-start | bytes 3538948
  168.7 27.5 %copy-start.12 = (bf16[128,768]{1,0:T(8,128)(2,1)S(1)}, bf16[128,768]{1,0:T(8,128)(2,1)}, u32[]{:S(2)}) copy-start(bf16[128,768]{1,0:T(8,128)(2,1)} %copy-done.11) | copy-start | bytes 589828
  189.4 10.1 %collective-permute-start.30 = (bf16[16,56,768]{2,1,0:T(8,128)(2,1)S(1)}, bf16[16,56,768]{2,1,0:T(8,128)(2,1)S(1)}, u32[]{:S(2)}, u32[]{:S(2)}) collective-permute-start(bf16[16,56,768]{2,1,0:T(8,128)(2,1)S(1)} %all_to_all.20.mine), channel_id=1, source_target_pairs={{0,1},{1,0},{2,3},{3,2},{4,5},{5,4},{6,7},{7,6},{8,9},{9,8},{10,11... | collective-permute-start | bytes 4128776 | tf_op jit(solution)/shard_map/ppermute | solution.py:29
